TPU v7x, 512 devices: a whole 4x8x8 slice. The times are simulated.
512 devices in a mesh: gz: 32 (over z_hi, y), ch: 16 (over x, z_lo, core).
Axes of the slice: x: 4, y: 8, z: 8 (z_hi: 4, z_lo: 2; z = z_hi * 2 + z_lo), core: 2. Of those that a mesh axis runs over, the one named last changes fastest.
Arguments:
- coarse: bfloat16 [256, 32, 128], P('ch', 'gz'), may hold values from -102 to 102
- encoder_skip: bfloat16 [128, 64, 512], P('ch', 'gz'), may hold values from -102 to 102
- up_weight: bfloat16 [27, 128, 256], P(None, None, 'ch'), may hold values from -0.21875 to 0.21875
- first_up: bfloat16 [27, 128, 128], P(None, None, 'ch'), may hold values from -0.078125 to 0.078125
- first_skip: bfloat16 [27, 128, 128], P(None, None, 'ch'), may hold values from -0.078125 to 0.078125
- second_weight: bfloat16 [27, 128, 128], P(None, None, 'ch'), may hold values from -0.109375 to 0.109375
- cotangent: bfloat16 [128, 64, 512], P('ch', 'gz'), may hold values from -33 to 33
Outputs:
- decoded: bfloat16 [128, 64, 512], P('ch', 'gz')
- grad_coarse: bfloat16 [256, 32, 128], P('ch', 'gz')
- grad_skip: bfloat16 [128, 64, 512], P('ch', 'gz')
- grad_up_weight: float32 [27, 128, 256], P(None, None, 'ch')
- grad_first_up: float32 [27, 128, 128], P(None, None, 'ch')
- grad_first_skip: float32 [27, 128, 128], P(None, None, 'ch')
- grad_second: float32 [27, 128, 128], P(None, None, 'ch')
All inputs are finite; a program needn't handle non-finite values.
Results may differ from a plain program's by a relative error of at most 0.015.
Values may be sent and summed in bfloat16 or wider, within the bound.
No kernel may reach another device: no remote copies, remote signals or barrier semaphores. Data moves between devices by JAX's collectives and lax.ppermute only.
A program may use at most 64 MiB of HBM per device.

v0:
```python
import math

import jax
import jax.numpy as jnp
from jax import lax
from jax.sharding import PartitionSpec as P

C_OUT = 128
XC = 16


LEAK_SLOPE = 0.01
KINK_WIDTH = 0.01
NORM_EPS = 1e-05
PARITY_TAPS = (((1, 0),), ((2, 0), (0, 1)))


def padded_2(block, sides, width):
    for axis, dim in sides:
        count = lax.axis_size(axis)
        forward = [(i, i + 1) for i in range(count - 1)]
        backward = [(target, source) for source, target in forward]
        low = lax.ppermute(
            lax.slice_in_dim(block, block.shape[dim] - width, None, axis=dim), axis, forward
        )
        high = lax.ppermute(lax.slice_in_dim(block, 0, width, axis=dim), axis, backward)
        block = jnp.concatenate([low, block, high], axis=dim)
    return block


def passed_along(block, axis, distance):
    devices = range(lax.axis_size(axis))
    route = [(i - distance, i) for i in devices if i - distance in devices]
    return lax.ppermute(block, axis, route)


def plane_shift(values, step_y, step_x, columns):
    extent = values.shape[-1]
    margins = [(0, 0)] * (values.ndim - 1) + [(columns + 1, columns + 1)]
    padded = jnp.pad(values, margins)
    offset_at = columns + 1 + step_y * columns + step_x
    shifted = lax.slice_in_dim(padded, offset_at, offset_at + extent, axis=values.ndim - 1)
    column = jnp.arange(extent, dtype=jnp.int32) % columns + step_x
    inside = (column >= 0) & (column < columns)
    return jnp.where(inside, shifted, jnp.zeros_like(shifted))


def activate(inputs):
    smooth = jnp.sqrt(inputs * inputs + KINK_WIDTH)
    return 0.5 * (1.0 + LEAK_SLOPE) * inputs + 0.5 * (1.0 - LEAK_SLOPE) * smooth


def activate_slope(inputs):
    return 0.5 * (1.0 + LEAK_SLOPE) + 0.5 * (1.0 - LEAK_SLOPE) * inputs / jnp.sqrt(
        inputs * inputs + KINK_WIDTH
    )


def up_forward(extended, weights, columns):
    channels = extended.shape[0]
    planes = extended.shape[1] - 1
    plane_cells = extended.shape[2]
    shifted = {}
    for y_off in (0, 1):
        for x_off in (0, 1):
            shifted[y_off, x_off] = plane_shift(extended, y_off, x_off, columns)
    results = []
    for z_par in (0, 1):
        for y_par in (0, 1):
            for x_par in (0, 1):
                left_parts = []
                right_parts = []
                for k_z, z_off in PARITY_TAPS[z_par]:
                    for k_y, y_off in PARITY_TAPS[y_par]:
                        for k_x, x_off in PARITY_TAPS[x_par]:
                            left_parts.append(weights[k_z * 9 + k_y * 3 + k_x])
                            source = shifted[y_off, x_off][:, z_off : z_off + planes]
                            right_parts.append(source.reshape(channels, planes * plane_cells))
                matrix = jnp.concatenate(left_parts, axis=1)
                stacked = jnp.concatenate(right_parts, axis=0)
                results.append(jnp.dot(matrix, stacked, preferred_element_type=jnp.float32))
    return jnp.stack(results)


def alternate(parities, planes, columns):
    outputs = parities.shape[1]
    coarse_rows = parities.shape[2] // (planes * columns)
    arranged = parities.reshape(2, 2, 2, outputs, planes, coarse_rows, columns)
    arranged = jnp.transpose(arranged, (3, 4, 0, 5, 1, 6, 2))
    return arranged.reshape(outputs, 2 * planes, 4 * coarse_rows * columns)


def split_parity(fine_grad, columns):
    outputs, planes = (fine_grad.shape[0], fine_grad.shape[1])
    coarse_rows = fine_grad.shape[2] // (4 * columns)
    arranged = fine_grad.reshape(outputs, planes, coarse_rows, 2, columns, 2)
    arranged = jnp.transpose(arranged, (3, 5, 0, 1, 2, 4))
    return arranged.reshape(2, 2, outputs, planes, coarse_rows * columns)


def up_backward(grad_ext, coarse, weights, columns):
    outputs = grad_ext.shape[0]
    channels, planes = (coarse.shape[0], coarse.shape[1])
    cells_all = planes * coarse.shape[2]
    flat_coarse = coarse.reshape(channels, cells_all)
    chosen = {
        (0, 0): grad_ext[:, 1 : 2 * planes : 2],
        (1, 0): grad_ext[:, 2 : 2 * planes + 1 : 2],
        (1, 1): grad_ext[:, 0 : 2 * planes : 2],
    }
    parted = {}
    for choice_key in chosen:
        parted[choice_key] = split_parity(chosen[choice_key], columns)
    d_coarse = jnp.zeros((channels, cells_all), jnp.float32)
    tap_grads = [None] * 27
    for z_par in (0, 1):
        for y_par in (0, 1):
            for x_par in (0, 1):
                left_parts = []
                right_parts = []
                for k_z, z_off in PARITY_TAPS[z_par]:
                    for k_y, y_off in PARITY_TAPS[y_par]:
                        for k_x, x_off in PARITY_TAPS[x_par]:
                            tap_index = k_z * 9 + k_y * 3 + k_x
                            source = parted[z_par, z_off][y_par, x_par]
                            shifted_grad = plane_shift(source, -y_off, -x_off, columns).reshape(
                                outputs, cells_all
                            )
                            left_parts.append(weights[tap_index])
                            right_parts.append(shifted_grad)
                            tap_grads[tap_index] = jnp.dot(
                                shifted_grad, flat_coarse.T, preferred_element_type=jnp.float32
                            )
                matrix = jnp.concatenate(left_parts, axis=0)
                stacked = jnp.concatenate(right_parts, axis=0)
                d_coarse = d_coarse + jnp.dot(matrix.T, stacked, preferred_element_type=jnp.float32)
    return (d_coarse.reshape(coarse.shape), jnp.stack(tap_grads))


def unfold(padded, columns):
    planes = padded.shape[1] - 2
    pieces = []
    for tap_index in range(27):
        k_z, k_y, k_x = (tap_index // 9, tap_index // 3 % 3, tap_index % 3)
        pieces.append(plane_shift(padded[:, k_z : k_z + planes], k_y - 1, k_x - 1, columns))
    return jnp.stack(pieces).reshape(27 * padded.shape[0], planes * padded.shape[2])


def spread_forward(gathered, weights, columns):
    channels, padded_planes, plane_cells = gathered.shape
    planes = padded_planes - 2
    outputs = weights.shape[1]
    mixture = jnp.dot(
        weights.reshape(27 * outputs, channels),
        gathered.reshape(channels, -1),
        preferred_element_type=jnp.float32,
    )
    mixture = mixture.reshape(27, outputs, padded_planes, plane_cells)
    result = jnp.zeros((outputs, planes, plane_cells), jnp.float32)
    for tap_index in range(27):
        k_z, k_y, k_x = (tap_index // 9, tap_index // 3 % 3, tap_index % 3)
        result = result + plane_shift(
            mixture[tap_index, :, k_z : k_z + planes], k_y - 1, k_x - 1, columns
        )
    return result


def spread_backward(gathered, weights, columns):
    outputs, padded_planes, plane_cells = gathered.shape
    planes = padded_planes - 2
    channels = weights.shape[2]
    flipped = jnp.transpose(weights, (0, 2, 1)).reshape(27 * channels, outputs)
    mixture = jnp.dot(flipped, gathered.reshape(outputs, -1), preferred_element_type=jnp.float32)
    mixture = mixture.reshape(27, channels, padded_planes, plane_cells)
    result = jnp.zeros((channels, planes, plane_cells), jnp.float32)
    for tap_index in range(27):
        k_z, k_y, k_x = (tap_index // 9, tap_index // 3 % 3, tap_index % 3)
        result = result + plane_shift(
            mixture[tap_index, :, 2 - k_z : 2 - k_z + planes], 1 - k_y, 1 - k_x, columns
        )
    return result


def layer_forward(padded, weights, columns):
    regrouped = lax.all_to_all(weights, "ch", split_axis=1, concat_axis=2, tiled=True)
    gathered = lax.all_gather(padded, "ch", axis=0, tiled=True)
    return spread_forward(gathered, regrouped, columns)


def layer_backward(grad, weights, unfolded, columns):
    grad_in = padded_2(grad, (("gz", 1),), 1)
    gathered = lax.all_gather(grad_in, "ch", axis=0, tiled=True)
    d_input = spread_backward(gathered, weights, columns)
    planes = grad.shape[1]
    outputs = gathered.shape[0]
    interior = gathered[:, 1 : planes + 1].reshape(outputs, -1)
    d_weight = lax.dot_general(
        interior, unfolded, (((1,), (1,)), ((), ())), preferred_element_type=jnp.float32
    )
    return (d_input, jnp.transpose(d_weight.reshape(outputs, 27, -1), (1, 0, 2)))


def normalize(summed, voxels):
    centre = lax.psum(jnp.sum(summed, axis=(1, 2)), "gz") / voxels
    deviation = summed - centre[:, None, None]
    spread = lax.psum(jnp.sum(deviation * deviation, axis=(1, 2)), "gz") / voxels
    inverse = lax.rsqrt(spread + NORM_EPS)
    return ((summed - centre[:, None, None]) * inverse[:, None, None], inverse)


def norm_back(slope_grad, normed, inverse, voxels):
    totals = lax.psum(
        (jnp.sum(slope_grad, axis=(1, 2)), jnp.sum(slope_grad * normed, axis=(1, 2))), "gz"
    )
    mean_grad = (totals[0] / voxels)[:, None, None]
    mean_cross = (totals[1] / voxels)[:, None, None]
    return inverse[:, None, None] * (slope_grad - mean_grad - normed * mean_cross)


def local(coarse, encoder_skip, up_weight, first_up, first_skip, second_weight, cotangent):
    fine_columns = 2 * XC
    share_out = C_OUT // lax.axis_size("ch")
    slab_cells = encoder_skip.shape[1] * encoder_skip.shape[2]
    voxels = lax.axis_size("gz") * slab_cells
    following = passed_along(coarse, "gz", -1)
    extended = jnp.concatenate([coarse, following], axis=1)
    regrouped_up = lax.all_to_all(up_weight, "ch", split_axis=1, concat_axis=2, tiled=True)
    parities = up_forward(lax.all_gather(extended, "ch", axis=0, tiled=True), regrouped_up, XC)
    upsampled = alternate(parities, coarse.shape[1], XC).astype(jnp.bfloat16)
    joined = jnp.concatenate([upsampled, encoder_skip], axis=0)
    first_in = padded_2(joined, (("gz", 1),), 1)
    first_weight = jnp.concatenate([first_up, first_skip], axis=2)
    first_cols = unfold(first_in, fine_columns)
    first_pre = layer_forward(first_in, first_weight, fine_columns)
    first_normed, first_inverse = normalize(first_pre, voxels)
    hidden = activate(first_normed).astype(jnp.bfloat16)
    second_in = padded_2(hidden, (("gz", 1),), 1)
    second_cols = unfold(second_in, fine_columns)
    second_pre = layer_forward(second_in, second_weight, fine_columns)
    second_normed, second_inverse = normalize(second_pre, voxels)
    decoded = activate(second_normed).astype(jnp.bfloat16)
    slope_two = cotangent.astype(jnp.float32) * activate_slope(second_normed)
    d_second = norm_back(slope_two, second_normed, second_inverse, voxels).astype(jnp.bfloat16)
    d_hidden, grad_second = layer_backward(d_second, second_weight, second_cols, fine_columns)
    slope_one = d_hidden * activate_slope(first_normed)
    d_first = norm_back(slope_one, first_normed, first_inverse, voxels).astype(jnp.bfloat16)
    d_joined, grad_first = layer_backward(d_first, first_weight, first_cols, fine_columns)
    d_up = d_joined[:share_out].astype(jnp.bfloat16)
    grad_skip = d_joined[share_out:].astype(jnp.bfloat16)
    previous = passed_along(d_up[:, -1:], "gz", 1)
    grad_ext = jnp.concatenate([previous, d_up], axis=1)
    d_part, w_part = up_backward(
        lax.all_gather(grad_ext, "ch", axis=0, tiled=True), coarse, up_weight, XC
    )
    summed = lax.psum((w_part, grad_first, grad_second), "gz")
    factor = 1.0 / math.sqrt(slab_cells)
    return (
        decoded,
        d_part.astype(jnp.bfloat16),
        grad_skip,
        summed[0] * factor,
        summed[1][:, :, :share_out] * factor,
        summed[1][:, :, share_out:] * factor,
        summed[2] * factor,
    )


def solution(mesh):
    return jax.shard_map(
        local,
        mesh=mesh,
        in_specs=(
            P("ch", "gz", None),
            P("ch", "gz", None),
            P(None, None, "ch"),
            P(None, None, "ch"),
            P(None, None, "ch"),
            P(None, None, "ch"),
            P("ch", "gz", None),
        ),
        out_specs=(
            P("ch", "gz", None),
            P("ch", "gz", None),
            P("ch", "gz", None),
            P(None, None, "ch"),
            P(None, None, "ch"),
            P(None, None, "ch"),
            P(None, None, "ch"),
        ),
        check_vma=False,
    )
```

profile of v0, /device:TPU:10, one launch (start us, length us, event | category | flops | bytes accessed | tf_op | source)
XLA Modules:
  0.0 1133.7 jit_solution(5758793602280112466)
XLA Ops:
  7.2 2.5 collective-permute-start
  11.1 1.5 reshape.825
  12.6 9.2 all-to-all-start.1
  22.6 1.5 slice_bitcast_fusion.133
  31.7 1.5 reshape.827
  33.3 17.9 %all_gather.18 = bf16[256,2,128]{2,0,1:T(8,128)(2,1)S(1)} all-gather(bf16[16,2,128]{2,0,1:T(8,128)(2,1)S(1)} %pad_maximum_fusion.25), channel_id=1, replica_groups=mesh['gz'=32,'ch'=16] {'ch'}, dimensions={0}, use_global_device_ids=true | all-gather | bytes 139264 | tf_op jit(solution)/shard_map/all_gather | solution.py:228
  57.8 6.1 all-to-all-start.2
  65.2 3.3 fusion.634
  68.5 5.2 fusion.633
  73.7 1.9 copy.197
  76.3 2.5 copy.199
  78.9 1.5 squeeze.584
  80.3 2.5 copy.198
  82.8 1.4 squeeze.583
  84.2 2.5 copy.196
  86.7 1.4 squeeze.581
  88.1 2.5 copy.195
  90.6 1.4 squeeze.580
  92.1 2.5 copy.194
  94.5 1.4 squeeze.579
  96.0 2.5 copy.193
  98.5 1.4 squeeze.578
  99.9 1.5 copy.192
  102.4 1.9 copy.218
  105.0 1.9 copy.217
  107.6 1.9 copy.216
  110.1 1.9 copy.215
  112.7 1.9 copy.214
  115.3 1.9 copy.213
  119.4 1.9 copy.211
  121.4 1.9 copy.210
  124.0 1.9 copy.209
  126.5 1.9 copy.208
  129.1 1.9 copy.207
  131.7 1.9 copy.206
  143.1 5.8 all-to-all-start
  148.9 1.9 collective-permute-start.1
  150.8 4.1 collective-permute-start.2
  155.6 1.7 copy.225
  159.5 1.7 copy.190
  164.8 38.0 %all-gather.2.cloned.1.call-done = bf16[256,4,512]{2,0,1:T(8,128)(2,1)} async-done(((bf16[16,4,512]{2,0,1:T(8,128)(2,1)}), bf16[256,4,512]{2,0,1:T(8,128)(2,1)}) %all-gather.2.cloned.1.call-update) | async-done | bytes 1048592 | tf_op jit(solution)/shard_map/all_gather | solution.py:186
  202.8 1.5 copy.222
  205.2 78.8 %psum.77 = f32[8]{0:T(128)S(1)} all-reduce(f32[8]{0:T(128)S(1)} %get-tuple-element.50), channel_id=1, replica_groups=mesh['gz'=32,'ch'=16] {'gz'}, use_global_device_ids=true, to_apply=%region_1.2 | all-reduce | flops 8 | bytes 64 | tf_op jit(solution)/shard_map/psum | solution.py:204
  284.3 81.6 %psum.78 = f32[8]{0:T(128)S(1)} all-reduce(f32[8]{0:T(128)S(1)} %multiply_reduce_fusion.3), channel_id=1, replica_groups=mesh['gz'=32,'ch'=16] {'gz'}, use_global_device_ids=true, to_apply=%region_3.4 | all-reduce | flops 8 | bytes 64 | tf_op jit(solution)/shard_map/psum | solution.py:206
  366.0 1.9 collective-permute-start.3
  368.0 3.9 collective-permute-start.4
  372.0 1.5 collective-permute-done.4
  373.5 18.2 %all_gather.20 = bf16[128,4,512]{2,0,1:T(8,128)(2,1)S(1)} all-gather(bf16[8,4,512]{2,0,1:T(8,128)(2,1)S(1)} %pad_maximum_fusion.19), channel_id=1, replica_groups=mesh['gz'=32,'ch'=16] {'ch'}, dimensions={0}, use_global_device_ids=true | all-gather | bytes 557056 | tf_op jit(solution)/shard_map/all_gather | solution.py:186
  394.8 78.8 %psum.79 = f32[8]{0:T(128)S(1)} all-reduce(f32[8]{0:T(128)S(1)} %get-tuple-element.48), channel_id=1, replica_groups=mesh['gz'=32,'ch'=16] {'gz'}, use_global_device_ids=true, to_apply=%region_5.6 | all-reduce | flops 8 | bytes 64 | tf_op jit(solution)/shard_map/psum | solution.py:204
  474.0 76.8 %psum.80 = f32[8]{0:T(128)S(1)} all-reduce(f32[8]{0:T(128)S(1)} %multiply_reduce_fusion.2), channel_id=1, replica_groups=mesh['gz'=32,'ch'=16] {'gz'}, use_global_device_ids=true, to_apply=%region_7.8 | all-reduce | flops 8 | bytes 64 | tf_op jit(solution)/shard_map/psum | solution.py:206
  551.0 78.9 %all-reduce.113 = (f32[8]{0:T(128)S(1)}, f32[8]{0:T(128)S(1)}) all-reduce(f32[8]{0:T(128)S(1)} %get-tuple-element.38, f32[8]{0:T(128)S(1)} %get-tuple-element.37), channel_id=1, replica_groups=mesh['gz'=32,'ch'=16] {'gz'}, use_global_device_ids=true, to_apply=%region_11.12 | all-reduce | flops 16 | bytes 128 | tf_op jit(solution)/shard_map/psum | solution.py:212
  630.1 1.9 collective-permute-start.5
  632.0 3.9 collective-permute-start.6
  637.6 19.0 %all_gather.21 = bf16[128,4,512]{2,0,1:T(8,128)(2,1)S(1)} all-gather(bf16[8,4,512]{2,0,1:T(8,128)(2,1)S(1)} %pad_maximum_fusion.20), channel_id=1, replica_groups=mesh['gz'=32,'ch'=16] {'ch'}, dimensions={0}, use_global_device_ids=true | all-gather | bytes 557056 | tf_op jit(solution)/shard_map/all_gather | solution.py:192
  657.9 78.8 %all-reduce.112 = (f32[8]{0:T(128)S(1)}, f32[8]{0:T(128)S(1)}) all-reduce(f32[8]{0:T(128)S(1)} %get-tuple-element.36, f32[8]{0:T(128)S(1)} %get-tuple-element.35), channel_id=1, replica_groups=mesh['gz'=32,'ch'=16] {'gz'}, use_global_device_ids=true, to_apply=%region_15.16 | all-reduce | flops 16 | bytes 128 | tf_op jit(solution)/shard_map/psum | solution.py:212
  736.8 1.9 collective-permute-start.7
  738.8 3.9 collective-permute-start.8
  744.3 19.7 %all_gather.22 = bf16[128,4,512]{2,0,1:T(8,128)(2,1)S(1)} all-gather(bf16[8,4,512]{2,0,1:T(8,128)(2,1)S(1)} %pad_maximum_fusion.21), channel_id=1, replica_groups=mesh['gz'=32,'ch'=16] {'ch'}, dimensions={0}, use_global_device_ids=true | all-gather | bytes 557056 | tf_op jit(solution)/shard_map/all_gather | solution.py:192
  765.6 1.9 collective-permute-start.9
  767.6 1.4 convolution_bitcast_fusion
  769.6 1.6 collective-permute-done.9
  771.2 18.7 %all_gather.23 = bf16[128,3,512]{2,0,1:T(8,128)(2,1)S(1)} all-gather(bf16[8,3,512]{2,0,1:T(8,128)(2,1)S(1)} %pad_maximum_fusion.22), channel_id=1, replica_groups=mesh['gz'=32,'ch'=16] {'ch'}, dimensions={0}, use_global_device_ids=true | all-gather | bytes 417792 | tf_op jit(solution)/shard_map/all_gather | solution.py:253
  799.2 321.7 %all-reduce.117.cloned.1.call-done = (f32[27,128,16]{1,2,0:T(8,128)}, f32[27,128,16]{1,0,2:T(8,128)}, f32[27,128,8]{1,0,2:T(8,128)}) async-done(((f32[27,128,16]{1,2,0:T(8,128)}, f32[27,128,16]{1,0,2:T(8,128)}, f32[27,128,8]{1,0,2:T(8,128)}), (f32[27,128,16]{1,2,0:T(8,128)}, f32[27,128,16]{1,0,2:T(8,128)}, f32[27,128,8]{1,0,2:T(8,128)})) %all-reduce.117.cloned.1.call-update) | async-done | bytes 552976 | tf_op jit(solution)/shard_map/psum | solution.py:255
  1120.9 1.6 broadcast_multiply_fusion
  (377 shorter events, 68.6 us)
Async XLA Ops:
  7.2 22.6 %copy-start.13 = (bf16[27,128,8]{1,2,0:T(8,128)(2,1)S(1)}, bf16[27,128,8]{1,2,0:T(8,128)(2,1)}, u32[]{:S(2)}) copy-start(bf16[27,128,8]{1,2,0:T(8,128)(2,1)} %param.11) | copy-start | bytes 165892
  7.2 22.7 %copy-start.23 = (bf16[8,2,512]{2,1,0:T(2,128)(2,1)S(1)}, bf16[8,2,512]{2,1,0:T(2,128)(2,1)}, u32[]{:S(2)}) copy-start(bf16[8,2,512]{2,1,0:T(2,128)(2,1)} %param.8) | copy-start | bytes 49156
  7.2 22.7 %copy-start.5 = (bf16[27,128,8]{1,2,0:T(8,128)(2,1)S(1)}, bf16[27,128,8]{1,2,0:T(8,128)(2,1)}, u32[]{:S(2)}) copy-start(bf16[27,128,8]{1,2,0:T(8,128)(2,1)} %param.12) | copy-start | bytes 165892
  7.2 26.1 %collective-permute-start = (bf16[16,1,128]{2,0,1:T(8,128)(2,1)}, bf16[16,1,128]{2,0,1:T(8,128)(2,1)S(1)}, u32[]{:S(2)}, u32[]{:S(2)}) collective-permute-start(bf16[16,1,128]{2,0,1:T(8,128)(2,1)} %param.7), channel_id=1, source_target_pairs={{16,0},{32,16},{48,32},{64,48},{80,64},{96,80},{112,96},{128,112},... | collective-permute-start | bytes 12296 | tf_op jit(solution)/shard_map/ppermute | solution.py:34
  11.1 22.2 %copy-start.3 = (bf16[16,1,128]{2,0,1:T(8,128)(2,1)S(1)}, bf16[16,1,128]{2,0,1:T(8,128)(2,1)}, u32[]{:S(2)}) copy-start(bf16[16,1,128]{2,0,1:T(8,128)(2,1)} %param.7) | copy-start | bytes 12292
  12.6 45.2 %all-to-all-start.1 = ((bf16[16,2,1728]{2,1,0:T(2,128)(2,1)}), bf16[16,2,1728]{2,1,0:T(2,128)(2,1)S(1)}, u32[]{:S(2)}, u32[]{:S(2)}) async-start(bf16[16,2,1728]{2,1,0:T(2,128)(2,1)} %reshape.825), calls=%async_computation.1 | async-start | bytes 229376 | tf_op jit(solution)/shard_map/all_to_all | solution.py:227
  29.0 24.4 %copy-start.14 = (bf16[1024,16]{0,1:T(8,128)(2,1)}, bf16[1024,16]{0,1:T(8,128)(2,1)S(1)}, u32[]{:S(2)}) copy-start(bf16[1024,16]{0,1:T(8,128)(2,1)S(1)} %constant_dynamic-update-slice_fusion.18) | copy-start | bytes 98308
  57.8 85.3 %all-to-all-start.2 = ((bf16[16,2,864]{2,1,0:T(2,128)(2,1)}), bf16[16,2,864]{2,1,0:T(2,128)(2,1)S(1)}, u32[]{:S(2)}, u32[]{:S(2)}) async-start(bf16[16,2,864]{2,1,0:T(2,128)(2,1)} %reshape.829), calls=%async_computation.2 | async-start | bytes 114688 | tf_op jit(solution)/shard_map/all_to_all | solution.py:185
  76.3 23.6 %copy-start.2 = (bf16[1,8,16,16]{0,3,1,2:T(8,128)(2,1)S(1)}, bf16[1,8,16,16]{0,3,1,2:T(8,128)(2,1)}, u32[]{:S(2)}) copy-start(bf16[1,8,16,16]{0,3,1,2:T(8,128)(2,1)} %get-tuple-element.174) | copy-start | bytes 12292
  102.4 15.4 %copy-start.1 = (bf16[1,8,16,16]{0,3,1,2:T(8,128)(2,1)S(1)}, bf16[1,8,16,16]{0,3,1,2:T(8,128)(2,1)}, u32[]{:S(2)}) copy-start(bf16[1,8,16,16]{0,3,1,2:T(8,128)(2,1)} %get-tuple-element.154) | copy-start | bytes 12292
  119.4 14.9 %copy-start = (bf16[1,8,16,16]{0,3,1,2:T(8,128)(2,1)S(1)}, bf16[1,8,16,16]{0,3,1,2:T(8,128)(2,1)}, u32[]{:S(2)}) copy-start(bf16[1,8,16,16]{0,3,1,2:T(8,128)(2,1)} %get-tuple-element.161) | copy-start | bytes 12292
  134.2 6.1 copy-start.7
  135.1 5.1 copy-start.22
  135.1 5.1 copy-start.21
  135.1 5.2 copy-start.20
  135.1 5.2 copy-start.19
  135.1 5.2 copy-start.18
  135.1 5.2 copy-start.17
  135.1 5.2 copy-start.16
  135.1 5.2 copy-start.11
  135.1 5.2 copy-start.48
  135.1 5.2 copy-start.49
  135.2 5.4 copy-start.10
  135.2 5.4 copy-start.46
  135.2 5.4 copy-start.47
  135.2 5.5 copy-start.8
  135.2 5.5 copy-start.43
  135.2 5.5 copy-start.44
  135.2 5.5 copy-start.45
  136.3 4.6 copy-start.6
  137.2 3.9 copy-start.12
  137.2 3.9 copy-start.54
  143.1 15.1 %all-to-all-start = ((bf16[16,2,1728]{2,1,0:T(2,128)(2,1)}), bf16[16,2,1728]{2,1,0:T(2,128)(2,1)S(1)}, u32[]{:S(2)}, u32[]{:S(2)}) async-start(bf16[16,2,1728]{2,1,0:T(2,128)(2,1)} %reshape.827), calls=%async_computation | async-start | bytes 229376 | tf_op jit(solution)/shard_map/all_to_all | solution.py:185
  148.8 53.9 %all-gather.2.cloned.1.call-start = ((), (), s32[]{:S(2)}) async-start(), calls=%async_computation.3 | async-start | bytes 1114112 | tf_op jit(solution)/shard_map/all_gather | solution.py:186
  148.9 13.2 %collective-permute-start.1 = (bf16[16,1,512]{2,0,1:T(8,128)(2,1)S(1)}, bf16[16,1,512]{2,0,1:T(8,128)(2,1)S(1)}, u32[]{:S(2)}, u32[]{:S(2)}) collective-permute-start(bf16[16,1,512]{2,0,1:T(8,128)(2,1)S(1)} %get-tuple-element.238), channel_id=1, source_target_pairs={{0,16},{16,32},{32,48},{48,64},{64,80},{80,96},{96,112},{112,128},... | collective-permute-start | bytes 49160 | tf_op jit(solution)/shard_map/ppermute | solution.py:23
  150.8 11.3 collective-permute-start.2
  162.8 958.1 %all-reduce.117.cloned.1.call-start = ((), (), s32[]{:S(2)}) async-start(), calls=%async_computation.4 | async-start | bytes 1228800 | tf_op jit(solution)/shard_map/psum | solution.py:255
  366.0 5.9 collective-permute-start.3
  368.0 5.5 collective-permute-start.4
  372.0 20.5 %copy-start.55 = (bf16[27,16,2,512]{3,1,2,0:T(8,128)(2,1)}, bf16[27,16,2,512]{3,1,2,0:T(8,128)(2,1)S(1)}, u32[]{:S(2)}) copy-start(bf16[27,16,2,512]{3,1,2,0:T(8,128)(2,1)S(1)} %constant_dynamic-update-slice_fusion.34) | copy-start | bytes 2654212
  392.5 158.3 %copy-start.24 = (bf16[8,2,512]{2,1,0:T(2,128)(2,1)S(1)}, bf16[8,2,512]{2,1,0:T(2,128)(2,1)}, u32[]{:S(2)}) copy-start(bf16[8,2,512]{2,1,0:T(2,128)(2,1)} %param.13) | copy-start | bytes 49156
  630.1 6.6 collective-permute-start.5
  632.0 5.5 collective-permute-start.6
  736.8 6.9 collective-permute-start.7
  738.8 5.5 collective-permute-start.8
  765.6 5.5 collective-permute-start.9
  791.7 5.6 copy-start.41
  791.7 5.7 copy-start.42
  791.8 5.7 copy-start.39
  791.8 5.6 copy-start.40
  791.8 5.8 copy-start.35
  791.8 5.8 copy-start.36
  791.8 5.8 copy-start.37
  791.8 5.8 copy-start.38
  792.9 4.8 copy-start.33
  792.9 4.8 copy-start.34
  793.4 4.6 copy-start.29
  793.4 4.6 copy-start.30
  793.4 4.6 copy-start.31
  793.4 4.6 copy-start.32
  794.7 3.5 copy-start.25
  794.7 3.5 copy-start.26
  794.7 3.5 copy-start.27
  794.7 3.5 copy-start.28
  (8 other events, 20.3 us)
Sparse Core Ops, SparseCore 0:
  162.9 39.7 all-gather.1
  797.4 323.4 all-reduce.116
where the time goes:
time: 1140 us; the launch traced here: 1130 us
  blocking collectives  567 us (50%)
  waiting for transfers between devices  364 us (32%)
  local copies, waits for them, and re-layouts  111 us (10%)
  starting transfers between devices  49.1 us (4%)
  between operations  15.6 us (1%)
  matrix products  14.2 us (1%)
  other arithmetic  12 us (1%)
    psum x1, waiting for transfers between devices, local(): summed = lax.psum((w_part, grad_first, grad_second), 'gz')  322 us
    psum x2, blocking collectives, normalize(): lax.psum(jnp.sum(deviation * deviation, axis=(1, 2)), 'gz') / voxels  158 us
    psum x2, blocking collectives, norm_back(): lax.psum((jnp.sum(slope_grad, axis=(1, 2)), jnp.sum(slope_grad * normed,...  158 us
    psum x2, blocking collectives, normalize(): centre = lax.psum(jnp.sum(summed, axis=(1, 2)), 'gz') / voxels  158 us
    slice x29, local copies, waits for them, and re-layouts, up_forward(): left_parts.append(weights[k_z * 9 + k_y * 3 + k_x])  55 us
    all_gather x2, blocking collectives, layer_backward(): gathered = lax.all_gather(grad_in, 'ch', axis=0, tiled=True)  38.8 us
    all_gather x1, waiting for transfers between devices, layer_forward(): gathered = lax.all_gather(padded, 'ch', axis=0, tiled=True)  38 us
    unnamed x150, local copies, waits for them, and re-layouts  23 us
  transfers between devices with their start and end apart: 15, of which 6 were waited for; matrix products, arithmetic and copies ran while one was open for 10% of the time, Pallas kernels for 0%

commit v1 on v0

v1 whole, which is shorter than its diff:
```python
import math

import jax
import jax.numpy as jnp
from jax import lax
from jax.experimental import pallas as pl
from jax.experimental.pallas import tpu as pltpu
from jax.sharding import PartitionSpec as P

C_OUT = 128
XC = 16
YC = 8
COARSE = YC * XC
FINE = 4 * COARSE
SLAB = 2 * FINE
HALOED = 4 * FINE
LEAK_SLOPE = 0.01
KINK_WIDTH = 0.01
NORM_EPS = 1e-05
PARITY = (((1, 0),), ((2, 0), (0, 1)))
GRAD_ROWS = 1280

f32 = jnp.float32
bf16 = jnp.bfloat16


def activate(u):
    q = u * u + KINK_WIDTH
    return 0.5 * (1.0 + LEAK_SLOPE) * u + 0.5 * (1.0 - LEAK_SLOPE) * (q * lax.rsqrt(q))


def activate_slope(u):
    return 0.5 * (1.0 + LEAK_SLOPE) + 0.5 * (1.0 - LEAK_SLOPE) * (
        u * lax.rsqrt(u * u + KINK_WIDTH)
    )


def shift(values, step_y, step_x, rows, columns):
    if step_y == 0 and step_x == 0:
        return values
    extent = values.shape[-1]
    cell = lax.broadcasted_iota(jnp.int32, (1, extent), 1)
    column = cell % columns + step_x
    row = cell // columns % rows + step_y
    inside = (column >= 0) & (column < columns) & (row >= 0) & (row < rows)
    moved = pltpu.roll(values, (-(step_y * columns + step_x)) % extent, 1)
    return moved * jnp.where(inside, 1.0, 0.0)


def fine_shift(values, step_y, step_x):
    return shift(values, step_y, step_x, 2 * YC, 2 * XC)


def coarse_shift(values, step_y, step_x):
    return shift(values, step_y, step_x, YC, XC)


def interleave_matrix(transposed):
    fine_dim = 0 if transposed else 1
    cell = lax.broadcasted_iota(jnp.int32, (FINE, FINE), fine_dim)
    other = lax.broadcasted_iota(jnp.int32, (FINE, FINE), 1 - fine_dim)
    y, x = cell // (2 * XC), cell % (2 * XC)
    source = ((y % 2) * 2 + x % 2) * COARSE + (y // 2) * XC + x // 2
    return jnp.where(source == other, 1.0, 0.0).astype(bf16)


def edge_mask(slab, slabs):
    plane = lax.broadcasted_iota(jnp.int32, (1, HALOED), 1) // FINE
    outside = ((plane == 0) & (slab == 0)) | ((plane == 3) & (slab == slabs - 1))
    return jnp.where(outside, 0.0, 1.0)


def as_row(column):
    return jnp.transpose(jnp.broadcast_to(column, (C_OUT, C_OUT)))[:1]


def as_column(row):
    return jnp.transpose(jnp.broadcast_to(row, (C_OUT, C_OUT)))[:, :1]


def call(kernel, outs, args, scratch=(), megabytes=24):
    specs = [pl.BlockSpec(memory_space=pltpu.SMEM)]
    specs += [pl.BlockSpec(memory_space=pltpu.VMEM)] * (len(args) - 1)
    return pl.pallas_call(
        kernel,
        out_shape=[jax.ShapeDtypeStruct(shape, dtype) for shape, dtype in outs],
        in_specs=specs,
        out_specs=[pl.BlockSpec(memory_space=pltpu.VMEM)] * len(outs),
        scratch_shapes=list(scratch),
        compiler_params=pltpu.CompilerParams(vmem_limit_bytes=megabytes * 2**20),
    )(*args)


def up_kernel(place, mixed, own_skip, skip_low, skip_high, first_up, first_skip, partial, joined, unfolded):
    slab = place[0]
    packed = mixed[...]
    weights = packed[:, :, :256].reshape(256, 256)
    mixture = []
    for plane in range(3):
        source = packed[:, :, 256 + plane * COARSE : 256 + (plane + 1) * COARSE].reshape(256, COARSE)
        mixture.append(
            lax.dot_general(weights, source, (((0,), (0,)), ((), ())), preferred_element_type=f32)
        )
    rows = []
    for sources in (((2, 0), (0, 1)), ((1, 1),), ((2, 1), (0, 2)), ((1, 2),)):
        cells = []
        for y_par in (0, 1):
            for x_par in (0, 1):
                total = None
                for k_z, plane in sources:
                    for k_y, y_off in PARITY[y_par]:
                        for k_x, x_off in PARITY[x_par]:
                            tap = k_z * 9 + k_y * 3 + k_x
                            term = coarse_shift(mixture[plane][tap * 8 : tap * 8 + 8], y_off, x_off)
                            total = term if total is None else total + term
                cells.append(total)
        rows.append(jnp.concatenate(cells, axis=1))
    spread = jnp.concatenate(rows, axis=0).astype(bf16)
    fine = jnp.dot(spread, interleave_matrix(False), preferred_element_type=f32)
    first_inside = jnp.where(slab == 0, 0.0, 1.0)
    upsampled = jnp.concatenate(
        [fine[0:8] * first_inside, fine[8:16], fine[16:24], fine[24:32]], axis=1
    )
    skip = jnp.concatenate(
        [skip_low[...].astype(f32), own_skip[...].astype(f32), skip_high[...].astype(f32)], axis=1
    )
    features = jnp.concatenate([upsampled, skip], axis=0)
    joined[...] = features.astype(bf16)
    for tap in range(9):
        unfolded[tap * 16 : tap * 16 + 16, :] = fine_shift(features, tap // 3 - 1, tap % 3 - 1).astype(bf16)
    total = jnp.zeros((C_OUT, SLAB), f32)
    for k_z in range(3):
        matrix = []
        for tap in range(9):
            up_part = first_up[k_z * 9 + tap].astype(f32)
            skip_part = first_skip[k_z * 9 + tap].astype(f32)
            matrix.append(jnp.concatenate([up_part, skip_part], axis=0))
        matrix = jnp.concatenate(matrix, axis=0).astype(bf16)
        total = total + lax.dot_general(
            matrix,
            unfolded[:, k_z * FINE : k_z * FINE + SLAB],
            (((0,), (0,)), ((), ())),
            preferred_element_type=f32,
        )
    partial[...] = total.reshape(16, 8, SLAB)


def first_sum_kernel(place, parts, pre, low, high, stats):
    total = jnp.sum(parts[...], axis=0)
    pre[...] = total
    low[...] = total[:, :FINE]
    high[...] = total[:, FINE:]
    mean = jnp.sum(total, axis=1, keepdims=True) / SLAB
    deviation = total - mean
    square = jnp.sum(deviation * deviation, axis=1, keepdims=True)
    lane = lax.broadcasted_iota(jnp.int32, (8, 128), 1)
    tile = jnp.where(lane < 64, mean, square)
    stats[...] = jnp.broadcast_to(tile[None], stats.shape)


def first_norm_kernel(place, pre, low, high, stats, cotangent, cot_low, cot_high, packed):
    slabs = stats.shape[0]
    gathered = stats[...]
    means = gathered[:, :, :1]
    mean = jnp.sum(means, axis=0) / slabs
    apart = means - mean[None]
    square = jnp.sum(gathered[:, :, 127:] + SLAB * apart * apart, axis=0)
    inverse = lax.rsqrt(square / (slabs * SLAB) + NORM_EPS)
    lower = jnp.concatenate([low[...], pre[:, :FINE]], axis=1)
    upper = jnp.concatenate([pre[:, FINE:], high[...]], axis=1)
    cot = cotangent[...].astype(f32)
    cot_lower = jnp.concatenate([cot_low[...].astype(f32), cot[:, :FINE]], axis=1)
    cot_upper = jnp.concatenate([cot[:, FINE:], cot_high[...].astype(f32)], axis=1)
    wide = jnp.broadcast_to(inverse, (8, 128))
    main = wide.astype(bf16).astype(f32)
    block = jnp.concatenate(
        [
            jnp.concatenate([(lower - mean) * inverse, cot_lower, main], axis=1),
            jnp.concatenate([(upper - mean) * inverse, cot_upper, wide - main], axis=1),
        ],
        axis=0,
    ).astype(bf16)
    for target in range(16):
        packed[target] = block


def read_planes(packed, block, offset):
    pair = packed[pl.ds(2 * block, 2), :, offset : offset + SLAB].astype(f32)
    return jnp.concatenate([pair[:, :8].reshape(16, SLAB), pair[:, 8:].reshape(16, SLAB)], axis=1)


def unfold_block(values, unfolded, block, sign):
    for tap in range(9):
        moved = fine_shift(values, sign * (tap // 3 - 1), sign * (tap % 3 - 1))
        unfolded[pl.ds(pl.multiple_of(tap * 128 + block * 16, 16), 16), :] = moved.astype(bf16)


def tap_matrix(weights, tap, first):
    both = weights[:, tap].astype(f32)
    return both[:, first * 8 : first * 8 + 8].reshape(C_OUT, C_OUT)


def second_conv_kernel(place, packed, weights, pre, low, high, stats, unfolded, matrix):
    mask = edge_mask(place[0], stats.shape[0])

    def prepare(block, carry):
        hidden = activate(read_planes(packed, block, 0)).astype(bf16).astype(f32) * mask
        unfold_block(hidden, unfolded, block, 1)
        return carry

    lax.fori_loop(0, 8, prepare, 0)
    for tap in range(27):
        matrix[:, tap * 128 : tap * 128 + 128] = jnp.transpose(tap_matrix(weights, tap, 0)).astype(bf16)
    total = jnp.zeros((C_OUT, SLAB), f32)
    for k_z in range(3):
        total = total + jnp.dot(
            matrix[:, k_z * 1152 : k_z * 1152 + 1152],
            unfolded[:, k_z * FINE : k_z * FINE + SLAB],
            preferred_element_type=f32,
        )
    pre[...] = total
    mean = jnp.sum(total, axis=1, keepdims=True) / SLAB
    deviation = total - mean
    square = jnp.sum(deviation * deviation, axis=1, keepdims=True)
    low[...] = deviation[:, :FINE].astype(bf16)
    high[...] = deviation[:, FINE:].astype(bf16)
    row = lax.broadcasted_iota(jnp.int32, (8, 128), 0)
    tile = jnp.where(row < 4, as_row(mean), as_row(square))
    stats[...] = jnp.broadcast_to(tile[None], stats.shape)


def second_norm_kernel(
    place, pre, low, high, stats, packed, decoded, normed, slope, inverse_out, sums
):
    slab, share = place[0], place[1]
    slabs = stats.shape[0]
    gathered = stats[...]
    means = gathered[:, 0:1]
    mean_row = jnp.sum(means, axis=0) / slabs
    apart = means - mean_row[None]
    square = jnp.sum(gathered[:, 7:8] + SLAB * apart * apart, axis=0)
    inverse_row = lax.rsqrt(square / (slabs * SLAB) + NORM_EPS)
    inverse_out[...] = jnp.broadcast_to(inverse_row, inverse_out.shape)
    below = stats[jnp.maximum(slab - 1, 0)][0:1] - mean_row
    above = stats[jnp.minimum(slab + 1, slabs - 1)][0:1] - mean_row
    mean, inverse = as_column(mean_row), as_column(inverse_row)
    normed[:, :FINE] = (low[...].astype(f32) + as_column(below)) * inverse
    normed[:, FINE : 3 * FINE] = (pre[...] - mean) * inverse
    normed[:, 3 * FINE :] = (high[...].astype(f32) + as_column(above)) * inverse
    own = normed[pl.ds(pl.multiple_of(share * 8, 8), 8), FINE : 3 * FINE]
    decoded[...] = activate(own).astype(bf16)

    def prepare(block, carry):
        at = pl.ds(pl.multiple_of(block * 16, 16), 16)
        slope[at, :] = read_planes(packed, block, SLAB) * activate_slope(normed[at, :])
        return carry

    lax.fori_loop(0, 8, prepare, 0)
    inner = slope[:, FINE : 3 * FINE]
    one = as_row(jnp.sum(inner, axis=1, keepdims=True))
    two = as_row(jnp.sum(inner * normed[:, FINE : 3 * FINE], axis=1, keepdims=True))
    row = lax.broadcasted_iota(jnp.int32, (8, 128), 0)
    sums[...] = jnp.broadcast_to(jnp.where(row < 4, one, two)[None], sums.shape)


def total_means(sums):
    totals = jnp.sum(sums[...], axis=0) / (sums.shape[0] * SLAB)
    return as_column(totals[0:1]), as_column(totals[7:8])


def second_back_kernel(
    place, normed, slope, inverse_row, sums_in, packed, weights,
    low, high, slope_one, sums, weight_grad, unfolded, matrix, grads, columns, own_cols,
):
    slab, share = place[0], place[1]
    mask = edge_mask(slab, sums.shape[0])
    mean_grad, mean_cross = total_means(sums_in)
    columns[0] = jnp.broadcast_to(mean_grad, (C_OUT, 128))
    columns[1] = jnp.broadcast_to(mean_cross, (C_OUT, 128))
    columns[2] = jnp.broadcast_to(as_column(inverse_row[0:1]), (C_OUT, 128))

    def prepare(block, carry):
        at = pl.ds(pl.multiple_of(block * 16, 16), 16)
        grad = columns[2, at, :1] * (slope[at, :] - columns[0, at, :1] - normed[at, :] * columns[1, at, :1])
        grad = grad.astype(bf16).astype(f32) * mask
        grads[at, :] = grad[:, FINE : 3 * FINE].astype(bf16)
        unfold_block(grad, unfolded, block, -1)
        return carry

    lax.fori_loop(0, 8, prepare, 0)
    for tap in range(27):
        matrix[:, tap * 128 : tap * 128 + 128] = tap_matrix(weights, tap, 0).astype(bf16)
    total = jnp.zeros((C_OUT, SLAB), f32)
    for k_z in range(3):
        total = total + jnp.dot(
            matrix[:, k_z * 1152 : k_z * 1152 + 1152],
            unfolded[:, (2 - k_z) * FINE : (2 - k_z) * FINE + SLAB],
            preferred_element_type=f32,
        )
    low[...] = total[:, :FINE].astype(bf16)
    high[...] = total[:, FINE:].astype(bf16)
    both = packed[:, :, :SLAB].astype(f32)
    first_normed = jnp.concatenate(
        [both[:, :8, FINE:].reshape(C_OUT, FINE), both[:, 8:, :FINE].reshape(C_OUT, FINE)], axis=1
    )
    inner = total * activate_slope(first_normed)
    slope_one[...] = inner
    one = as_row(jnp.sum(inner, axis=1, keepdims=True))
    two = as_row(jnp.sum(inner * first_normed, axis=1, keepdims=True))
    row = lax.broadcasted_iota(jnp.int32, (8, 128), 0)
    sums[...] = jnp.broadcast_to(jnp.where(row < 4, one, two)[None], sums.shape)
    own = packed[share].astype(f32)
    own = jnp.concatenate([own[:8, :SLAB], own[8:, :SLAB]], axis=1)
    own = activate(own).astype(bf16).astype(f32) * mask
    for tap in range(9):
        moved = fine_shift(own, tap // 3 - 1, tap % 3 - 1)
        for k_z in range(3):
            at = (k_z * 9 + tap) * 8
            own_cols[at : at + 8, :] = moved[:, k_z * FINE : k_z * FINE + SLAB]
    weight_grad[...] = lax.dot_general(
        own_cols[...].astype(bf16), grads[...], (((1,), (1,)), ((), ())), preferred_element_type=f32
    )


def first_back_kernel(
    place, slope, low, high, sums_in, packed, weights, first_skip, up_weight, coarse, joined, second_grad,
    skip_grad, coarse_own, coarse_next, weight_grads,
    unfolded, matrix, grads, columns, own_cols, spread, up_matrix,
):
    slab = place[0]
    mask = edge_mask(slab, sums_in.shape[0])
    mean_grad, mean_cross = total_means(sums_in)
    columns[0] = jnp.broadcast_to(mean_grad, (C_OUT, 128))
    columns[1] = jnp.broadcast_to(mean_cross, (C_OUT, 128))
    wide = packed[:, :, 2 * SLAB :].astype(f32)
    columns[2] = (wide[:, :8] + wide[:, 8:]).reshape(C_OUT, 128)

    def prepare(block, carry):
        at = pl.ds(pl.multiple_of(block * 16, 16), 16)
        normed = read_planes(packed, block, 0)
        bottom = low[at, :].astype(f32) * activate_slope(normed[:, :FINE])
        top = high[at, :].astype(f32) * activate_slope(normed[:, 3 * FINE :])
        inner = jnp.concatenate([bottom, slope[at, :], top], axis=1)
        grad = columns[2, at, :1] * (inner - columns[0, at, :1] - normed * columns[1, at, :1])
        grad = grad.astype(bf16).astype(f32) * mask
        grads[at, :] = grad[:, FINE : 3 * FINE].astype(bf16)
        unfold_block(grad, unfolded, block, -1)
        return carry

    lax.fori_loop(0, 8, prepare, 0)
    for tap in range(27):
        at = slice(tap * 128, tap * 128 + 128)
        skip_part = jnp.concatenate([first_skip[tap].astype(f32), jnp.zeros((8, 128), f32)], axis=0)
        matrix[0:128, at] = tap_matrix(weights, tap, 1).astype(bf16)
        matrix[128:144, at] = skip_part.astype(bf16)
    total = jnp.zeros((144, SLAB), f32)
    for k_z in range(3):
        total = total + jnp.dot(
            matrix[:, k_z * 1152 : k_z * 1152 + 1152],
            unfolded[:, (2 - k_z) * FINE : (2 - k_z) * FINE + SLAB],
            preferred_element_type=f32,
        )
    skip_grad[...] = total[128:136].astype(bf16)
    own = joined[...].astype(f32)
    for tap in range(9):
        moved = fine_shift(own, tap // 3 - 1, tap % 3 - 1).astype(bf16)
        for k_z in range(3):
            at = (k_z * 9 + tap) * 16
            own_cols[at : at + 16, :] = moved[:, k_z * FINE : k_z * FINE + SLAB]
    d_up = jnp.concatenate([total[:128, :FINE], total[:128, FINE:]], axis=0).astype(bf16)
    parted = jnp.dot(d_up, interleave_matrix(True), preferred_element_type=f32)
    for y_par in (0, 1):
        for x_par in (0, 1):
            at = (y_par * 2 + x_par) * COARSE
            source = jnp.concatenate(
                [parted[:128, at : at + COARSE], parted[128:, at : at + COARSE]], axis=1
            )
            for k_y, y_off in PARITY[y_par]:
                for k_x, x_off in PARITY[x_par]:
                    tap = k_y * 3 + k_x
                    spread[tap * 128 : tap * 128 + 128, :] = coarse_shift(
                        source, -y_off, -x_off
                    ).astype(bf16)
    for tap in range(27):
        at = (tap // 9) * 1152 + (tap % 9) * 128
        up_matrix[:, at : at + 128] = up_weight[tap]
    low_plane, high_plane = spread[:, :COARSE], spread[:, COARSE:]
    coarse_own[...] = jnp.dot(
        up_matrix[:, 1152:2304], low_plane, preferred_element_type=f32
    ) + jnp.dot(up_matrix[:, 2304:], high_plane, preferred_element_type=f32)
    coarse_next[...] = jnp.dot(up_matrix[:, :1152], high_plane, preferred_element_type=f32)
    last = (((1,), (1,)), ((), ()))
    here, following = coarse[0], coarse[1]
    for k_z, source, plane in ((0, following, high_plane), (1, here, low_plane), (2, here, high_plane)):
        product = lax.dot_general(source, plane, last, preferred_element_type=f32)
        for tap in range(9):
            at = (k_z * 9 + tap) * 16
            weight_grads[at : at + 16, :] = product[:, tap * 128 : tap * 128 + 128].astype(bf16)
    weight_grads[432:864, :] = lax.dot_general(
        own_cols[...], grads[...], last, preferred_element_type=f32
    ).astype(bf16)
    rest = jnp.concatenate([second_grad[...], jnp.zeros((GRAD_ROWS - 1080, 128), f32)], axis=0)
    weight_grads[864:, :] = rest.astype(bf16)


def grad_sum_kernel(place, parts, spread):
    total = jnp.sum(parts[...].astype(f32), axis=0) * (1.0 / math.sqrt(SLAB))
    spread[...] = jnp.broadcast_to(total.astype(bf16)[None], spread.shape)


def grad_split_kernel(place, gathered, up, first_up, first_skip, second):
    values = gathered[...].reshape(GRAD_ROWS, 128).astype(f32)
    up[...] = values[:432].reshape(27, 16, 128)
    first = values[432:864].reshape(27, 16, 128)
    first_up[...] = first[:, :8]
    first_skip[...] = first[:, 8:]
    second[...] = values[864:1080].reshape(27, 8, 128)


def local(coarse, encoder_skip, up_weight, first_up, first_skip, second_weight, cotangent):
    slabs, shares = lax.axis_size("gz"), lax.axis_size("ch")
    place = jnp.stack([lax.axis_index("gz"), lax.axis_index("ch")]).astype(jnp.int32)
    upward = [(i, i + 1) for i in range(slabs - 1)]
    downward = [(i + 1, i) for i in range(slabs - 1)]

    def from_below(block):
        return lax.ppermute(block, "gz", upward)

    def from_above(block):
        return lax.ppermute(block, "gz", downward)

    def swap(block, axis):
        return lax.all_to_all(block, axis, 0, 0, tiled=True)

    def io_major(weight):
        return jnp.transpose(weight, (0, 2, 1))

    up_own, up_first = io_major(up_weight), io_major(first_up)
    skip_first, second_own = io_major(first_skip), io_major(second_weight)
    kernels = lax.all_gather(jnp.concatenate([second_own, up_first], axis=1), "ch", axis=0)

    here = coarse.reshape(16, COARSE)
    before, after = from_below(here), from_above(here)
    skip_low, skip_high = from_below(encoder_skip[:, 1]), from_above(encoder_skip[:, 0])
    cot_low, cot_high = from_below(cotangent[:, 1]), from_above(cotangent[:, 0])
    pieces = jnp.transpose(up_weight.reshape(27, 16, 8, 16), (1, 3, 0, 2)).reshape(16, 16, 216)
    pieces = jnp.pad(pieces, ((0, 0), (0, 0), (0, 40)))
    planes = jnp.concatenate([before, here, after], axis=1)
    planes = jnp.broadcast_to(planes[None], (shares, 16, 3 * COARSE))
    mixed = swap(jnp.concatenate([pieces, planes], axis=2), "ch")

    partial, joined = call(
        up_kernel,
        [((16, 8, SLAB), f32), ((16, HALOED), bf16)],
        (place, mixed, encoder_skip.reshape(8, SLAB), skip_low, skip_high, up_first, skip_first),
        [pltpu.VMEM((144, HALOED), bf16)],
    )
    pre, low, high, stats = call(
        first_sum_kernel,
        [((8, SLAB), f32), ((8, FINE), f32), ((8, FINE), f32), ((slabs, 8, 128), f32)],
        (place, swap(partial, "ch")),
    )
    (packed,) = call(
        first_norm_kernel,
        [((16, 16, 2 * SLAB + 128), bf16)],
        (
            place, pre, from_below(high), from_above(low), swap(stats, "gz"),
            cotangent.reshape(8, SLAB), cot_low, cot_high,
        ),
    )
    packed = swap(packed, "ch")
    unfolded = pltpu.VMEM((1152, HALOED), bf16)
    second_pre, low, high, stats = call(
        second_conv_kernel,
        [((128, SLAB), f32), ((128, FINE), bf16), ((128, FINE), bf16), ((slabs, 8, 128), f32)],
        (place, packed, kernels),
        [unfolded, pltpu.VMEM((128, 3456), bf16)],
    )
    decoded, normed, slope, inverse, sums = call(
        second_norm_kernel,
        [
            ((8, SLAB), bf16), ((128, HALOED), f32), ((128, HALOED), f32), ((8, 128), f32),
            ((slabs, 8, 128), f32),
        ],
        (place, second_pre, from_below(high), from_above(low), swap(stats, "gz"), packed),
    )
    low, high, slope_one, sums, second_grad = call(
        second_back_kernel,
        [
            ((128, FINE), bf16), ((128, FINE), bf16), ((128, SLAB), f32), ((slabs, 8, 128), f32),
            ((216, 128), f32),
        ],
        (place, normed, slope, inverse, swap(sums, "gz"), packed, kernels),
        [
            unfolded, pltpu.VMEM((128, 3456), bf16), pltpu.VMEM((128, SLAB), bf16),
            pltpu.VMEM((3, 128, 128), f32), pltpu.VMEM((216, SLAB), f32),
        ],
    )
    skip_grad, coarse_own, coarse_next, weight_grads = call(
        first_back_kernel,
        [((8, SLAB), bf16), ((16, COARSE), f32), ((16, COARSE), f32), ((GRAD_ROWS, 128), bf16)],
        (
            place, slope_one, from_below(high), from_above(low), swap(sums, "gz"), packed, kernels,
            skip_first, up_own, jnp.stack([here, after]), joined, second_grad,
        ),
        [
            unfolded, pltpu.VMEM((144, 3456), bf16), pltpu.VMEM((128, SLAB), bf16),
            pltpu.VMEM((3, 128, 128), f32), pltpu.VMEM((432, SLAB), bf16),
            pltpu.VMEM((1152, 2 * COARSE), bf16), pltpu.VMEM((16, 3456), bf16),
        ],
    )
    coarse_grad = (coarse_own + from_below(coarse_next)).astype(bf16)
    rows = GRAD_ROWS // slabs
    (spread,) = call(
        grad_sum_kernel,
        [((slabs, rows, 128), bf16)],
        (place, swap(weight_grads.reshape(slabs, rows, 128), "gz")),
    )
    grads = call(
        grad_split_kernel,
        [((27, 16, 128), f32), ((27, 8, 128), f32), ((27, 8, 128), f32), ((27, 8, 128), f32)],
        (place, swap(spread, "gz")),
    )
    grads = [jnp.transpose(grad, (0, 2, 1)) for grad in grads]
    return (
        decoded.reshape(8, 2, FINE),
        coarse_grad.reshape(16, 1, COARSE),
        skip_grad.reshape(8, 2, FINE),
        *grads,
    )


def solution(mesh):
    volume, kernel = P("ch", "gz", None), P(None, None, "ch")
    return jax.shard_map(
        local,
        mesh=mesh,
        in_specs=(volume, volume, kernel, kernel, kernel, kernel, volume),
        out_specs=(volume, volume, volume, kernel, kernel, kernel, kernel),
        check_vma=False,
    )
```

time: 1140 us -> 269 us (0.24)
  the two profiles are of different devices: /device:TPU:10 before, /device:TPU:8 now
where the time goes in v1:
time: 269 us; the launch traced here: 268 us
  starting transfers between devices  100 us (37%)
  blocking collectives  51.8 us (19%)
  waiting for transfers between devices  50.9 us (19%)
  Pallas kernels  25.6 us (10%)
  local copies, waits for them, and re-layouts  21.1 us (8%)
  between operations  14.5 us (5%)
  other arithmetic  3.51 us (1%)
    all_to_all x7, starting transfers between devices, swap(): return lax.all_to_all(block, axis, 0, 0, tiled=True)  58 us
    all_to_all x2, blocking collectives, swap(): return lax.all_to_all(block, axis, 0, 0, tiled=True)  51.8 us
    all_to_all x7, waiting for transfers between devices, swap(): return lax.all_to_all(block, axis, 0, 0, tiled=True)  37 us
    pallas_call x9, Pallas kernels, call(): pl.pallas_call(kernel, out_shape=[jax.ShapeDtypeStruct(shape, dtype) for...  25.6 us
    ppermute x6, starting transfers between devices, from_above(): return lax.ppermute(block, 'gz', downward)  21.7 us
    ppermute x7, starting transfers between devices, from_below(): return lax.ppermute(block, 'gz', upward)  20.7 us
    unnamed x77, local copies, waits for them, and re-layouts  19.8 us
    ppermute x6, waiting for transfers between devices, from_above(): return lax.ppermute(block, 'gz', downward)  9.71 us
  transfers between devices with their start and end apart: 21, of which 14 were waited for; matrix products, arithmetic and copies ran while one was open for 3% of the time, Pallas kernels for 1%

profile of v1, /device:TPU:8, one launch (start us, length us, event | category | flops | bytes accessed | tf_op | source)
XLA Modules:
  0.0 267.8 jit_solution(1720205255123453976)
XLA Ops:
  7.2 7.7 %collective-permute-start.1 = (bf16[16,128]{1,0:T(8,128)(2,1)}, bf16[16,128]{1,0:T(8,128)(2,1)S(1)}, u32[]{:S(2)}, u32[]{:S(2)}) collective-permute-start(bf16[16,128]{1,0:T(8,128)(2,1)} %bitcast.57), channel_id=1, source_target_pairs={{16,0},{32,16},{48,32},{64,48},{80,64},{96,80},{112,96},{128,112},... | collective-permute-start | bytes 12296 | tf_op jit(solution)/shard_map/ppermute | solution.py:430
  14.9 1.9 collective-permute-start
  16.8 1.4 copy.30
  18.2 0.9 copy.31
  19.5 1.1 collective-permute-done
  20.7 0.8 fusion.1
  21.4 3.7 %all-to-all-start = ((bf16[16,16,640]{2,1,0:T(8,128)(2,1)}), bf16[16,16,640]{2,1,0:T(8,128)(2,1)S(1)}, u32[]{:S(2)}, u32[]{:S(2)}) async-start(bf16[16,16,640]{2,1,0:T(8,128)(2,1)} %fusion.1), calls=%async_computation | async-start | bytes 655360 | tf_op jit(solution)/shard_map/all_to_all | solution.py:433
  25.2 1.9 collective-permute-start.2
  27.1 3.9 %collective-permute-start.3 = (bf16[8,512]{1,0:T(8,128)(2,1)S(1)}, bf16[8,512]{1,0:T(8,128)(2,1)S(1)}, u32[]{:S(2)}, u32[]{:S(2)}) collective-permute-start(bf16[8,512]{1,0:T(8,128)(2,1)S(1)} %bitcast.63), channel_id=1, source_target_pairs={{16,0},{32,16},{48,32},{64,48},{80,64},{96,80},{112,96},{128,112},... | collective-permute-start | bytes 24584 | tf_op jit(solution)/shard_map/ppermute | solution.py:430
  31.1 1.6 collective-permute-done.3.skip_high
  32.8 1.1 all-to-all-done.mixed
  33.8 2.4 shard_map.126
  36.9 4.8 %all-to-all-start.1 = ((f32[16,8,1024]{2,1,0:T(8,128)}), f32[16,8,1024]{2,1,0:T(8,128)S(1)}, u32[]{:S(2)}, u32[]{:S(2)}) async-start(f32[16,8,1024]{2,1,0:T(8,128)} %get-tuple-element.35), calls=%async_computation.1 | async-start | bytes 1048576 | tf_op jit(solution)/shard_map/all_to_all | solution.py:433
  41.7 0.7 pad_maximum_fusion
  42.4 10.1 %all-to-all-done.1.parts = f32[16,8,1024]{2,1,0:T(8,128)S(1)} async-done(((f32[16,8,1024]{2,1,0:T(8,128)}), f32[16,8,1024]{2,1,0:T(8,128)S(1)}, u32[]{:S(2)}, u32[]{:S(2)}) %all-to-all-start.1) | async-done | bytes 524320 | tf_op jit(solution)/shard_map/all_to_all | solution.py:433
  52.5 1.4 shard_map.127
  53.9 20.7 %all-to-all-start.2 = ((f32[32,8,128]{2,1,0:T(8,128)}), f32[32,8,128]{2,1,0:T(8,128)S(1)}, u32[]{:S(2)}, u32[]{:S(2)}) async-start(f32[32,8,128]{2,1,0:T(8,128)} %get-tuple-element.39), calls=%async_computation.2 | async-start | bytes 262144 | tf_op jit(solution)/shard_map/all_to_all | solution.py:433
  74.7 3.4 %collective-permute-start.4 = (f32[8,512]{1,0:T(8,128)S(1)}, f32[8,512]{1,0:T(8,128)S(1)}, u32[]{:S(2)}, u32[]{:S(2)}) collective-permute-start(f32[8,512]{1,0:T(8,128)S(1)} %get-tuple-element.37), channel_id=1, source_target_pairs={{0,16},{16,32},{32,48},{48,64},{64,80},{80,96},{96,112},{112,128},... | collective-permute-start | bytes 49160 | tf_op jit(solution)/shard_map/ppermute | solution.py:427
  78.0 2.5 collective-permute-start.5
  80.6 3.4 %collective-permute-start.6 = (bf16[8,512]{1,0:T(8,128)(2,1)S(1)}, bf16[8,512]{1,0:T(8,128)(2,1)S(1)}, u32[]{:S(2)}, u32[]{:S(2)}) collective-permute-start(bf16[8,512]{1,0:T(8,128)(2,1)S(1)} %bitcast.64), channel_id=1, source_target_pairs={{0,16},{16,32},{32,48},{48,64},{64,80},{80,96},{96,112},{112,128},... | collective-permute-start | bytes 24584 | tf_op jit(solution)/shard_map/ppermute | solution.py:427
  84.0 2.5 collective-permute-start.7
  86.5 3.2 %collective-permute-done.7.cot_high = bf16[8,512]{1,0:T(8,128)(2,1)S(1)} collective-permute-done((bf16[8,512]{1,0:T(8,128)(2,1)S(1)}, bf16[8,512]{1,0:T(8,128)(2,1)S(1)}, u32[]{:S(2)}, u32[]{:S(2)}) %collective-permute-start.7) | collective-permute-done | bytes 8224 | tf_op jit(solution)/shard_map/ppermute | solution.py:430
  89.6 1.8 shard_map.128
  91.4 3.7 %all-to-all-start.3 = ((bf16[16,16,2176]{2,1,0:T(8,128)(2,1)}), bf16[16,16,2176]{2,1,0:T(8,128)(2,1)S(1)}, u32[]{:S(2)}, u32[]{:S(2)}) async-start(bf16[16,16,2176]{2,1,0:T(8,128)(2,1)} %shard_map.128), calls=%async_computation.3 | async-start | bytes 2228224 | tf_op jit(solution)/shard_map/all_to_all | solution.py:433
  95.2 17.3 %all-to-all-done.3.packed = bf16[16,16,2176]{2,1,0:T(8,128)(2,1)S(1)} async-done(((bf16[16,16,2176]{2,1,0:T(8,128)(2,1)}), bf16[16,16,2176]{2,1,0:T(8,128)(2,1)S(1)}, u32[]{:S(2)}, u32[]{:S(2)}) %all-to-all-start.3) | async-done | bytes 1114144 | tf_op jit(solution)/shard_map/all_to_all | solution.py:433
  112.5 1.5 copy-done
  113.9 4.5 %shard_map.129 = (f32[128,1024]{1,0:T(8,128)S(1)}, bf16[128,512]{1,0:T(8,128)(2,1)S(1)}, bf16[128,512]{1,0:T(8,128)(2,1)S(1)}, f32[32,8,128]{2,1,0:T(8,128)S(1)}) custom-call(s32[2]{0:T(128)S(1)} %pad_add_fusion.place, bf16[16,16,2176]{2,1,0:T(8,128)(2,1)S(1)} %all-to-all-done.3.packed, bf16[16,27,16,128]{3,2,1,0:T(8,128)(2,1)S(1)} %bitcast.39), custom_call_target="tpu_custom_call" | custom-call | tf_op jit(solution)/shard_map/pallas_call | solution.py:84
  119.1 0.7 copy-done.26
  120.4 16.9 %all-to-all-start.4 = ((f32[32,8,128]{2,1,0:T(8,128)}), f32[32,8,128]{2,1,0:T(8,128)S(1)}, u32[]{:S(2)}, u32[]{:S(2)}) async-start(f32[32,8,128]{2,1,0:T(8,128)} %copy-done.15), calls=%async_computation.4 | async-start | bytes 262144 | tf_op jit(solution)/shard_map/all_to_all | solution.py:433
  137.4 3.4 %collective-permute-start.8 = (bf16[128,512]{1,0:T(8,128)(2,1)}, bf16[128,512]{1,0:T(8,128)(2,1)S(1)}, u32[]{:S(2)}, u32[]{:S(2)}) collective-permute-start(bf16[128,512]{1,0:T(8,128)(2,1)} %copy-done.27), channel_id=1, source_target_pairs={{0,16},{16,32},{32,48},{48,64},{64,80},{80,96},{96,112},{112,128},... | collective-permute-start | bytes 393224 | tf_op jit(solution)/shard_map/ppermute | solution.py:427
  140.7 2.5 collective-permute-start.9
  143.2 1.6 collective-permute-done.8.low
  145.5 2.3 collective-permute-done.9.high
  147.8 0.7 copy-done.12
  148.5 1.0 all-to-all-done.4.stats
  149.5 0.9 copy-done.11
  150.4 0.9 copy-done.13
  151.3 1.5 shard_map.130
  152.8 25.1 %all_to_all.45.sums_in = f32[32,8,128]{2,1,0:T(8,128)S(1)} all-to-all(f32[32,8,128]{2,1,0:T(8,128)S(1)} %get-tuple-element.48), channel_id=1, replica_groups=mesh['gz'=32,'ch'=16] {'gz'}, dimensions={0} | all-to-all | bytes 262144 | tf_op jit(solution)/shard_map/all_to_all | solution.py:433
  177.9 5.2 %shard_map.131 = (bf16[128,512]{1,0:T(8,128)(2,1)S(1)}, bf16[128,512]{1,0:T(8,128)(2,1)S(1)}, f32[128,1024]{1,0:T(8,128)S(1)}, f32[32,8,128]{2,1,0:T(8,128)S(1)}, f32[216,128]{1,0:T(8,128)S(1)}) custom-call(s32[2]{0:T(128)S(1)} %pad_add_fusion.place, f32[128,2048]{1,0:T(8,128)S(1)} %get-tuple-element.45.normed, f32[128,2048]{1,0:T(8,128)S(1)} %get-tuple-element.46.slope, ...), custom_call_target="tpu_custom_call" | custom-call | tf_op jit(solution)/shard_map/pallas_call | solution.py:84
  184.4 0.7 copy-done.24
  185.7 4.4 %all-to-all-start.6 = ((f32[32,8,128]{2,1,0:T(8,128)}), f32[32,8,128]{2,1,0:T(8,128)S(1)}, u32[]{:S(2)}, u32[]{:S(2)}) async-start(f32[32,8,128]{2,1,0:T(8,128)} %copy-done.14), calls=%async_computation.6 | async-start | bytes 262144 | tf_op jit(solution)/shard_map/all_to_all | solution.py:433
  190.1 3.4 %collective-permute-start.10 = (bf16[128,512]{1,0:T(8,128)(2,1)}, bf16[128,512]{1,0:T(8,128)(2,1)S(1)}, u32[]{:S(2)}, u32[]{:S(2)}) collective-permute-start(bf16[128,512]{1,0:T(8,128)(2,1)} %copy-done.25), channel_id=1, source_target_pairs={{0,16},{16,32},{32,48},{48,64},{64,80},{80,96},{96,112},{112,128},... | collective-permute-start | bytes 393224 | tf_op jit(solution)/shard_map/ppermute | solution.py:427
  193.5 2.6 collective-permute-start.11
  196.1 0.7 pad_maximum_fusion.2.coarse
  197.9 2.6 collective-permute-done.11.high
  200.5 0.7 copy-done.8
  201.2 0.9 all-to-all-done.6.sums_in
  202.1 0.9 copy-done.2
  203.0 0.8 copy-done.4
  203.8 0.9 copy-done.7
  204.7 0.9 copy-done.9
  205.6 0.9 copy-done.17
  206.5 0.8 copy-done.19
  207.3 6.2 %shard_map.132 = (bf16[8,1024]{1,0:T(8,128)(2,1)S(1)}, f32[16,128]{1,0:T(8,128)S(1)}, f32[16,128]{1,0:T(8,128)S(1)}, bf16[1280,128]{1,0:T(8,128)(2,1)S(1)}) custom-call(s32[2]{0:T(128)S(1)} %pad_add_fusion.place, f32[128,1024]{1,0:T(8,128)S(1)} %get-tuple-element.49.slope, bf16[128,512]{1,0:T(8,128)(2,1)S(1)} %copy-done.7, bf16[128,512]{1,0:T(8,128)(2,1)S(1)} %copy-done.9, ...), custom_call_target="tpu_custom_call" | custom-call | tf_op jit(solution)/shard_map/pallas_call | solution.py:84
  213.6 26.7 %all_to_all.46.parts = bf16[32,40,128]{2,1,0:T(8,128)(2,1)S(1)} all-to-all(bf16[32,40,128]{2,1,0:T(8,128)(2,1)S(1)} %bitcast.43), channel_id=1, replica_groups=mesh['gz'=32,'ch'=16] {'gz'}, dimensions={0} | all-to-all | bytes 655360 | tf_op jit(solution)/shard_map/all_to_all | solution.py:433
  240.2 1.4 shard_map.133
  241.6 3.9 %all-to-all-start.8 = ((bf16[32,40,128]{2,1,0:T(8,128)(2,1)}), bf16[32,40,128]{2,1,0:T(8,128)(2,1)S(1)}, u32[]{:S(2)}, u32[]{:S(2)}) async-start(bf16[32,40,128]{2,1,0:T(8,128)(2,1)} %shard_map.133), calls=%async_computation.8 | async-start | bytes 655360 | tf_op jit(solution)/shard_map/all_to_all | solution.py:433
  245.5 3.4 %collective-permute-start.12 = (f32[16,128]{1,0:T(8,128)}, f32[16,128]{1,0:T(8,128)S(1)}, u32[]{:S(2)}, u32[]{:S(2)}) collective-permute-start(f32[16,128]{1,0:T(8,128)} %copy-done.28), channel_id=1, source_target_pairs={{0,16},{16,32},{32,48},{48,64},{64,80},{80,96},{96,112},{112,128},... | collective-permute-start | bytes 24584 | tf_op jit(solution)/shard_map/ppermute | solution.py:427
  249.5 1.3 copy.38
  250.8 0.9 collective-permute-done.12
  251.8 1.3 fusion.2
  253.0 6.6 %all-to-all-done.8.gathered = bf16[32,40,128]{2,1,0:T(8,128)(2,1)S(1)} async-done(((bf16[32,40,128]{2,1,0:T(8,128)(2,1)}), bf16[32,40,128]{2,1,0:T(8,128)(2,1)S(1)}, u32[]{:S(2)}, u32[]{:S(2)}) %all-to-all-start.8) | async-done | bytes 327712 | tf_op jit(solution)/shard_map/all_to_all | solution.py:433
  259.7 1.3 shard_map.134
  (78 shorter events, 6.9 us)
Async XLA Ops:
  7.2 12.3 %collective-permute-start.1 = (bf16[16,128]{1,0:T(8,128)(2,1)}, bf16[16,128]{1,0:T(8,128)(2,1)S(1)}, u32[]{:S(2)}, u32[]{:S(2)}) collective-permute-start(bf16[16,128]{1,0:T(8,128)(2,1)} %bitcast.57), channel_id=1, source_target_pairs={{16,0},{32,16},{48,32},{64,48},{80,64},{96,80},{112,96},{128,112},... | collective-permute-start | bytes 12296 | tf_op jit(solution)/shard_map/ppermute | solution.py:430
  14.9 5.7 %collective-permute-start = (bf16[16,128]{1,0:T(8,128)(2,1)}, bf16[16,128]{1,0:T(8,128)(2,1)S(1)}, u32[]{:S(2)}, u32[]{:S(2)}) collective-permute-start(bf16[16,128]{1,0:T(8,128)(2,1)} %bitcast.58), channel_id=1, source_target_pairs={{0,16},{16,32},{32,48},{48,64},{64,80},{80,96},{96,112},{112,128},... | collective-permute-start | bytes 12296 | tf_op jit(solution)/shard_map/ppermute | solution.py:427
  18.2 2.4 copy-start.32
  19.1 6.0 %copy-start.29 = (bf16[8,2,512]{2,1,0:T(2,128)(2,1)S(1)}, bf16[8,2,512]{2,1,0:T(2,128)(2,1)}, u32[]{:S(2)}) copy-start(bf16[8,2,512]{2,1,0:T(2,128)(2,1)} %param.8) | copy-start | bytes 49156
  19.4 14.4 %copy-start.3 = (bf16[27,128,8]{1,2,0:T(8,128)(2,1)S(1)}, bf16[27,128,8]{1,2,0:T(8,128)(2,1)}, u32[]{:S(2)}) copy-start(bf16[27,128,8]{1,2,0:T(8,128)(2,1)} %param.11) | copy-start | bytes 165892
  19.4 14.4 %copy-start.5 = (bf16[27,128,8]{1,2,0:T(8,128)(2,1)S(1)}, bf16[27,128,8]{1,2,0:T(8,128)(2,1)}, u32[]{:S(2)}) copy-start(bf16[27,128,8]{1,2,0:T(8,128)(2,1)} %param.10) | copy-start | bytes 165892
  19.5 17.4 %copy-start.33 = (bf16[16,128]{1,0:T(8,128)(2,1)}, bf16[16,128]{1,0:T(8,128)(2,1)S(1)}, u32[]{:S(2)}) copy-start(bf16[16,128]{1,0:T(8,128)(2,1)S(1)} %collective-permute-done.1) | copy-start | bytes 12292
  21.4 20.3 %copy-start.31 = (bf16[27,128,8]{1,2,0:T(8,128)(2,1)S(1)}, bf16[27,128,8]{1,2,0:T(8,128)(2,1)}, u32[]{:S(2)}) copy-start(bf16[27,128,8]{1,2,0:T(8,128)(2,1)} %param.12) | copy-start | bytes 165892
  21.4 12.4 %all-to-all-start = ((bf16[16,16,640]{2,1,0:T(8,128)(2,1)}), bf16[16,16,640]{2,1,0:T(8,128)(2,1)S(1)}, u32[]{:S(2)}, u32[]{:S(2)}) async-start(bf16[16,16,640]{2,1,0:T(8,128)(2,1)} %fusion.1), calls=%async_computation | async-start | bytes 655360 | tf_op jit(solution)/shard_map/all_to_all | solution.py:433
  25.2 6.0 %collective-permute-start.2 = (bf16[8,512]{1,0:T(8,128)(2,1)S(1)}, bf16[8,512]{1,0:T(8,128)(2,1)S(1)}, u32[]{:S(2)}, u32[]{:S(2)}) collective-permute-start(bf16[8,512]{1,0:T(8,128)(2,1)S(1)} %bitcast.62), channel_id=1, source_target_pairs={{0,16},{16,32},{32,48},{48,64},{64,80},{80,96},{96,112},{112,128},... | collective-permute-start | bytes 24584 | tf_op jit(solution)/shard_map/ppermute | solution.py:427
  27.1 5.6 %collective-permute-start.3 = (bf16[8,512]{1,0:T(8,128)(2,1)S(1)}, bf16[8,512]{1,0:T(8,128)(2,1)S(1)}, u32[]{:S(2)}, u32[]{:S(2)}) collective-permute-start(bf16[8,512]{1,0:T(8,128)(2,1)S(1)} %bitcast.63), channel_id=1, source_target_pairs={{16,0},{32,16},{48,32},{64,48},{80,64},{96,80},{112,96},{128,112},... | collective-permute-start | bytes 24584 | tf_op jit(solution)/shard_map/ppermute | solution.py:430
  36.2 0.6 copy-start.18
  36.9 43.6 %copy-start.30 = (bf16[8,2,512]{2,1,0:T(2,128)(2,1)S(1)}, bf16[8,2,512]{2,1,0:T(2,128)(2,1)}, u32[]{:S(2)}) copy-start(bf16[8,2,512]{2,1,0:T(2,128)(2,1)} %param.13) | copy-start | bytes 49156
  36.9 15.6 %all-to-all-start.1 = ((f32[16,8,1024]{2,1,0:T(8,128)}), f32[16,8,1024]{2,1,0:T(8,128)S(1)}, u32[]{:S(2)}, u32[]{:S(2)}) async-start(f32[16,8,1024]{2,1,0:T(8,128)} %get-tuple-element.35), calls=%async_computation.1 | async-start | bytes 1048576 | tf_op jit(solution)/shard_map/all_to_all | solution.py:433
  41.7 53.5 %all-gather.3.cloned.1.call-start = ((), (), s32[]{:S(2)}) async-start(), calls=%async_computation.9 | async-start | bytes 1880064 | tf_op jit(solution)/shard_map/all_gather | solution.py:440
  53.9 35.7 %all-to-all-start.2 = ((f32[32,8,128]{2,1,0:T(8,128)}), f32[32,8,128]{2,1,0:T(8,128)S(1)}, u32[]{:S(2)}, u32[]{:S(2)}) async-start(f32[32,8,128]{2,1,0:T(8,128)} %get-tuple-element.39), calls=%async_computation.2 | async-start | bytes 262144 | tf_op jit(solution)/shard_map/all_to_all | solution.py:433
  74.7 15.0 %collective-permute-start.4 = (f32[8,512]{1,0:T(8,128)S(1)}, f32[8,512]{1,0:T(8,128)S(1)}, u32[]{:S(2)}, u32[]{:S(2)}) collective-permute-start(f32[8,512]{1,0:T(8,128)S(1)} %get-tuple-element.37), channel_id=1, source_target_pairs={{0,16},{16,32},{32,48},{48,64},{64,80},{80,96},{96,112},{112,128},... | collective-permute-start | bytes 49160 | tf_op jit(solution)/shard_map/ppermute | solution.py:427
  78.0 11.6 %collective-permute-start.5 = (f32[8,512]{1,0:T(8,128)S(1)}, f32[8,512]{1,0:T(8,128)S(1)}, u32[]{:S(2)}, u32[]{:S(2)}) collective-permute-start(f32[8,512]{1,0:T(8,128)S(1)} %get-tuple-element.38), channel_id=1, source_target_pairs={{16,0},{32,16},{48,32},{64,48},{80,64},{96,80},{112,96},{128,112},... | collective-permute-start | bytes 49160 | tf_op jit(solution)/shard_map/ppermute | solution.py:430
  80.6 5.9 %collective-permute-start.6 = (bf16[8,512]{1,0:T(8,128)(2,1)S(1)}, bf16[8,512]{1,0:T(8,128)(2,1)S(1)}, u32[]{:S(2)}, u32[]{:S(2)}) collective-permute-start(bf16[8,512]{1,0:T(8,128)(2,1)S(1)} %bitcast.64), channel_id=1, source_target_pairs={{0,16},{16,32},{32,48},{48,64},{64,80},{80,96},{96,112},{112,128},... | collective-permute-start | bytes 24584 | tf_op jit(solution)/shard_map/ppermute | solution.py:427
  84.0 5.7 %collective-permute-start.7 = (bf16[8,512]{1,0:T(8,128)(2,1)S(1)}, bf16[8,512]{1,0:T(8,128)(2,1)S(1)}, u32[]{:S(2)}, u32[]{:S(2)}) collective-permute-start(bf16[8,512]{1,0:T(8,128)(2,1)S(1)} %bitcast.65), channel_id=1, source_target_pairs={{16,0},{32,16},{48,32},{64,48},{80,64},{96,80},{112,96},{128,112},... | collective-permute-start | bytes 24584 | tf_op jit(solution)/shard_map/ppermute | solution.py:430
  91.4 21.0 %all-to-all-start.3 = ((bf16[16,16,2176]{2,1,0:T(8,128)(2,1)}), bf16[16,16,2176]{2,1,0:T(8,128)(2,1)S(1)}, u32[]{:S(2)}, u32[]{:S(2)}) async-start(bf16[16,16,2176]{2,1,0:T(8,128)(2,1)} %shard_map.128), calls=%async_computation.3 | async-start | bytes 2228224 | tf_op jit(solution)/shard_map/all_to_all | solution.py:433
  112.5 1.5 copy-start
  118.5 0.7 copy-start.15
  119.1 0.7 copy-start.26
  119.8 0.7 copy-start.27
  120.4 29.0 %all-to-all-start.4 = ((f32[32,8,128]{2,1,0:T(8,128)}), f32[32,8,128]{2,1,0:T(8,128)S(1)}, u32[]{:S(2)}, u32[]{:S(2)}) async-start(f32[32,8,128]{2,1,0:T(8,128)} %copy-done.15), calls=%async_computation.4 | async-start | bytes 262144 | tf_op jit(solution)/shard_map/all_to_all | solution.py:433
  137.4 7.5 %collective-permute-start.8 = (bf16[128,512]{1,0:T(8,128)(2,1)}, bf16[128,512]{1,0:T(8,128)(2,1)S(1)}, u32[]{:S(2)}, u32[]{:S(2)}) collective-permute-start(bf16[128,512]{1,0:T(8,128)(2,1)} %copy-done.27), channel_id=1, source_target_pairs={{0,16},{16,32},{32,48},{48,64},{64,80},{80,96},{96,112},{112,128},... | collective-permute-start | bytes 393224 | tf_op jit(solution)/shard_map/ppermute | solution.py:427
  140.7 7.1 %collective-permute-start.9 = (bf16[128,512]{1,0:T(8,128)(2,1)}, bf16[128,512]{1,0:T(8,128)(2,1)S(1)}, u32[]{:S(2)}, u32[]{:S(2)}) collective-permute-start(bf16[128,512]{1,0:T(8,128)(2,1)} %copy-done.26), channel_id=1, source_target_pairs={{16,0},{32,16},{48,32},{64,48},{80,64},{96,80},{112,96},{128,112},... | collective-permute-start | bytes 393224 | tf_op jit(solution)/shard_map/ppermute | solution.py:430
  144.9 0.7 copy-start.10
  147.8 0.7 copy-start.12
  149.5 0.9 copy-start.11
  150.4 0.9 copy-start.13
  151.3 26.6 %copy-start.1 = (bf16[432,16,128]{2,1,0:T(8,128)(2,1)S(1)}, bf16[432,16,128]{2,1,0:T(8,128)(2,1)}, u32[]{:S(2)}) copy-start(bf16[432,16,128]{2,1,0:T(8,128)(2,1)} %all-gather.3.cloned.1.call-done) | copy-start | bytes 5308420
  152.7 25.1 %copy-start.20 = (bf16[8,1024]{1,0:T(8,128)(2,1)}, bf16[8,1024]{1,0:T(8,128)(2,1)S(1)}, u32[]{:S(2)}) copy-start(bf16[8,1024]{1,0:T(8,128)(2,1)S(1)} %get-tuple-element.44) | copy-start | bytes 49156
  183.1 0.7 copy-start.14
  183.7 0.6 copy-start.16
  184.4 0.7 copy-start.24
  185.1 0.7 copy-start.25
  185.7 16.4 %all-to-all-start.6 = ((f32[32,8,128]{2,1,0:T(8,128)}), f32[32,8,128]{2,1,0:T(8,128)S(1)}, u32[]{:S(2)}, u32[]{:S(2)}) async-start(f32[32,8,128]{2,1,0:T(8,128)} %copy-done.14), calls=%async_computation.6 | async-start | bytes 262144 | tf_op jit(solution)/shard_map/all_to_all | solution.py:433
  190.1 7.2 %collective-permute-start.10 = (bf16[128,512]{1,0:T(8,128)(2,1)}, bf16[128,512]{1,0:T(8,128)(2,1)S(1)}, u32[]{:S(2)}, u32[]{:S(2)}) collective-permute-start(bf16[128,512]{1,0:T(8,128)(2,1)} %copy-done.25), channel_id=1, source_target_pairs={{0,16},{16,32},{32,48},{48,64},{64,80},{80,96},{96,112},{112,128},... | collective-permute-start | bytes 393224 | tf_op jit(solution)/shard_map/ppermute | solution.py:427
  193.5 7.1 %collective-permute-start.11 = (bf16[128,512]{1,0:T(8,128)(2,1)}, bf16[128,512]{1,0:T(8,128)(2,1)S(1)}, u32[]{:S(2)}, u32[]{:S(2)}) collective-permute-start(bf16[128,512]{1,0:T(8,128)(2,1)} %copy-done.24), channel_id=1, source_target_pairs={{16,0},{32,16},{48,32},{64,48},{80,64},{96,80},{112,96},{128,112},... | collective-permute-start | bytes 393224 | tf_op jit(solution)/shard_map/ppermute | solution.py:430
  197.3 0.7 copy-start.6
  200.5 0.7 copy-start.8
  202.1 0.9 copy-start.2
  203.0 0.8 copy-start.4
  203.8 0.9 copy-start.7
  204.7 0.9 copy-start.9
  205.6 0.9 copy-start.17
  206.5 0.8 copy-start.19
  213.5 26.7 %copy-start.22 = (bf16[8,1024]{1,0:T(8,128)(2,1)}, bf16[8,1024]{1,0:T(8,128)(2,1)S(1)}, u32[]{:S(2)}) copy-start(bf16[8,1024]{1,0:T(8,128)(2,1)S(1)} %get-tuple-element.57) | copy-start | bytes 49156
  213.5 26.7 %copy-start.23 = (f32[16,128]{1,0:T(8,128)}, f32[16,128]{1,0:T(8,128)S(1)}, u32[]{:S(2)}) copy-start(f32[16,128]{1,0:T(8,128)S(1)} %get-tuple-element.55) | copy-start | bytes 24580
  213.5 26.7 %copy-start.28 = (f32[16,128]{1,0:T(8,128)}, f32[16,128]{1,0:T(8,128)S(1)}, u32[]{:S(2)}) copy-start(f32[16,128]{1,0:T(8,128)S(1)} %get-tuple-element.56) | copy-start | bytes 24580
  213.6 35.3 %copy-start.21 = (bf16[8,1024]{1,0:T(8,128)(2,1)S(1)}, bf16[8,1024]{1,0:T(8,128)(2,1)}, u32[]{:S(2)}) copy-start(bf16[8,1024]{1,0:T(8,128)(2,1)} %copy-done.20) | copy-start | bytes 49156
  241.6 18.0 %all-to-all-start.8 = ((bf16[32,40,128]{2,1,0:T(8,128)(2,1)}), bf16[32,40,128]{2,1,0:T(8,128)(2,1)S(1)}, u32[]{:S(2)}, u32[]{:S(2)}) async-start(bf16[32,40,128]{2,1,0:T(8,128)(2,1)} %shard_map.133), calls=%async_computation.8 | async-start | bytes 655360 | tf_op jit(solution)/shard_map/all_to_all | solution.py:433
  245.5 6.3 %collective-permute-start.12 = (f32[16,128]{1,0:T(8,128)}, f32[16,128]{1,0:T(8,128)S(1)}, u32[]{:S(2)}, u32[]{:S(2)}) collective-permute-start(f32[16,128]{1,0:T(8,128)} %copy-done.28), channel_id=1, source_target_pairs={{0,16},{16,32},{32,48},{48,64},{64,80},{80,96},{96,112},{112,128},... | collective-permute-start | bytes 24584 | tf_op jit(solution)/shard_map/ppermute | solution.py:427
Sparse Core Ops, SparseCore 0:
  45.2 49.5 all-gather.2

commit v2 on v1

--- a/solution.py
+++ b/solution.py
@@ -78,7 +78,7 @@
     return jnp.transpose(jnp.broadcast_to(row, (C_OUT, C_OUT)))[:, :1]
 
 
-def call(kernel, outs, args, scratch=(), megabytes=24):
+def call(kernel, outs, args, scratch=(), megabytes=8):
     specs = [pl.BlockSpec(memory_space=pltpu.SMEM)]
     specs += [pl.BlockSpec(memory_space=pltpu.VMEM)] * (len(args) - 1)
     return pl.pallas_call(
@@ -91,7 +91,38 @@
     )(*args)
 
 
-def up_kernel(place, mixed, own_skip, skip_low, skip_high, first_up, first_skip, partial, joined, unfolded):
+def halo_kernel(place, coarse, skip, cotangent, upward, downward, own_skip, own_cot):
+    cells = coarse[...].astype(f32)
+    cells = [cells[:8], cells[8:]]
+    skip_planes, cot_planes = skip[...].astype(f32), cotangent[...].astype(f32)
+    last = cells + [skip_planes[:, 1], cot_planes[:, 1]]
+    first = cells + [skip_planes[:, 0], cot_planes[:, 0]]
+    upward[...] = jnp.concatenate(last, axis=1).astype(bf16)
+    downward[...] = jnp.concatenate(first, axis=1).astype(bf16)
+    own_skip[...] = jnp.concatenate([skip_planes[:, 0], skip_planes[:, 1]], axis=1).astype(bf16)
+    own_cot[...] = jnp.concatenate([cot_planes[:, 0], cot_planes[:, 1]], axis=1).astype(bf16)
+
+
+def mix_kernel(place, pieces, coarse, low, high, own_cot, mixed, pair, cot_planes):
+    below, above = low[...].astype(f32), high[...].astype(f32)
+    here = coarse[...].astype(f32)
+    before = jnp.concatenate([below[:, :COARSE], below[:, COARSE : 2 * COARSE]], axis=0)
+    after = jnp.concatenate([above[:, :COARSE], above[:, COARSE : 2 * COARSE]], axis=0)
+    planes = jnp.concatenate([before, here, after], axis=1).astype(bf16)
+    mixed[:, :, :256] = jnp.zeros((16, 16, 256), bf16)
+    for target in range(16):
+        mixed[target, :, :216] = pieces[target]
+        mixed[target, :, 256:] = planes
+    pair[0] = coarse[...]
+    pair[1] = after.astype(bf16)
+    cot = own_cot[...].astype(f32)
+    lower = jnp.concatenate([below[:, 2 * COARSE + FINE :], cot[:, :FINE]], axis=1)
+    upper = jnp.concatenate([cot[:, FINE:], above[:, 2 * COARSE + FINE :]], axis=1)
+    cot_planes[0:16] = jnp.concatenate([lower, upper], axis=0).astype(bf16)
+    cot_planes[16:32] = jnp.zeros((16, SLAB), bf16)
+
+
+def up_kernel(place, mixed, own_skip, low, high, first_up, first_skip, partial, joined, unfolded):
     slab = place[0]
     packed = mixed[...]
     weights = packed[:, :, :256].reshape(256, 256)
@@ -121,8 +152,9 @@
     upsampled = jnp.concatenate(
         [fine[0:8] * first_inside, fine[8:16], fine[16:24], fine[24:32]], axis=1
     )
+    skip_at = slice(2 * COARSE, 2 * COARSE + FINE)
     skip = jnp.concatenate(
-        [skip_low[...].astype(f32), own_skip[...].astype(f32), skip_high[...].astype(f32)], axis=1
+        [low[:, skip_at].astype(f32), own_skip[...].astype(f32), high[:, skip_at].astype(f32)], axis=1
     )
     features = jnp.concatenate([upsampled, skip], axis=0)
     joined[...] = features.astype(bf16)
@@ -145,38 +177,64 @@
     partial[...] = total.reshape(16, 8, SLAB)
 
 
-def first_sum_kernel(place, parts, pre, low, high, stats):
+def in_parts(values):
+    high = values.astype(bf16).astype(f32)
+    middle = (values - high).astype(bf16).astype(f32)
+    rest = values - high - middle
+    lane = lax.broadcasted_iota(jnp.int32, (values.shape[0], 128), 1)
+    return jnp.where(
+        lane == 0, high, jnp.where(lane == 1, middle, jnp.where(lane == 2, rest, 0.0))
+    )
+
+
+def first_sum_kernel(place, parts, pre, stats):
     total = jnp.sum(parts[...], axis=0)
     pre[...] = total
-    low[...] = total[:, :FINE]
-    high[...] = total[:, FINE:]
     mean = jnp.sum(total, axis=1, keepdims=True) / SLAB
     deviation = total - mean
     square = jnp.sum(deviation * deviation, axis=1, keepdims=True)
-    lane = lax.broadcasted_iota(jnp.int32, (8, 128), 1)
-    tile = jnp.where(lane < 64, mean, square)
-    stats[...] = jnp.broadcast_to(tile[None], stats.shape)
-
-
-def first_norm_kernel(place, pre, low, high, stats, cotangent, cot_low, cot_high, packed):
-    slabs = stats.shape[0]
-    gathered = stats[...]
-    means = gathered[:, :, :1]
+    tail = in_parts(jnp.concatenate([mean, square], axis=0))
+    half = FINE // 2
+    first = jnp.concatenate([deviation[:, :half], deviation[:, half:FINE]], axis=0)
+    last = jnp.concatenate([deviation[:, FINE : FINE + half], deviation[:, FINE + half :]], axis=0)
+    first = jnp.concatenate([first, tail], axis=1).astype(bf16)
+    last = jnp.concatenate([last, tail], axis=1).astype(bf16)
+    for target in range(stats.shape[0]):
+        above = target > place[0]
+
+        @pl.when(above)
+        def _():
+            stats[target] = last
+
+        @pl.when(jnp.logical_not(above))
+        def _():
+            stats[target] = first
+
+
+def first_norm_kernel(place, pre, stats, packed):
+    slab, slabs = place[0], stats.shape[0]
+    half = FINE // 2
+    tails = jnp.sum(stats[:, :, half:].astype(f32), axis=2, keepdims=True)
+    means = tails[:, :8]
     mean = jnp.sum(means, axis=0) / slabs
     apart = means - mean[None]
-    square = jnp.sum(gathered[:, :, 127:] + SLAB * apart * apart, axis=0)
+    square = jnp.sum(tails[:, 8:] + SLAB * apart * apart, axis=0)
     inverse = lax.rsqrt(square / (slabs * SLAB) + NORM_EPS)
-    lower = jnp.concatenate([low[...], pre[:, :FINE]], axis=1)
-    upper = jnp.concatenate([pre[:, FINE:], high[...]], axis=1)
-    cot = cotangent[...].astype(f32)
-    cot_lower = jnp.concatenate([cot_low[...].astype(f32), cot[:, :FINE]], axis=1)
-    cot_upper = jnp.concatenate([cot[:, FINE:], cot_high[...].astype(f32)], axis=1)
+
+    def neighbour(index):
+        block = stats[index].astype(f32)
+        centre = jnp.sum(block[:8, half:], axis=1, keepdims=True)
+        return jnp.concatenate([block[:8, :half], block[8:, :half]], axis=1) + centre
+
+    low, high = neighbour(jnp.maximum(slab - 1, 0)), neighbour(jnp.minimum(slab + 1, slabs - 1))
+    lower = jnp.concatenate([low, pre[:, :FINE]], axis=1)
+    upper = jnp.concatenate([pre[:, FINE:], high], axis=1)
     wide = jnp.broadcast_to(inverse, (8, 128))
     main = wide.astype(bf16).astype(f32)
     block = jnp.concatenate(
         [
-            jnp.concatenate([(lower - mean) * inverse, cot_lower, main], axis=1),
-            jnp.concatenate([(upper - mean) * inverse, cot_upper, wide - main], axis=1),
+            jnp.concatenate([(lower - mean) * inverse, main], axis=1),
+            jnp.concatenate([(upper - mean) * inverse, wide - main], axis=1),
         ],
         axis=0,
     ).astype(bf16)
@@ -184,8 +242,8 @@
         packed[target] = block
 
 
-def read_planes(packed, block, offset):
-    pair = packed[pl.ds(2 * block, 2), :, offset : offset + SLAB].astype(f32)
+def read_planes(packed, block):
+    pair = packed[pl.ds(2 * block, 2), 0:16, :SLAB].astype(f32)
     return jnp.concatenate([pair[:, :8].reshape(16, SLAB), pair[:, 8:].reshape(16, SLAB)], axis=1)
 
 
@@ -204,7 +262,7 @@
     mask = edge_mask(place[0], stats.shape[0])
 
     def prepare(block, carry):
-        hidden = activate(read_planes(packed, block, 0)).astype(bf16).astype(f32) * mask
+        hidden = activate(read_planes(packed, block)).astype(bf16).astype(f32) * mask
         unfold_block(hidden, unfolded, block, 1)
         return carry
 
@@ -230,7 +288,7 @@
 
 
 def second_norm_kernel(
-    place, pre, low, high, stats, packed, decoded, normed, slope, inverse_out, sums
+    place, pre, low, high, stats, cotangent, decoded, normed, slope, inverse_out, sums
 ):
     slab, share = place[0], place[1]
     slabs = stats.shape[0]
@@ -252,7 +310,7 @@
 
     def prepare(block, carry):
         at = pl.ds(pl.multiple_of(block * 16, 16), 16)
-        slope[at, :] = read_planes(packed, block, SLAB) * activate_slope(normed[at, :])
+        slope[at, :] = read_planes(cotangent, block) * activate_slope(normed[at, :])
         return carry
 
     lax.fori_loop(0, 8, prepare, 0)
@@ -332,12 +390,12 @@
     mean_grad, mean_cross = total_means(sums_in)
     columns[0] = jnp.broadcast_to(mean_grad, (C_OUT, 128))
     columns[1] = jnp.broadcast_to(mean_cross, (C_OUT, 128))
-    wide = packed[:, :, 2 * SLAB :].astype(f32)
+    wide = packed[:, :, SLAB:].astype(f32)
     columns[2] = (wide[:, :8] + wide[:, 8:]).reshape(C_OUT, 128)
 
     def prepare(block, carry):
         at = pl.ds(pl.multiple_of(block * 16, 16), 16)
-        normed = read_planes(packed, block, 0)
+        normed = read_planes(packed, block)
         bottom = low[at, :].astype(f32) * activate_slope(normed[:, :FINE])
         top = high[at, :].astype(f32) * activate_slope(normed[:, 3 * FINE :])
         inner = jnp.concatenate([bottom, slope[at, :], top], axis=1)
@@ -440,33 +498,34 @@
     kernels = lax.all_gather(jnp.concatenate([second_own, up_first], axis=1), "ch", axis=0)
 
     here = coarse.reshape(16, COARSE)
-    before, after = from_below(here), from_above(here)
-    skip_low, skip_high = from_below(encoder_skip[:, 1]), from_above(encoder_skip[:, 0])
-    cot_low, cot_high = from_below(cotangent[:, 1]), from_above(cotangent[:, 0])
+    halo = ((8, 2 * COARSE + 2 * FINE), bf16)
+    upper, lower, own_skip, own_cot = call(
+        halo_kernel,
+        [halo, halo, ((8, SLAB), bf16), ((8, SLAB), bf16)],
+        (place, here, encoder_skip, cotangent),
+    )
+    low, high = from_below(upper), from_above(lower)
     pieces = jnp.transpose(up_weight.reshape(27, 16, 8, 16), (1, 3, 0, 2)).reshape(16, 16, 216)
-    pieces = jnp.pad(pieces, ((0, 0), (0, 0), (0, 40)))
-    planes = jnp.concatenate([before, here, after], axis=1)
-    planes = jnp.broadcast_to(planes[None], (shares, 16, 3 * COARSE))
-    mixed = swap(jnp.concatenate([pieces, planes], axis=2), "ch")
+    mixed, pair, cot_planes = call(
+        mix_kernel,
+        [((16, 16, 640), bf16), ((2, 16, COARSE), bf16), ((32, SLAB), bf16)],
+        (place, pieces, here, low, high, own_cot),
+    )
+    cot_planes = lax.all_gather(cot_planes, "ch", axis=0)
 
     partial, joined = call(
         up_kernel,
         [((16, 8, SLAB), f32), ((16, HALOED), bf16)],
-        (place, mixed, encoder_skip.reshape(8, SLAB), skip_low, skip_high, up_first, skip_first),
+        (place, swap(mixed, "ch"), own_skip, low, high, up_first, skip_first),
         [pltpu.VMEM((144, HALOED), bf16)],
     )
-    pre, low, high, stats = call(
+    pre, stats = call(
         first_sum_kernel,
-        [((8, SLAB), f32), ((8, FINE), f32), ((8, FINE), f32), ((slabs, 8, 128), f32)],
+        [((8, SLAB), f32), ((slabs, 16, FINE // 2 + 128), bf16)],
         (place, swap(partial, "ch")),
     )
     (packed,) = call(
-        first_norm_kernel,
-        [((16, 16, 2 * SLAB + 128), bf16)],
-        (
-            place, pre, from_below(high), from_above(low), swap(stats, "gz"),
-            cotangent.reshape(8, SLAB), cot_low, cot_high,
-        ),
+        first_norm_kernel, [((16, 16, SLAB + 128), bf16)], (place, pre, swap(stats, "gz"))
     )
     packed = swap(packed, "ch")
     unfolded = pltpu.VMEM((1152, HALOED), bf16)
@@ -475,6 +534,7 @@
         [((128, SLAB), f32), ((128, FINE), bf16), ((128, FINE), bf16), ((slabs, 8, 128), f32)],
         (place, packed, kernels),
         [unfolded, pltpu.VMEM((128, 3456), bf16)],
+        16,
     )
     decoded, normed, slope, inverse, sums = call(
         second_norm_kernel,
@@ -482,7 +542,7 @@
             ((8, SLAB), bf16), ((128, HALOED), f32), ((128, HALOED), f32), ((8, 128), f32),
             ((slabs, 8, 128), f32),
         ],
-        (place, second_pre, from_below(high), from_above(low), swap(stats, "gz"), packed),
+        (place, second_pre, from_below(high), from_above(low), swap(stats, "gz"), cot_planes),
     )
     low, high, slope_one, sums, second_grad = call(
         second_back_kernel,
@@ -495,19 +555,21 @@
             unfolded, pltpu.VMEM((128, 3456), bf16), pltpu.VMEM((128, SLAB), bf16),
             pltpu.VMEM((3, 128, 128), f32), pltpu.VMEM((216, SLAB), f32),
         ],
+        16,
     )
     skip_grad, coarse_own, coarse_next, weight_grads = call(
         first_back_kernel,
         [((8, SLAB), bf16), ((16, COARSE), f32), ((16, COARSE), f32), ((GRAD_ROWS, 128), bf16)],
         (
             place, slope_one, from_below(high), from_above(low), swap(sums, "gz"), packed, kernels,
-            skip_first, up_own, jnp.stack([here, after]), joined, second_grad,
+            skip_first, up_own, pair, joined, second_grad,
         ),
         [
             unfolded, pltpu.VMEM((144, 3456), bf16), pltpu.VMEM((128, SLAB), bf16),
             pltpu.VMEM((3, 128, 128), f32), pltpu.VMEM((432, SLAB), bf16),
             pltpu.VMEM((1152, 2 * COARSE), bf16), pltpu.VMEM((16, 3456), bf16),
         ],
+        20,
     )
     coarse_grad = (coarse_own + from_below(coarse_next)).astype(bf16)
     rows = GRAD_ROWS // slabs

time: 269 us -> 246 us (0.914)
  starting transfers between devices: 100 us -> 55.8 us
  blocking collectives: 51.8 us -> 79.7 us
  local copies, waits for them, and re-layouts: 21.1 us -> 14.1 us
    all_to_all x2 -> x4, blocking collectives: 51.8 us -> 79.7 us  [swap(): return lax.all_to_all(block, axis, 0, 0, tiled=True)]
    all_to_all x7 -> x5, starting transfers between devices: 58 us -> 31.4 us  [swap(): return lax.all_to_all(block, axis, 0, 0, tiled=True)]
    ppermute x6 -> x3, starting transfers between devices: 21.7 us -> 10.7 us  [from_above(): return lax.ppermute(block, 'gz', downward)]
    ppermute x7 -> x4, starting transfers between devices: 20.7 us -> 13.6 us  [from_below(): return lax.ppermute(block, 'gz', upward)]
    unnamed x77 -> x53, local copies, waits for them, and re-layouts: 19.8 us -> 12.9 us
    ppermute x6 -> x3, waiting for transfers between devices: 9.71 us -> 6.01 us  [from_above(): return lax.ppermute(block, 'gz', downward)]
    pallas_call x9 -> x11, Pallas kernels: 25.6 us -> 28.1 us  [call(): pl.pallas_call(kernel, out_shape=[jax.ShapeDtypeStruct(shape, dtype) for...]
    all_to_all x7 -> x5, waiting for transfers between devices: 37 us -> 39.1 us  [swap(): return lax.all_to_all(block, axis, 0, 0, tiled=True)]
  transfers between devices with their start and end apart: 21 -> 14, of which waited for: 14 -> 10; matrix products, arithmetic and copies ran while one was open for 3% -> 2% of each run, Pallas kernels for 1% -> 5%
where the time goes in v2:
time: 246 us; the launch traced here: 245 us
  blocking collectives  79.7 us (32%)
  starting transfers between devices  55.8 us (23%)
  waiting for transfers between devices  49.8 us (20%)
  Pallas kernels  28.1 us (11%)
  between operations  14.3 us (6%)
  local copies, waits for them, and re-layouts  14.1 us (6%)
  other arithmetic  2.87 us (1%)
    all_to_all x4, blocking collectives, swap(): return lax.all_to_all(block, axis, 0, 0, tiled=True)  79.7 us
    all_to_all x5, waiting for transfers between devices, swap(): return lax.all_to_all(block, axis, 0, 0, tiled=True)  39.1 us
    all_to_all x5, starting transfers between devices, swap(): return lax.all_to_all(block, axis, 0, 0, tiled=True)  31.4 us
    pallas_call x11, Pallas kernels, call(): pl.pallas_call(kernel, out_shape=[jax.ShapeDtypeStruct(shape, dtype) for...  28.1 us
    ppermute x4, starting transfers between devices, from_below(): return lax.ppermute(block, 'gz', upward)  13.6 us
    unnamed x53, local copies, waits for them, and re-layouts  12.9 us
    ppermute x3, starting transfers between devices, from_above(): return lax.ppermute(block, 'gz', downward)  10.7 us
    ppermute x3, waiting for transfers between devices, from_above(): return lax.ppermute(block, 'gz', downward)  6.01 us
  transfers between devices with their start and end apart: 14, of which 10 were waited for; matrix products, arithmetic and copies ran while one was open for 2% of the time, Pallas kernels for 5%

profile of v2, /device:TPU:8, one launch (start us, length us, event | category | flops | bytes accessed | tf_op | source)
XLA Modules:
  0.0 244.7 jit_solution(3670652309622943595)
XLA Ops:
  7.2 0.0 all-gather.5.cloned.1.call-start
  7.2 1.5 pad_maximum_fusion
  8.7 0.0 all-gather.5.cloned.1.call-update
  8.8 0.1 pad_add_fusion.place
  8.8 0.7 copy-done.12
  9.5 0.7 copy-done.14
  10.2 0.7 copy-done.15
  11.0 0.6 shard_map.126
  11.5 3.5 %collective-permute-start = (bf16[8,1280]{1,0:T(8,128)(2,1)S(1)}, bf16[8,1280]{1,0:T(8,128)(2,1)S(1)}, u32[]{:S(2)}, u32[]{:S(2)}) collective-permute-start(bf16[8,1280]{1,0:T(8,128)(2,1)S(1)} %get-tuple-element.40), channel_id=1, source_target_pairs={{0,16},{16,32},{32,48},{48,64},{64,80},{80,96},{96,112},{112,128},... | collective-permute-start | bytes 61448 | tf_op jit(solution)/shard_map/ppermute | solution.py:485
  15.0 5.5 %collective-permute-start.1 = (bf16[8,1280]{1,0:T(8,128)(2,1)S(1)}, bf16[8,1280]{1,0:T(8,128)(2,1)S(1)}, u32[]{:S(2)}, u32[]{:S(2)}) collective-permute-start(bf16[8,1280]{1,0:T(8,128)(2,1)S(1)} %get-tuple-element.41), channel_id=1, source_target_pairs={{16,0},{32,16},{48,32},{64,48},{80,64},{96,80},{112,96},{128,112},... | collective-permute-start | bytes 61448 | tf_op jit(solution)/shard_map/ppermute | solution.py:488
  20.6 1.4 copy.22
  22.0 0.9 copy.23
  22.9 0.3 copy.24.pieces
  23.2 0.0 collective-permute-done.1.high
  23.2 1.2 shard_map.127
  24.4 13.6 %all_to_all.45.mixed = bf16[16,16,640]{2,1,0:T(8,128)(2,1)S(1)} all-to-all(bf16[16,16,640]{2,1,0:T(8,128)(2,1)S(1)} %get-tuple-element.43), channel_id=1, replica_groups=mesh['gz'=32,'ch'=16] {'ch'}, dimensions={0} | all-to-all | bytes 655360 | tf_op jit(solution)/shard_map/all_to_all | solution.py:491
  38.0 1.6 shard_map.128
  39.6 0.6 copy-done.6
  40.3 15.6 %all_to_all.46.parts = f32[16,8,1024]{2,1,0:T(8,128)S(1)} all-to-all(f32[16,8,1024]{2,1,0:T(8,128)S(1)} %get-tuple-element.45), channel_id=1, replica_groups=mesh['gz'=32,'ch'=16] {'ch'}, dimensions={0} | all-to-all | bytes 1048576 | tf_op jit(solution)/shard_map/all_to_all | solution.py:491
  55.8 1.9 shard_map.129
  57.7 15.1 %all-to-all-start.2 = ((bf16[32,16,384]{2,1,0:T(8,128)(2,1)}), bf16[32,16,384]{2,1,0:T(8,128)(2,1)S(1)}, u32[]{:S(2)}, u32[]{:S(2)}) async-start(bf16[32,16,384]{2,1,0:T(8,128)(2,1)} %get-tuple-element.47), calls=%async_computation.2 | async-start | bytes 786432 | tf_op jit(solution)/shard_map/all_to_all | solution.py:491
  72.8 0.0 all-gather.7.cloned.1.call-start
  72.8 0.7 all-gather.7.cloned.1.call-update
  73.5 16.6 %all-to-all-done.2.stats = bf16[32,16,384]{2,1,0:T(8,128)(2,1)S(1)} async-done(((bf16[32,16,384]{2,1,0:T(8,128)(2,1)}), bf16[32,16,384]{2,1,0:T(8,128)(2,1)S(1)}, u32[]{:S(2)}, u32[]{:S(2)}) %all-to-all-start.2) | async-done | bytes 393248 | tf_op jit(solution)/shard_map/all_to_all | solution.py:491
  90.1 1.5 shard_map.130
  91.6 3.6 %all-to-all-start.3 = ((bf16[16,16,1152]{2,1,0:T(8,128)(2,1)}), bf16[16,16,1152]{2,1,0:T(8,128)(2,1)S(1)}, u32[]{:S(2)}, u32[]{:S(2)}) async-start(bf16[16,16,1152]{2,1,0:T(8,128)(2,1)} %shard_map.130), calls=%async_computation.3 | async-start | bytes 1179648 | tf_op jit(solution)/shard_map/all_to_all | solution.py:491
  95.2 0.0 all-gather.5.cloned.1.call-done
  95.3 12.7 %all-to-all-done.3.packed = bf16[16,16,1152]{2,1,0:T(8,128)(2,1)S(1)} async-done(((bf16[16,16,1152]{2,1,0:T(8,128)(2,1)}), bf16[16,16,1152]{2,1,0:T(8,128)(2,1)S(1)}, u32[]{:S(2)}, u32[]{:S(2)}) %all-to-all-start.3) | async-done | bytes 589856 | tf_op jit(solution)/shard_map/all_to_all | solution.py:491
  108.0 1.5 copy-done
  109.4 5.1 %shard_map.131 = (f32[128,1024]{1,0:T(8,128)S(1)}, bf16[128,512]{1,0:T(8,128)(2,1)S(1)}, bf16[128,512]{1,0:T(8,128)(2,1)}, f32[32,8,128]{2,1,0:T(8,128)}) custom-call(s32[2]{0:T(128)S(1)} %pad_add_fusion.place, bf16[16,16,1152]{2,1,0:T(8,128)(2,1)S(1)} %all-to-all-done.3.packed, bf16[16,27,16,128]{3,2,1,0:T(8,128)(2,1)S(1)} %bitcast.22), custom_call_target="tpu_custom_call" | custom-call | tf_op jit(solution)/shard_map/pallas_call | solution.py:84
  114.6 0.6 copy-done.23
  115.2 4.5 %all-to-all-start.4 = ((f32[32,8,128]{2,1,0:T(8,128)}), f32[32,8,128]{2,1,0:T(8,128)S(1)}, u32[]{:S(2)}, u32[]{:S(2)}) async-start(f32[32,8,128]{2,1,0:T(8,128)} %get-tuple-element.51), calls=%async_computation.4 | async-start | bytes 262144 | tf_op jit(solution)/shard_map/all_to_all | solution.py:491
  119.8 3.4 %collective-permute-start.2 = (bf16[128,512]{1,0:T(8,128)(2,1)}, bf16[128,512]{1,0:T(8,128)(2,1)S(1)}, u32[]{:S(2)}, u32[]{:S(2)}) collective-permute-start(bf16[128,512]{1,0:T(8,128)(2,1)} %get-tuple-element.49), channel_id=1, source_target_pairs={{0,16},{16,32},{32,48},{48,64},{64,80},{80,96},{96,112},{112,128},... | collective-permute-start | bytes 393224 | tf_op jit(solution)/shard_map/ppermute | solution.py:485
  123.2 2.5 %collective-permute-start.3 = (bf16[128,512]{1,0:T(8,128)(2,1)}, bf16[128,512]{1,0:T(8,128)(2,1)S(1)}, u32[]{:S(2)}, u32[]{:S(2)}) collective-permute-start(bf16[128,512]{1,0:T(8,128)(2,1)} %copy-done.23), channel_id=1, source_target_pairs={{16,0},{32,16},{48,32},{64,48},{80,64},{96,80},{112,96},{128,112},... | collective-permute-start | bytes 393224 | tf_op jit(solution)/shard_map/ppermute | solution.py:488
  125.6 0.0 all-gather.7.cloned.1.call-done
  125.7 1.8 collective-permute-done.2.low
  127.5 2.7 %collective-permute-done.3.high = bf16[128,512]{1,0:T(8,128)(2,1)S(1)} collective-permute-done((bf16[128,512]{1,0:T(8,128)(2,1)}, bf16[128,512]{1,0:T(8,128)(2,1)S(1)}, u32[]{:S(2)}, u32[]{:S(2)}) %collective-permute-start.3) | collective-permute-done | bytes 131104 | tf_op jit(solution)/shard_map/ppermute | solution.py:488
  130.2 1.8 all-to-all-done.4.stats
  132.0 1.2 copy-done.2
  133.3 1.5 shard_map.132
  134.8 24.5 %all_to_all.47.sums_in = f32[32,8,128]{2,1,0:T(8,128)S(1)} all-to-all(f32[32,8,128]{2,1,0:T(8,128)S(1)} %get-tuple-element.57), channel_id=1, replica_groups=mesh['gz'=32,'ch'=16] {'gz'}, dimensions={0} | all-to-all | bytes 262144 | tf_op jit(solution)/shard_map/all_to_all | solution.py:491
  159.3 0.6 copy-done.9
  159.9 5.8 %shard_map.133 = (bf16[128,512]{1,0:T(8,128)(2,1)S(1)}, bf16[128,512]{1,0:T(8,128)(2,1)}, f32[128,1024]{1,0:T(8,128)S(1)}, f32[32,8,128]{2,1,0:T(8,128)}, f32[216,128]{1,0:T(8,128)S(1)}) custom-call(s32[2]{0:T(128)S(1)} %copy-done.9, f32[128,2048]{1,0:T(8,128)S(1)} %get-tuple-element.54.normed, f32[128,2048]{1,0:T(8,128)S(1)} %get-tuple-element.55.slope, ...), custom_call_target="tpu_custom_call" | custom-call | tf_op jit(solution)/shard_map/pallas_call | solution.py:84
  165.7 0.6 copy-done.22
  166.3 4.4 %all-to-all-start.6 = ((f32[32,8,128]{2,1,0:T(8,128)}), f32[32,8,128]{2,1,0:T(8,128)S(1)}, u32[]{:S(2)}, u32[]{:S(2)}) async-start(f32[32,8,128]{2,1,0:T(8,128)} %get-tuple-element.61), calls=%async_computation.6 | async-start | bytes 262144 | tf_op jit(solution)/shard_map/all_to_all | solution.py:491
  170.7 3.4 %collective-permute-start.4 = (bf16[128,512]{1,0:T(8,128)(2,1)}, bf16[128,512]{1,0:T(8,128)(2,1)S(1)}, u32[]{:S(2)}, u32[]{:S(2)}) collective-permute-start(bf16[128,512]{1,0:T(8,128)(2,1)} %get-tuple-element.59), channel_id=1, source_target_pairs={{0,16},{16,32},{32,48},{48,64},{64,80},{80,96},{96,112},{112,128},... | collective-permute-start | bytes 393224 | tf_op jit(solution)/shard_map/ppermute | solution.py:485
  174.1 2.6 %collective-permute-start.5 = (bf16[128,512]{1,0:T(8,128)(2,1)}, bf16[128,512]{1,0:T(8,128)(2,1)S(1)}, u32[]{:S(2)}, u32[]{:S(2)}) collective-permute-start(bf16[128,512]{1,0:T(8,128)(2,1)} %copy-done.22), channel_id=1, source_target_pairs={{16,0},{32,16},{48,32},{64,48},{80,64},{96,80},{112,96},{128,112},... | collective-permute-start | bytes 393224 | tf_op jit(solution)/shard_map/ppermute | solution.py:488
  176.7 1.1 collective-permute-done.4.low
  177.9 3.3 %collective-permute-done.5.high = bf16[128,512]{1,0:T(8,128)(2,1)S(1)} collective-permute-done((bf16[128,512]{1,0:T(8,128)(2,1)}, bf16[128,512]{1,0:T(8,128)(2,1)S(1)}, u32[]{:S(2)}, u32[]{:S(2)}) %collective-permute-start.5) | collective-permute-done | bytes 131104 | tf_op jit(solution)/shard_map/ppermute | solution.py:488
  181.2 1.5 all-to-all-done.6.sums_in
  182.6 0.8 copy-done.7
  183.5 0.6 copy-done.10
  184.1 0.7 copy-done.20
  184.8 6.1 %shard_map.134 = (bf16[8,1024]{1,0:T(8,128)(2,1)S(1)}, f32[16,128]{1,0:T(8,128)S(1)}, f32[16,128]{1,0:T(8,128)S(1)}, bf16[1280,128]{1,0:T(8,128)(2,1)S(1)}) custom-call(s32[2]{0:T(128)S(1)} %copy-done.10, f32[128,1024]{1,0:T(8,128)S(1)} %get-tuple-element.58.slope, bf16[128,512]{1,0:T(8,128)(2,1)S(1)} %collective-permute-done.4.low, ...), custom_call_target="tpu_custom_call" | custom-call | tf_op jit(solution)/shard_map/pallas_call | solution.py:84
  191.0 26.0 %all_to_all.48.parts = bf16[32,40,128]{2,1,0:T(8,128)(2,1)S(1)} all-to-all(bf16[32,40,128]{2,1,0:T(8,128)(2,1)S(1)} %bitcast.27), channel_id=1, replica_groups=mesh['gz'=32,'ch'=16] {'gz'}, dimensions={0} | all-to-all | bytes 655360 | tf_op jit(solution)/shard_map/all_to_all | solution.py:491
  217.0 1.3 shard_map.135
  218.4 3.9 %all-to-all-start.8 = ((bf16[32,40,128]{2,1,0:T(8,128)(2,1)}), bf16[32,40,128]{2,1,0:T(8,128)(2,1)S(1)}, u32[]{:S(2)}, u32[]{:S(2)}) async-start(bf16[32,40,128]{2,1,0:T(8,128)(2,1)} %shard_map.135), calls=%async_computation.8 | async-start | bytes 655360 | tf_op jit(solution)/shard_map/all_to_all | solution.py:491
  222.3 3.4 %collective-permute-start.6 = (f32[16,128]{1,0:T(8,128)}, f32[16,128]{1,0:T(8,128)S(1)}, u32[]{:S(2)}, u32[]{:S(2)}) collective-permute-start(f32[16,128]{1,0:T(8,128)} %copy-done.24), channel_id=1, source_target_pairs={{0,16},{16,32},{32,48},{48,64},{64,80},{80,96},{96,112},{112,128},... | collective-permute-start | bytes 24584 | tf_op jit(solution)/shard_map/ppermute | solution.py:485
  225.7 0.6 copy.25
  226.3 1.3 copy.26
  227.6 0.9 collective-permute-done.6
  228.6 1.3 fusion
  229.9 6.6 %all-to-all-done.8.gathered = bf16[32,40,128]{2,1,0:T(8,128)(2,1)S(1)} async-done(((bf16[32,40,128]{2,1,0:T(8,128)(2,1)}), bf16[32,40,128]{2,1,0:T(8,128)(2,1)S(1)}, u32[]{:S(2)}, u32[]{:S(2)}) %all-to-all-start.8) | async-done | bytes 327712 | tf_op jit(solution)/shard_map/all_to_all | solution.py:491
  236.5 1.3 shard_map.136
  (39 shorter events, 0.1 us)
Async XLA Ops:
  7.2 16.0 %copy-start.13 = (bf16[16,1,128]{2,0,1:T(8,128)(2,1)S(1)}, bf16[16,1,128]{2,0,1:T(8,128)(2,1)}, u32[]{:S(2)}) copy-start(bf16[16,1,128]{2,0,1:T(8,128)(2,1)} %param.7) | copy-start | bytes 12292
  7.2 88.1 %all-gather.5.cloned.1.call-start = ((), (), s32[]{:S(2)}) async-start(), calls=%async_computation.9 | async-start | bytes 1880064 | tf_op jit(solution)/shard_map/all_gather | solution.py:498
  8.8 123.2 %copy-start.8 = (s32[2]{0:T(128)}, s32[2]{0:T(128)S(1)}, u32[]{:S(2)}) copy-start(s32[2]{0:T(128)S(1)} %pad_add_fusion.place) | copy-start | bytes 28
  8.8 0.7 copy-start.12
  9.5 0.7 copy-start.14
  10.2 0.7 copy-start.15
  11.5 11.7 %collective-permute-start = (bf16[8,1280]{1,0:T(8,128)(2,1)S(1)}, bf16[8,1280]{1,0:T(8,128)(2,1)S(1)}, u32[]{:S(2)}, u32[]{:S(2)}) collective-permute-start(bf16[8,1280]{1,0:T(8,128)(2,1)S(1)} %get-tuple-element.40), channel_id=1, source_target_pairs={{0,16},{16,32},{32,48},{48,64},{64,80},{80,96},{96,112},{112,128},... | collective-permute-start | bytes 61448 | tf_op jit(solution)/shard_map/ppermute | solution.py:485
  15.0 8.2 %collective-permute-start.1 = (bf16[8,1280]{1,0:T(8,128)(2,1)S(1)}, bf16[8,1280]{1,0:T(8,128)(2,1)S(1)}, u32[]{:S(2)}, u32[]{:S(2)}) collective-permute-start(bf16[8,1280]{1,0:T(8,128)(2,1)S(1)} %get-tuple-element.41), channel_id=1, source_target_pairs={{16,0},{32,16},{48,32},{64,48},{80,64},{96,80},{112,96},{128,112},... | collective-permute-start | bytes 61448 | tf_op jit(solution)/shard_map/ppermute | solution.py:488
  21.9 16.1 %copy-start.4 = (bf16[27,128,8]{1,2,0:T(8,128)(2,1)S(1)}, bf16[27,128,8]{1,2,0:T(8,128)(2,1)}, u32[]{:S(2)}) copy-start(bf16[27,128,8]{1,2,0:T(8,128)(2,1)} %param.11) | copy-start | bytes 165892
  22.0 16.0 %copy-start.5 = (bf16[27,128,8]{1,2,0:T(8,128)(2,1)S(1)}, bf16[27,128,8]{1,2,0:T(8,128)(2,1)}, u32[]{:S(2)}) copy-start(bf16[27,128,8]{1,2,0:T(8,128)(2,1)} %param.10) | copy-start | bytes 165892
  24.4 49.1 %copy-start.19 = (bf16[2,16,128]{2,1,0:T(8,128)(2,1)}, bf16[2,16,128]{2,1,0:T(8,128)(2,1)S(1)}, u32[]{:S(2)}) copy-start(bf16[2,16,128]{2,1,0:T(8,128)(2,1)S(1)} %get-tuple-element.62.coarse) | copy-start | bytes 24580
  39.6 0.6 copy-start.6
  57.7 32.4 %all-to-all-start.2 = ((bf16[32,16,384]{2,1,0:T(8,128)(2,1)}), bf16[32,16,384]{2,1,0:T(8,128)(2,1)S(1)}, u32[]{:S(2)}, u32[]{:S(2)}) async-start(bf16[32,16,384]{2,1,0:T(8,128)(2,1)} %get-tuple-element.47), calls=%async_computation.2 | async-start | bytes 786432 | tf_op jit(solution)/shard_map/all_to_all | solution.py:491
  72.8 52.9 %all-gather.7.cloned.1.call-start = ((), (), s32[]{:S(2)}) async-start(), calls=%async_computation.10 | async-start | bytes 1114112 | tf_op jit(solution)/shard_map/all_gather | solution.py:514
  91.6 16.3 %all-to-all-start.3 = ((bf16[16,16,1152]{2,1,0:T(8,128)(2,1)}), bf16[16,16,1152]{2,1,0:T(8,128)(2,1)S(1)}, u32[]{:S(2)}, u32[]{:S(2)}) async-start(bf16[16,16,1152]{2,1,0:T(8,128)(2,1)} %shard_map.130), calls=%async_computation.3 | async-start | bytes 1179648 | tf_op jit(solution)/shard_map/all_to_all | solution.py:491
  108.0 1.5 copy-start
  114.6 0.6 copy-start.23
  114.6 44.7 %copy-start.1 = (bf16[432,16,128]{2,1,0:T(8,128)(2,1)S(1)}, bf16[432,16,128]{2,1,0:T(8,128)(2,1)}, u32[]{:S(2)}) copy-start(bf16[432,16,128]{2,1,0:T(8,128)(2,1)} %all-gather.5.cloned.1.call-done) | copy-start | bytes 5308420
  115.2 16.8 %all-to-all-start.4 = ((f32[32,8,128]{2,1,0:T(8,128)}), f32[32,8,128]{2,1,0:T(8,128)S(1)}, u32[]{:S(2)}, u32[]{:S(2)}) async-start(f32[32,8,128]{2,1,0:T(8,128)} %get-tuple-element.51), calls=%async_computation.4 | async-start | bytes 262144 | tf_op jit(solution)/shard_map/all_to_all | solution.py:491
  119.8 7.7 %collective-permute-start.2 = (bf16[128,512]{1,0:T(8,128)(2,1)}, bf16[128,512]{1,0:T(8,128)(2,1)S(1)}, u32[]{:S(2)}, u32[]{:S(2)}) collective-permute-start(bf16[128,512]{1,0:T(8,128)(2,1)} %get-tuple-element.49), channel_id=1, source_target_pairs={{0,16},{16,32},{32,48},{48,64},{64,80},{80,96},{96,112},{112,128},... | collective-permute-start | bytes 393224 | tf_op jit(solution)/shard_map/ppermute | solution.py:485
  123.2 7.1 %collective-permute-start.3 = (bf16[128,512]{1,0:T(8,128)(2,1)}, bf16[128,512]{1,0:T(8,128)(2,1)S(1)}, u32[]{:S(2)}, u32[]{:S(2)}) collective-permute-start(bf16[128,512]{1,0:T(8,128)(2,1)} %copy-done.23), channel_id=1, source_target_pairs={{16,0},{32,16},{48,32},{64,48},{80,64},{96,80},{112,96},{128,112},... | collective-permute-start | bytes 393224 | tf_op jit(solution)/shard_map/ppermute | solution.py:488
  132.0 1.2 copy-start.2
  134.7 24.5 %copy-start.16 = (bf16[8,1024]{1,0:T(8,128)(2,1)}, bf16[8,1024]{1,0:T(8,128)(2,1)S(1)}, u32[]{:S(2)}) copy-start(bf16[8,1024]{1,0:T(8,128)(2,1)S(1)} %get-tuple-element.53) | copy-start | bytes 49156
  159.3 0.6 copy-start.9
  159.9 22.8 %copy-start.3 = (bf16[27,128,16]{1,2,0:T(8,128)(2,1)S(1)}, bf16[27,128,16]{1,2,0:T(8,128)(2,1)}, u32[]{:S(2)}) copy-start(bf16[27,128,16]{1,2,0:T(8,128)(2,1)} %param.9) | copy-start | bytes 331780
  165.7 0.7 copy-start.22
  166.3 16.3 %all-to-all-start.6 = ((f32[32,8,128]{2,1,0:T(8,128)}), f32[32,8,128]{2,1,0:T(8,128)S(1)}, u32[]{:S(2)}, u32[]{:S(2)}) async-start(f32[32,8,128]{2,1,0:T(8,128)} %get-tuple-element.61), calls=%async_computation.6 | async-start | bytes 262144 | tf_op jit(solution)/shard_map/all_to_all | solution.py:491
  170.7 7.2 %collective-permute-start.4 = (bf16[128,512]{1,0:T(8,128)(2,1)}, bf16[128,512]{1,0:T(8,128)(2,1)S(1)}, u32[]{:S(2)}, u32[]{:S(2)}) collective-permute-start(bf16[128,512]{1,0:T(8,128)(2,1)} %get-tuple-element.59), channel_id=1, source_target_pairs={{0,16},{16,32},{32,48},{48,64},{64,80},{80,96},{96,112},{112,128},... | collective-permute-start | bytes 393224 | tf_op jit(solution)/shard_map/ppermute | solution.py:485
  174.1 7.1 %collective-permute-start.5 = (bf16[128,512]{1,0:T(8,128)(2,1)}, bf16[128,512]{1,0:T(8,128)(2,1)S(1)}, u32[]{:S(2)}, u32[]{:S(2)}) collective-permute-start(bf16[128,512]{1,0:T(8,128)(2,1)} %copy-done.22), channel_id=1, source_target_pairs={{16,0},{32,16},{48,32},{64,48},{80,64},{96,80},{112,96},{128,112},... | collective-permute-start | bytes 393224 | tf_op jit(solution)/shard_map/ppermute | solution.py:488
  182.6 0.8 copy-start.7
  183.5 0.6 copy-start.10
  184.1 0.7 copy-start.20
  190.9 26.1 %copy-start.18 = (bf16[8,1024]{1,0:T(8,128)(2,1)}, bf16[8,1024]{1,0:T(8,128)(2,1)S(1)}, u32[]{:S(2)}) copy-start(bf16[8,1024]{1,0:T(8,128)(2,1)S(1)} %get-tuple-element.67) | copy-start | bytes 49156
  190.9 26.1 %copy-start.21 = (f32[16,128]{1,0:T(8,128)}, f32[16,128]{1,0:T(8,128)S(1)}, u32[]{:S(2)}) copy-start(f32[16,128]{1,0:T(8,128)S(1)} %get-tuple-element.65) | copy-start | bytes 24580
  191.0 26.1 %copy-start.24 = (f32[16,128]{1,0:T(8,128)}, f32[16,128]{1,0:T(8,128)S(1)}, u32[]{:S(2)}) copy-start(f32[16,128]{1,0:T(8,128)S(1)} %get-tuple-element.66) | copy-start | bytes 24580
  191.0 34.7 %copy-start.17 = (bf16[8,1024]{1,0:T(8,128)(2,1)S(1)}, bf16[8,1024]{1,0:T(8,128)(2,1)}, u32[]{:S(2)}) copy-start(bf16[8,1024]{1,0:T(8,128)(2,1)} %copy-done.16) | copy-start | bytes 49156
  191.0 45.5 %copy-start.11 = (s32[2]{0:T(128)S(1)}, s32[2]{0:T(128)}, u32[]{:S(2)}) copy-start(s32[2]{0:T(128)} %copy-done.8) | copy-start | bytes 28
  218.4 18.1 %all-to-all-start.8 = ((bf16[32,40,128]{2,1,0:T(8,128)(2,1)}), bf16[32,40,128]{2,1,0:T(8,128)(2,1)S(1)}, u32[]{:S(2)}, u32[]{:S(2)}) async-start(bf16[32,40,128]{2,1,0:T(8,128)(2,1)} %shard_map.135), calls=%async_computation.8 | async-start | bytes 655360 | tf_op jit(solution)/shard_map/all_to_all | solution.py:491
  222.3 6.3 %collective-permute-start.6 = (f32[16,128]{1,0:T(8,128)}, f32[16,128]{1,0:T(8,128)S(1)}, u32[]{:S(2)}, u32[]{:S(2)}) collective-permute-start(f32[16,128]{1,0:T(8,128)} %copy-done.24), channel_id=1, source_target_pairs={{0,16},{16,32},{32,48},{48,64},{64,80},{80,96},{96,112},{112,128},... | collective-permute-start | bytes 24584 | tf_op jit(solution)/shard_map/ppermute | solution.py:485
Sparse Core Ops, SparseCore 0:
  10.7 48.4 all-gather.4
  76.3 38.9 all-gather.6

commit v3 on v2

--- a/solution.py
+++ b/solution.py
@@ -78,20 +78,45 @@
     return jnp.transpose(jnp.broadcast_to(row, (C_OUT, C_OUT)))[:, :1]
 
 
-def call(kernel, outs, args, scratch=(), megabytes=8):
-    specs = [pl.BlockSpec(memory_space=pltpu.SMEM)]
-    specs += [pl.BlockSpec(memory_space=pltpu.VMEM)] * (len(args) - 1)
+def call(kernel, outs, args, scratch=(), megabytes=8, far=(), far_outs=(), near=(), near_outs=()):
+    args = list(args)
+    for index in far:
+        args[index] = pltpu.with_memory_space_constraint(args[index], pltpu.HBM)
+    for index in near:
+        args[index] = pltpu.with_memory_space_constraint(args[index], pltpu.VMEM)
+
+    def spec(index, which):
+        return pl.BlockSpec(memory_space=pltpu.HBM if index in which else pltpu.VMEM)
+
+    def out(index, shape, dtype):
+        if index in far_outs:
+            return pltpu.HBM(shape, dtype)
+        return pltpu.VMEM(shape, dtype) if index in near_outs else jax.ShapeDtypeStruct(shape, dtype)
+
     return pl.pallas_call(
         kernel,
-        out_shape=[jax.ShapeDtypeStruct(shape, dtype) for shape, dtype in outs],
-        in_specs=specs,
-        out_specs=[pl.BlockSpec(memory_space=pltpu.VMEM)] * len(outs),
+        out_shape=[out(index, *shape) for index, shape in enumerate(outs)],
+        in_specs=[spec(index, far) for index in range(len(args))],
+        out_specs=[spec(index, far_outs) for index in range(len(outs))],
         scratch_shapes=list(scratch),
         compiler_params=pltpu.CompilerParams(vmem_limit_bytes=megabytes * 2**20),
     )(*args)
 
 
-def halo_kernel(place, coarse, skip, cotangent, upward, downward, own_skip, own_cot):
+def copies(sources, targets, semaphores):
+    started = []
+    for index, (source, target) in enumerate(zip(sources, targets)):
+        copy = pltpu.make_async_copy(source, target, semaphores.at[index])
+        copy.start()
+        started.append(copy)
+    return started
+
+
+def halo_kernel(
+    far_coarse, far_skip, far_cot, upward, downward, own_skip, own_cot, coarse, skip, cotangent, semaphores
+):
+    for copy in copies((far_coarse, far_skip, far_cot), (coarse, skip, cotangent), semaphores):
+        copy.wait()
     cells = coarse[...].astype(f32)
     cells = [cells[:8], cells[8:]]
     skip_planes, cot_planes = skip[...].astype(f32), cotangent[...].astype(f32)
@@ -103,7 +128,7 @@
     own_cot[...] = jnp.concatenate([cot_planes[:, 0], cot_planes[:, 1]], axis=1).astype(bf16)
 
 
-def mix_kernel(place, pieces, coarse, low, high, own_cot, mixed, pair, cot_planes):
+def mix_kernel(pieces, coarse, low, high, own_cot, mixed, pair, cot_planes):
     below, above = low[...].astype(f32), high[...].astype(f32)
     here = coarse[...].astype(f32)
     before = jnp.concatenate([below[:, :COARSE], below[:, COARSE : 2 * COARSE]], axis=0)
@@ -122,8 +147,8 @@
     cot_planes[16:32] = jnp.zeros((16, SLAB), bf16)
 
 
-def up_kernel(place, mixed, own_skip, low, high, first_up, first_skip, partial, joined, unfolded):
-    slab = place[0]
+def up_kernel(mixed, own_skip, low, high, first_up, first_skip, partial, joined, unfolded):
+    slab = lax.axis_index("gz")
     packed = mixed[...]
     weights = packed[:, :, :256].reshape(256, 256)
     mixture = []
@@ -174,7 +199,11 @@
             (((0,), (0,)), ((), ())),
             preferred_element_type=f32,
         )
-    partial[...] = total.reshape(16, 8, SLAB)
+    mean = jnp.sum(total, axis=1, keepdims=True) / SLAB
+    deviation = total - mean
+    first = jnp.concatenate([deviation[:, :FINE], in_parts(mean)], axis=1).reshape(16, 8, FINE + 128)
+    second = jnp.concatenate([deviation[:, FINE:], jnp.zeros((C_OUT, 128), f32)], axis=1)
+    partial[...] = jnp.concatenate([first, second.reshape(16, 8, FINE + 128)], axis=1).astype(bf16)
 
 
 def in_parts(values):
@@ -187,8 +216,11 @@
     )
 
 
-def first_sum_kernel(place, parts, pre, stats):
-    total = jnp.sum(parts[...], axis=0)
+def first_sum_kernel(parts, pre, stats):
+    slab = lax.axis_index("gz")
+    both = jnp.sum(parts[...].astype(f32), axis=0)
+    total = jnp.concatenate([both[:8, :FINE], both[8:, :FINE]], axis=1)
+    total = total + jnp.sum(both[:8, FINE:], axis=1, keepdims=True)
     pre[...] = total
     mean = jnp.sum(total, axis=1, keepdims=True) / SLAB
     deviation = total - mean
@@ -200,7 +232,7 @@
     first = jnp.concatenate([first, tail], axis=1).astype(bf16)
     last = jnp.concatenate([last, tail], axis=1).astype(bf16)
     for target in range(stats.shape[0]):
-        above = target > place[0]
+        above = target > slab
 
         @pl.when(above)
         def _():
@@ -211,8 +243,8 @@
             stats[target] = first
 
 
-def first_norm_kernel(place, pre, stats, packed):
-    slab, slabs = place[0], stats.shape[0]
+def first_norm_kernel(pre, stats, packed):
+    slab, slabs = lax.axis_index("gz"), stats.shape[0]
     half = FINE // 2
     tails = jnp.sum(stats[:, :, half:].astype(f32), axis=2, keepdims=True)
     means = tails[:, :8]
@@ -250,7 +282,7 @@
 def unfold_block(values, unfolded, block, sign):
     for tap in range(9):
         moved = fine_shift(values, sign * (tap // 3 - 1), sign * (tap % 3 - 1))
-        unfolded[pl.ds(pl.multiple_of(tap * 128 + block * 16, 16), 16), :] = moved.astype(bf16)
+        unfolded[tap, pl.ds(pl.multiple_of(block * 16, 16), 16), :] = moved.astype(bf16)
 
 
 def tap_matrix(weights, tap, first):
@@ -258,8 +290,23 @@
     return both[:, first * 8 : first * 8 + 8].reshape(C_OUT, C_OUT)
 
 
-def second_conv_kernel(place, packed, weights, pre, low, high, stats, unfolded, matrix):
-    mask = edge_mask(place[0], stats.shape[0])
+def matrix_kernel(weights, first_skip, forward, far_backward, far_first, backward, first, semaphores):
+    for tap in range(27):
+        at = slice(tap * 128, tap * 128 + 128)
+        second = tap_matrix(weights, tap, 0)
+        forward[:, at] = jnp.transpose(second).astype(bf16)
+        backward[:, at] = second.astype(bf16)
+        skip_part = jnp.concatenate([first_skip[tap].astype(f32), jnp.zeros((8, 128), f32)], axis=0)
+        first[0:128, at] = tap_matrix(weights, tap, 1).astype(bf16)
+        first[128:144, at] = skip_part.astype(bf16)
+    for copy in copies((backward, first), (far_backward, far_first), semaphores):
+        copy.wait()
+
+
+def second_conv_kernel(
+    packed, matrix, pre, low, high, stats, unfolded
+):
+    mask = edge_mask(lax.axis_index("gz"), stats.shape[0])
 
     def prepare(block, carry):
         hidden = activate(read_planes(packed, block)).astype(bf16).astype(f32) * mask
@@ -267,13 +314,11 @@
         return carry
 
     lax.fori_loop(0, 8, prepare, 0)
-    for tap in range(27):
-        matrix[:, tap * 128 : tap * 128 + 128] = jnp.transpose(tap_matrix(weights, tap, 0)).astype(bf16)
     total = jnp.zeros((C_OUT, SLAB), f32)
     for k_z in range(3):
         total = total + jnp.dot(
             matrix[:, k_z * 1152 : k_z * 1152 + 1152],
-            unfolded[:, k_z * FINE : k_z * FINE + SLAB],
+            unfolded[:, :, k_z * FINE : k_z * FINE + SLAB].reshape(1152, SLAB),
             preferred_element_type=f32,
         )
     pre[...] = total
@@ -282,29 +327,30 @@
     square = jnp.sum(deviation * deviation, axis=1, keepdims=True)
     low[...] = deviation[:, :FINE].astype(bf16)
     high[...] = deviation[:, FINE:].astype(bf16)
-    row = lax.broadcasted_iota(jnp.int32, (8, 128), 0)
-    tile = jnp.where(row < 4, as_row(mean), as_row(square))
+    row = lax.broadcasted_iota(jnp.int32, (2, 128), 0)
+    tile = jnp.where(row < 1, as_row(mean), as_row(square))
     stats[...] = jnp.broadcast_to(tile[None], stats.shape)
 
 
 def second_norm_kernel(
-    place, pre, low, high, stats, cotangent, decoded, normed, slope, inverse_out, sums
+    pre, low, high, stats, far_cot, decoded, normed, slope, inverse_out, sums, cotangent, semaphores
 ):
-    slab, share = place[0], place[1]
+    (fetch,) = copies((far_cot.at[:, pl.ds(0, 16)],), (cotangent,), semaphores)
+    slab, share = lax.axis_index("gz"), lax.axis_index("ch")
     slabs = stats.shape[0]
     gathered = stats[...]
     means = gathered[:, 0:1]
     mean_row = jnp.sum(means, axis=0) / slabs
     apart = means - mean_row[None]
-    square = jnp.sum(gathered[:, 7:8] + SLAB * apart * apart, axis=0)
+    square = jnp.sum(gathered[:, 1:2] + SLAB * apart * apart, axis=0)
     inverse_row = lax.rsqrt(square / (slabs * SLAB) + NORM_EPS)
     inverse_out[...] = jnp.broadcast_to(inverse_row, inverse_out.shape)
     below = stats[jnp.maximum(slab - 1, 0)][0:1] - mean_row
     above = stats[jnp.minimum(slab + 1, slabs - 1)][0:1] - mean_row
     mean, inverse = as_column(mean_row), as_column(inverse_row)
     normed[:, :FINE] = (low[...].astype(f32) + as_column(below)) * inverse
+    normed[:, 3 * FINE :] = (high[...].astype(f32) + as_column(above)) * inverse
     normed[:, FINE : 3 * FINE] = (pre[...] - mean) * inverse
-    normed[:, 3 * FINE :] = (high[...].astype(f32) + as_column(above)) * inverse
     own = normed[pl.ds(pl.multiple_of(share * 8, 8), 8), FINE : 3 * FINE]
     decoded[...] = activate(own).astype(bf16)
 
@@ -313,24 +359,27 @@
         slope[at, :] = read_planes(cotangent, block) * activate_slope(normed[at, :])
         return carry
 
+    fetch.wait()
     lax.fori_loop(0, 8, prepare, 0)
     inner = slope[:, FINE : 3 * FINE]
     one = as_row(jnp.sum(inner, axis=1, keepdims=True))
     two = as_row(jnp.sum(inner * normed[:, FINE : 3 * FINE], axis=1, keepdims=True))
-    row = lax.broadcasted_iota(jnp.int32, (8, 128), 0)
-    sums[...] = jnp.broadcast_to(jnp.where(row < 4, one, two)[None], sums.shape)
+    row = lax.broadcasted_iota(jnp.int32, (2, 128), 0)
+    sums[...] = jnp.broadcast_to(jnp.where(row < 1, one, two)[None], sums.shape)
 
 
 def total_means(sums):
     totals = jnp.sum(sums[...], axis=0) / (sums.shape[0] * SLAB)
-    return as_column(totals[0:1]), as_column(totals[7:8])
+    return as_column(totals[0:1]), as_column(totals[1:2])
 
 
 def second_back_kernel(
-    place, normed, slope, inverse_row, sums_in, packed, weights,
-    low, high, slope_one, sums, weight_grad, unfolded, matrix, grads, columns, own_cols,
+    normed, slope, inverse_row, sums_in, packed, far_matrix,
+    low, high, slope_one, sums, weight_grad,
+    unfolded, grads, columns, matrix, own_unfolded, semaphores,
 ):
-    slab, share = place[0], place[1]
+    (fetch,) = copies((far_matrix,), (matrix,), semaphores)
+    slab, share = lax.axis_index("gz"), lax.axis_index("ch")
     mask = edge_mask(slab, sums.shape[0])
     mean_grad, mean_cross = total_means(sums_in)
     columns[0] = jnp.broadcast_to(mean_grad, (C_OUT, 128))
@@ -341,18 +390,17 @@
         at = pl.ds(pl.multiple_of(block * 16, 16), 16)
         grad = columns[2, at, :1] * (slope[at, :] - columns[0, at, :1] - normed[at, :] * columns[1, at, :1])
         grad = grad.astype(bf16).astype(f32) * mask
-        grads[at, :] = grad[:, FINE : 3 * FINE].astype(bf16)
+        grads[at, :] = grad[:, FINE : 3 * FINE]
         unfold_block(grad, unfolded, block, -1)
         return carry
 
     lax.fori_loop(0, 8, prepare, 0)
-    for tap in range(27):
-        matrix[:, tap * 128 : tap * 128 + 128] = tap_matrix(weights, tap, 0).astype(bf16)
+    fetch.wait()
     total = jnp.zeros((C_OUT, SLAB), f32)
     for k_z in range(3):
         total = total + jnp.dot(
             matrix[:, k_z * 1152 : k_z * 1152 + 1152],
-            unfolded[:, (2 - k_z) * FINE : (2 - k_z) * FINE + SLAB],
+            unfolded[:, :, (2 - k_z) * FINE : (2 - k_z) * FINE + SLAB].reshape(1152, SLAB),
             preferred_element_type=f32,
         )
     low[...] = total[:, :FINE].astype(bf16)
@@ -365,27 +413,27 @@
     slope_one[...] = inner
     one = as_row(jnp.sum(inner, axis=1, keepdims=True))
     two = as_row(jnp.sum(inner * first_normed, axis=1, keepdims=True))
-    row = lax.broadcasted_iota(jnp.int32, (8, 128), 0)
-    sums[...] = jnp.broadcast_to(jnp.where(row < 4, one, two)[None], sums.shape)
-    own = packed[share].astype(f32)
-    own = jnp.concatenate([own[:8, :SLAB], own[8:, :SLAB]], axis=1)
-    own = activate(own).astype(bf16).astype(f32) * mask
+    row = lax.broadcasted_iota(jnp.int32, (2, 128), 0)
+    sums[...] = jnp.broadcast_to(jnp.where(row < 1, one, two)[None], sums.shape)
+    own = activate(read_planes(packed, share // 2)).astype(bf16).astype(f32) * mask
     for tap in range(9):
-        moved = fine_shift(own, tap // 3 - 1, tap % 3 - 1)
-        for k_z in range(3):
-            at = (k_z * 9 + tap) * 8
-            own_cols[at : at + 8, :] = moved[:, k_z * FINE : k_z * FINE + SLAB]
-    weight_grad[...] = lax.dot_general(
-        own_cols[...].astype(bf16), grads[...], (((1,), (1,)), ((), ())), preferred_element_type=f32
-    )
+        own_unfolded[tap * 16 : tap * 16 + 16, :] = fine_shift(own, tap // 3 - 1, tap % 3 - 1).astype(bf16)
+    odd = share % 2 == 1
+    turned = jnp.transpose(grads[...]).astype(bf16)
+    for k_z in range(3):
+        product = jnp.dot(
+            own_unfolded[:, k_z * FINE : k_z * FINE + SLAB], turned, preferred_element_type=f32
+        ).reshape(9, 2, 8, 128)
+        weight_grad[k_z * 72 : k_z * 72 + 72, :] = jnp.where(odd, product[:, 1], product[:, 0]).reshape(72, 128)
 
 
 def first_back_kernel(
-    place, slope, low, high, sums_in, packed, weights, first_skip, up_weight, coarse, joined, second_grad,
+    slope, low, high, sums_in, packed, far_matrix, up_weight, coarse, joined, second_grad,
     skip_grad, coarse_own, coarse_next, weight_grads,
-    unfolded, matrix, grads, columns, own_cols, spread, up_matrix,
+    unfolded, grads, columns, spread, up_matrix, matrix, own_unfolded, semaphores,
 ):
-    slab = place[0]
+    (fetch,) = copies((far_matrix,), (matrix,), semaphores)
+    slab = lax.axis_index("gz")
     mask = edge_mask(slab, sums_in.shape[0])
     mean_grad, mean_cross = total_means(sums_in)
     columns[0] = jnp.broadcast_to(mean_grad, (C_OUT, 128))
@@ -401,31 +449,22 @@
         inner = jnp.concatenate([bottom, slope[at, :], top], axis=1)
         grad = columns[2, at, :1] * (inner - columns[0, at, :1] - normed * columns[1, at, :1])
         grad = grad.astype(bf16).astype(f32) * mask
-        grads[at, :] = grad[:, FINE : 3 * FINE].astype(bf16)
+        grads[at, :] = grad[:, FINE : 3 * FINE]
         unfold_block(grad, unfolded, block, -1)
         return carry
 
     lax.fori_loop(0, 8, prepare, 0)
-    for tap in range(27):
-        at = slice(tap * 128, tap * 128 + 128)
-        skip_part = jnp.concatenate([first_skip[tap].astype(f32), jnp.zeros((8, 128), f32)], axis=0)
-        matrix[0:128, at] = tap_matrix(weights, tap, 1).astype(bf16)
-        matrix[128:144, at] = skip_part.astype(bf16)
+    fetch.wait()
     total = jnp.zeros((144, SLAB), f32)
     for k_z in range(3):
         total = total + jnp.dot(
             matrix[:, k_z * 1152 : k_z * 1152 + 1152],
-            unfolded[:, (2 - k_z) * FINE : (2 - k_z) * FINE + SLAB],
+            unfolded[:, :, (2 - k_z) * FINE : (2 - k_z) * FINE + SLAB].reshape(1152, SLAB),
             preferred_element_type=f32,
         )
     skip_grad[...] = total[128:136].astype(bf16)
-    own = joined[...].astype(f32)
-    for tap in range(9):
-        moved = fine_shift(own, tap // 3 - 1, tap % 3 - 1).astype(bf16)
-        for k_z in range(3):
-            at = (k_z * 9 + tap) * 16
-            own_cols[at : at + 16, :] = moved[:, k_z * FINE : k_z * FINE + SLAB]
     d_up = jnp.concatenate([total[:128, :FINE], total[:128, FINE:]], axis=0).astype(bf16)
+    last = (((1,), (1,)), ((), ()))
     parted = jnp.dot(d_up, interleave_matrix(True), preferred_element_type=f32)
     for y_par in (0, 1):
         for x_par in (0, 1):
@@ -447,26 +486,31 @@
         up_matrix[:, 1152:2304], low_plane, preferred_element_type=f32
     ) + jnp.dot(up_matrix[:, 2304:], high_plane, preferred_element_type=f32)
     coarse_next[...] = jnp.dot(up_matrix[:, :1152], high_plane, preferred_element_type=f32)
-    last = (((1,), (1,)), ((), ()))
     here, following = coarse[0], coarse[1]
     for k_z, source, plane in ((0, following, high_plane), (1, here, low_plane), (2, here, high_plane)):
         product = lax.dot_general(source, plane, last, preferred_element_type=f32)
         for tap in range(9):
             at = (k_z * 9 + tap) * 16
             weight_grads[at : at + 16, :] = product[:, tap * 128 : tap * 128 + 128].astype(bf16)
-    weight_grads[432:864, :] = lax.dot_general(
-        own_cols[...], grads[...], last, preferred_element_type=f32
-    ).astype(bf16)
+    own = joined[...].astype(f32)
+    for tap in range(9):
+        own_unfolded[tap * 16 : tap * 16 + 16, :] = fine_shift(own, tap // 3 - 1, tap % 3 - 1).astype(bf16)
+    turned = jnp.transpose(grads[...]).astype(bf16)
+    for k_z in range(3):
+        product = jnp.dot(
+            own_unfolded[:, k_z * FINE : k_z * FINE + SLAB], turned, preferred_element_type=f32
+        )
+        weight_grads[432 + k_z * 144 : 576 + k_z * 144, :] = product.astype(bf16)
     rest = jnp.concatenate([second_grad[...], jnp.zeros((GRAD_ROWS - 1080, 128), f32)], axis=0)
     weight_grads[864:, :] = rest.astype(bf16)
 
 
-def grad_sum_kernel(place, parts, spread):
+def grad_sum_kernel(parts, spread):
     total = jnp.sum(parts[...].astype(f32), axis=0) * (1.0 / math.sqrt(SLAB))
     spread[...] = jnp.broadcast_to(total.astype(bf16)[None], spread.shape)
 
 
-def grad_split_kernel(place, gathered, up, first_up, first_skip, second):
+def grad_split_kernel(gathered, up, first_up, first_skip, second):
     values = gathered[...].reshape(GRAD_ROWS, 128).astype(f32)
     up[...] = values[:432].reshape(27, 16, 128)
     first = values[432:864].reshape(27, 16, 128)
@@ -477,7 +521,6 @@
 
 def local(coarse, encoder_skip, up_weight, first_up, first_skip, second_weight, cotangent):
     slabs, shares = lax.axis_size("gz"), lax.axis_size("ch")
-    place = jnp.stack([lax.axis_index("gz"), lax.axis_index("ch")]).astype(jnp.int32)
     upward = [(i, i + 1) for i in range(slabs - 1)]
     downward = [(i + 1, i) for i in range(slabs - 1)]
 
@@ -495,93 +538,124 @@
 
     up_own, up_first = io_major(up_weight), io_major(first_up)
     skip_first, second_own = io_major(first_skip), io_major(second_weight)
-    kernels = lax.all_gather(jnp.concatenate([second_own, up_first], axis=1), "ch", axis=0)
 
     here = coarse.reshape(16, COARSE)
     halo = ((8, 2 * COARSE + 2 * FINE), bf16)
     upper, lower, own_skip, own_cot = call(
         halo_kernel,
         [halo, halo, ((8, SLAB), bf16), ((8, SLAB), bf16)],
-        (place, here, encoder_skip, cotangent),
+        (here, encoder_skip, cotangent),
+        [
+            pltpu.VMEM((16, COARSE), bf16), pltpu.VMEM((8, 2, FINE), bf16), pltpu.VMEM((8, 2, FINE), bf16),
+            pltpu.SemaphoreType.DMA((3,)),
+        ],
+        far=(0, 1, 2),
     )
     low, high = from_below(upper), from_above(lower)
     pieces = jnp.transpose(up_weight.reshape(27, 16, 8, 16), (1, 3, 0, 2)).reshape(16, 16, 216)
     mixed, pair, cot_planes = call(
         mix_kernel,
         [((16, 16, 640), bf16), ((2, 16, COARSE), bf16), ((32, SLAB), bf16)],
-        (place, pieces, here, low, high, own_cot),
-    )
+        (pieces, here, low, high, own_cot),
+    )
+    mixed, second_own, up_shared = lax.optimization_barrier((mixed, second_own, up_first))
+    kernels = lax.all_gather(jnp.concatenate([second_own, up_shared], axis=1), "ch", axis=0)
     cot_planes = lax.all_gather(cot_planes, "ch", axis=0)
 
     partial, joined = call(
         up_kernel,
-        [((16, 8, SLAB), f32), ((16, HALOED), bf16)],
-        (place, swap(mixed, "ch"), own_skip, low, high, up_first, skip_first),
+        [((16, 16, FINE + 128), bf16), ((16, HALOED), bf16)],
+        (swap(mixed, "ch"), own_skip, low, high, up_first, skip_first),
         [pltpu.VMEM((144, HALOED), bf16)],
+        near_outs=(1,),
     )
     pre, stats = call(
         first_sum_kernel,
         [((8, SLAB), f32), ((slabs, 16, FINE // 2 + 128), bf16)],
-        (place, swap(partial, "ch")),
+        (swap(partial, "ch"),),
     )
     (packed,) = call(
-        first_norm_kernel, [((16, 16, SLAB + 128), bf16)], (place, pre, swap(stats, "gz"))
-    )
+        first_norm_kernel, [((16, 16, SLAB + 128), bf16)], (pre, swap(stats, "gz"))
+    )
+    packed, kernels = lax.optimization_barrier((packed, kernels))
     packed = swap(packed, "ch")
-    unfolded = pltpu.VMEM((1152, HALOED), bf16)
+    forward, backward, first = call(
+        matrix_kernel,
+        [((128, 3456), bf16), ((128, 3456), bf16), ((144, 3456), bf16)],
+        (kernels, skip_first),
+        [pltpu.VMEM((128, 3456), bf16), pltpu.VMEM((144, 3456), bf16), pltpu.SemaphoreType.DMA((2,))],
+        far_outs=(1, 2),
+        near_outs=(0,),
+    )
+    unfolded = pltpu.VMEM((9, 128, HALOED), bf16)
     second_pre, low, high, stats = call(
         second_conv_kernel,
-        [((128, SLAB), f32), ((128, FINE), bf16), ((128, FINE), bf16), ((slabs, 8, 128), f32)],
-        (place, packed, kernels),
-        [unfolded, pltpu.VMEM((128, 3456), bf16)],
-        16,
+        [
+            ((128, SLAB), f32), ((128, FINE), bf16), ((128, FINE), bf16), ((slabs, 2, 128), f32),
+        ],
+        (packed, forward),
+        [unfolded],
+        14,
+        near=(1,),
+        near_outs=(0, 1, 2),
     )
     decoded, normed, slope, inverse, sums = call(
         second_norm_kernel,
         [
             ((8, SLAB), bf16), ((128, HALOED), f32), ((128, HALOED), f32), ((8, 128), f32),
-            ((slabs, 8, 128), f32),
+            ((slabs, 2, 128), f32),
         ],
-        (place, second_pre, from_below(high), from_above(low), swap(stats, "gz"), cot_planes),
+        (second_pre, from_below(high), from_above(low), swap(stats, "gz"), cot_planes),
+        [pltpu.VMEM((16, 16, SLAB), bf16), pltpu.SemaphoreType.DMA((1,))],
+        far=(4,),
+        near=(0,),
+        near_outs=(1, 2),
     )
     low, high, slope_one, sums, second_grad = call(
         second_back_kernel,
         [
-            ((128, FINE), bf16), ((128, FINE), bf16), ((128, SLAB), f32), ((slabs, 8, 128), f32),
+            ((128, FINE), bf16), ((128, FINE), bf16), ((128, SLAB), f32), ((slabs, 2, 128), f32),
             ((216, 128), f32),
         ],
-        (place, normed, slope, inverse, swap(sums, "gz"), packed, kernels),
+        (
+            normed, slope, inverse, swap(sums, "gz"), packed, backward,
+        ),
         [
-            unfolded, pltpu.VMEM((128, 3456), bf16), pltpu.VMEM((128, SLAB), bf16),
-            pltpu.VMEM((3, 128, 128), f32), pltpu.VMEM((216, SLAB), f32),
+            unfolded, pltpu.VMEM((128, SLAB), f32), pltpu.VMEM((3, 128, 128), f32),
+            pltpu.VMEM((128, 3456), bf16), pltpu.VMEM((144, HALOED), bf16), pltpu.SemaphoreType.DMA((1,)),
         ],
-        16,
+        15,
+        far=(5,),
+        near=(0, 1),
+        near_outs=(0, 1, 2, 4),
     )
     skip_grad, coarse_own, coarse_next, weight_grads = call(
         first_back_kernel,
         [((8, SLAB), bf16), ((16, COARSE), f32), ((16, COARSE), f32), ((GRAD_ROWS, 128), bf16)],
         (
-            place, slope_one, from_below(high), from_above(low), swap(sums, "gz"), packed, kernels,
-            skip_first, up_own, pair, joined, second_grad,
+            slope_one, from_below(high), from_above(low), swap(sums, "gz"), packed, first,
+            up_own, pair, joined, second_grad,
         ),
         [
-            unfolded, pltpu.VMEM((144, 3456), bf16), pltpu.VMEM((128, SLAB), bf16),
-            pltpu.VMEM((3, 128, 128), f32), pltpu.VMEM((432, SLAB), bf16),
+            unfolded, pltpu.VMEM((128, SLAB), f32), pltpu.VMEM((3, 128, 128), f32),
             pltpu.VMEM((1152, 2 * COARSE), bf16), pltpu.VMEM((16, 3456), bf16),
+            pltpu.VMEM((144, 3456), bf16), pltpu.VMEM((144, HALOED), bf16), pltpu.SemaphoreType.DMA((1,)),
         ],
-        20,
+        17,
+        far=(5,),
+        near=(0, 8, 9),
     )
     coarse_grad = (coarse_own + from_below(coarse_next)).astype(bf16)
     rows = GRAD_ROWS // slabs
     (spread,) = call(
         grad_sum_kernel,
         [((slabs, rows, 128), bf16)],
-        (place, swap(weight_grads.reshape(slabs, rows, 128), "gz")),
+        (swap(weight_grads.reshape(slabs, rows, 128), "gz"),),
     )
     grads = call(
         grad_split_kernel,
         [((27, 16, 128), f32), ((27, 8, 128), f32), ((27, 8, 128), f32), ((27, 8, 128), f32)],
-        (place, swap(spread, "gz")),
+        (swap(spread, "gz"),),
     )
     grads = [jnp.transpose(grad, (0, 2, 1)) for grad in grads]
     return (

time: 246 us -> 225 us (0.915)
  local copies, waits for them, and re-layouts: 14.1 us -> 5.32 us
  Pallas kernels: 28.1 us -> 24.7 us
  blocking collectives: 79.7 us -> 77.2 us
    unnamed x53 -> x15, local copies, waits for them, and re-layouts: 12.9 us -> 4.11 us
    all_to_all x5 -> x4, waiting for transfers between devices: 39.1 us -> 45.5 us  [swap(): return lax.all_to_all(block, axis, 0, 0, tiled=True)]
    ppermute x3, waiting for transfers between devices: 6.01 us -> 0.02 us  [from_above(): return lax.ppermute(block, 'gz', downward)]
    pallas_call x11 -> x12, Pallas kernels: 28.1 us -> 24.7 us  [call(): pl.pallas_call(kernel, out_shape=[out(index, *shape) for index, shape in...]
    all_to_all x4 -> x5, blocking collectives: 79.7 us -> 77.2 us  [swap(): return lax.all_to_all(block, axis, 0, 0, tiled=True)]
    all_to_all x5 -> x4, starting transfers between devices: 31.4 us -> 29.6 us  [swap(): return lax.all_to_all(block, axis, 0, 0, tiled=True)]
  transfers between devices with their start and end apart: 14 -> 13, of which waited for: 10 -> 5; matrix products, arithmetic and copies ran while one was open for 2% -> 2% of each run, Pallas kernels for 5% -> 4%
where the time goes in v3:
time: 225 us; the launch traced here: 224 us
  blocking collectives  77.2 us (34%)
  starting transfers between devices  53.7 us (24%)
  waiting for transfers between devices  48 us (21%)
  Pallas kernels  24.7 us (11%)
  between operations  14.3 us (6%)
  local copies, waits for them, and re-layouts  5.32 us (2%)
    all_to_all x5, blocking collectives, swap(): return lax.all_to_all(block, axis, 0, 0, tiled=True)  77.2 us
    all_to_all x4, waiting for transfers between devices, swap(): return lax.all_to_all(block, axis, 0, 0, tiled=True)  45.5 us
    all_to_all x4, starting transfers between devices, swap(): return lax.all_to_all(block, axis, 0, 0, tiled=True)  29.6 us
    pallas_call x12, Pallas kernels, call(): pl.pallas_call(kernel, out_shape=[out(index, *shape) for index, shape in...  24.7 us
    ppermute x3, starting transfers between devices, from_above(): return lax.ppermute(block, 'gz', downward)  12.4 us
    ppermute x4, starting transfers between devices, from_below(): return lax.ppermute(block, 'gz', upward)  11.7 us
  transfers between devices with their start and end apart: 13, of which 5 were waited for; matrix products, arithmetic and copies ran while one was open for 2% of the time, Pallas kernels for 4%

profile of v3, /device:TPU:8, one launch (start us, length us, event | category | flops | bytes accessed | tf_op | source)
XLA Modules:
  0.0 224.4 jit_solution(12668889108057913668)
XLA Ops:
  7.2 0.0 copy-start.4
  7.2 0.0 copy-start.5
  7.2 0.0 copy-start.2
  7.2 0.0 all-gather.5.cloned.1.call-start
  7.2 0.8 shard_map.126
  8.1 3.5 %collective-permute-start = (bf16[8,1280]{1,0:T(8,128)(2,1)S(1)}, bf16[8,1280]{1,0:T(8,128)(2,1)S(1)}, u32[]{:S(2)}, u32[]{:S(2)}) collective-permute-start(bf16[8,1280]{1,0:T(8,128)(2,1)S(1)} %get-tuple-element.48), channel_id=1, source_target_pairs={{0,16},{16,32},{32,48},{48,64},{64,80},{80,96},{96,112},{112,128},... | collective-permute-start | bytes 61448 | tf_op jit(solution)/shard_map/ppermute | solution.py:528
  11.5 5.5 %collective-permute-start.1 = (bf16[8,1280]{1,0:T(8,128)(2,1)S(1)}, bf16[8,1280]{1,0:T(8,128)(2,1)S(1)}, u32[]{:S(2)}, u32[]{:S(2)}) collective-permute-start(bf16[8,1280]{1,0:T(8,128)(2,1)S(1)} %get-tuple-element.49), channel_id=1, source_target_pairs={{16,0},{32,16},{48,32},{64,48},{80,64},{96,80},{112,96},{128,112},... | collective-permute-start | bytes 61448 | tf_op jit(solution)/shard_map/ppermute | solution.py:531
  17.1 1.4 copy.22
  18.5 0.0 copy-start.3
  18.5 0.9 copy.23
  19.4 0.3 copy.24.pieces
  19.7 0.0 collective-permute-done.low
  19.7 0.0 collective-permute-done.1.high
  19.7 0.0 copy-done.4
  19.7 0.7 shard_map.127
  20.4 0.0 copy-done.5
  20.4 0.0 copy-done.2
  20.4 0.7 pad_maximum_fusion
  21.1 0.0 all-gather.5.cloned.1.call-update
  21.1 12.3 %all_to_all.45.mixed = bf16[16,16,640]{2,1,0:T(8,128)(2,1)S(1)} all-to-all(bf16[16,16,640]{2,1,0:T(8,128)(2,1)S(1)} %get-tuple-element.52), channel_id=1, replica_groups=mesh['gz'=32,'ch'=16] {'ch'}, dimensions={0} | all-to-all | bytes 655360 | tf_op jit(solution)/shard_map/all_to_all | solution.py:534
  33.4 0.0 copy-done.3
  33.4 1.2 shard_map.128
  34.5 12.8 %all_to_all.46.parts = bf16[16,16,640]{2,1,0:T(8,128)(2,1)S(1)} all-to-all(bf16[16,16,640]{2,1,0:T(8,128)(2,1)S(1)} %get-tuple-element.54), channel_id=1, replica_groups=mesh['gz'=32,'ch'=16] {'ch'}, dimensions={0} | all-to-all | bytes 655360 | tf_op jit(solution)/shard_map/all_to_all | solution.py:534
  47.4 1.3 shard_map.129
  48.7 15.8 %all-to-all-start.2 = ((bf16[32,16,384]{2,1,0:T(8,128)(2,1)}), bf16[32,16,384]{2,1,0:T(8,128)(2,1)S(1)}, u32[]{:S(2)}, u32[]{:S(2)}) async-start(bf16[32,16,384]{2,1,0:T(8,128)(2,1)} %get-tuple-element.56), calls=%async_computation.2 | async-start | bytes 786432 | tf_op jit(solution)/shard_map/all_to_all | solution.py:534
  64.5 0.0 all-gather.7.cloned.1.call-start
  64.6 0.7 all-gather.7.cloned.1.call-update
  65.3 16.7 %all-to-all-done.2.stats = bf16[32,16,384]{2,1,0:T(8,128)(2,1)S(1)} async-done(((bf16[32,16,384]{2,1,0:T(8,128)(2,1)}), bf16[32,16,384]{2,1,0:T(8,128)(2,1)S(1)}, u32[]{:S(2)}, u32[]{:S(2)}) %all-to-all-start.2) | async-done | bytes 393248 | tf_op jit(solution)/shard_map/all_to_all | solution.py:534
  82.0 1.0 shard_map.130
  83.0 0.0 all-gather.5.cloned.1.call-done
  83.0 3.6 %all-to-all-start.3 = ((bf16[16,16,1152]{2,1,0:T(8,128)(2,1)}), bf16[16,16,1152]{2,1,0:T(8,128)(2,1)S(1)}, u32[]{:S(2)}, u32[]{:S(2)}) async-start(bf16[16,16,1152]{2,1,0:T(8,128)(2,1)} %shard_map.130), calls=%async_computation.3 | async-start | bytes 1179648 | tf_op jit(solution)/shard_map/all_to_all | solution.py:534
  86.6 0.0 copy-start
  86.6 1.5 copy-done
  88.1 1.5 shard_map.131
  89.6 10.3 %all-to-all-done.3.packed = bf16[16,16,1152]{2,1,0:T(8,128)(2,1)S(1)} async-done(((bf16[16,16,1152]{2,1,0:T(8,128)(2,1)}), bf16[16,16,1152]{2,1,0:T(8,128)(2,1)S(1)}, u32[]{:S(2)}, u32[]{:S(2)}) %all-to-all-start.3) | async-done | bytes 589856 | tf_op jit(solution)/shard_map/all_to_all | solution.py:534
  99.9 4.5 %shard_map.132 = (f32[128,1024]{1,0:T(8,128)S(1)}, bf16[128,512]{1,0:T(8,128)(2,1)S(1)}, bf16[128,512]{1,0:T(8,128)(2,1)S(1)}, f32[32,2,128]{2,1,0:T(2,128)}) custom-call(bf16[16,16,1152]{2,1,0:T(8,128)(2,1)S(1)} %all-to-all-done.3.packed, bf16[128,3456]{1,0:T(8,128)(2,1)S(1)} %get-tuple-element.61.matrix), custom_call_target="tpu_custom_call" | custom-call | tf_op jit(solution)/shard_map/pallas_call | solution.py:96
  104.4 2.3 %collective-permute-start.2 = (bf16[128,512]{1,0:T(8,128)(2,1)S(1)}, bf16[128,512]{1,0:T(8,128)(2,1)S(1)}, u32[]{:S(2)}, u32[]{:S(2)}) collective-permute-start(bf16[128,512]{1,0:T(8,128)(2,1)S(1)} %get-tuple-element.63), channel_id=1, source_target_pairs={{0,16},{16,32},{32,48},{48,64},{64,80},{80,96},{96,112},{112,128},... | collective-permute-start | bytes 393224 | tf_op jit(solution)/shard_map/ppermute | solution.py:528
  106.7 3.5 %collective-permute-start.3 = (bf16[128,512]{1,0:T(8,128)(2,1)S(1)}, bf16[128,512]{1,0:T(8,128)(2,1)S(1)}, u32[]{:S(2)}, u32[]{:S(2)}) collective-permute-start(bf16[128,512]{1,0:T(8,128)(2,1)S(1)} %get-tuple-element.64), channel_id=1, source_target_pairs={{16,0},{32,16},{48,32},{64,48},{80,64},{96,80},{112,96},{128,112},... | collective-permute-start | bytes 393224 | tf_op jit(solution)/shard_map/ppermute | solution.py:531
  110.2 6.0 %all-to-all-start.4 = ((f32[32,2,128]{2,1,0:T(2,128)}), f32[32,2,128]{2,1,0:T(2,128)S(1)}, u32[]{:S(2)}, u32[]{:S(2)}) async-start(f32[32,2,128]{2,1,0:T(2,128)} %get-tuple-element.65), calls=%async_computation.4 | async-start | bytes 65536 | tf_op jit(solution)/shard_map/all_to_all | solution.py:534
  116.2 0.0 all-gather.7.cloned.1.call-done
  116.3 11.2 %all-to-all-done.4.stats = f32[32,2,128]{2,1,0:T(2,128)S(1)} async-done(((f32[32,2,128]{2,1,0:T(2,128)}), f32[32,2,128]{2,1,0:T(2,128)S(1)}, u32[]{:S(2)}, u32[]{:S(2)}) %all-to-all-start.4) | async-done | bytes 32800 | tf_op jit(solution)/shard_map/all_to_all | solution.py:534
  127.5 0.0 collective-permute-done.2.low
  127.5 0.0 collective-permute-done.3.high
  127.5 1.6 shard_map.133
  129.1 15.3 %all_to_all.47.sums_in = f32[32,2,128]{2,1,0:T(2,128)S(1)} all-to-all(f32[32,2,128]{2,1,0:T(2,128)S(1)} %get-tuple-element.71), channel_id=1, replica_groups=mesh['gz'=32,'ch'=16] {'gz'}, dimensions={0} | all-to-all | bytes 65536 | tf_op jit(solution)/shard_map/all_to_all | solution.py:534
  144.4 0.0 copy-start.1
  144.4 4.8 %shard_map.134 = (bf16[128,512]{1,0:T(8,128)(2,1)S(1)}, bf16[128,512]{1,0:T(8,128)(2,1)S(1)}, f32[128,1024]{1,0:T(8,128)S(1)}, f32[32,2,128]{2,1,0:T(2,128)S(1)}, f32[216,128]{1,0:T(8,128)S(1)}) custom-call(f32[128,2048]{1,0:T(8,128)S(1)} %get-tuple-element.68.normed, f32[128,2048]{1,0:T(8,128)S(1)} %get-tuple-element.69.slope, ...), custom_call_target="tpu_custom_call" | custom-call | tf_op jit(solution)/shard_map/pallas_call | solution.py:96
  149.2 2.5 %collective-permute-start.4 = (bf16[128,512]{1,0:T(8,128)(2,1)S(1)}, bf16[128,512]{1,0:T(8,128)(2,1)S(1)}, u32[]{:S(2)}, u32[]{:S(2)}) collective-permute-start(bf16[128,512]{1,0:T(8,128)(2,1)S(1)} %get-tuple-element.74), channel_id=1, source_target_pairs={{0,16},{16,32},{32,48},{48,64},{64,80},{80,96},{96,112},{112,128},... | collective-permute-start | bytes 393224 | tf_op jit(solution)/shard_map/ppermute | solution.py:528
  151.8 3.3 %collective-permute-start.5 = (bf16[128,512]{1,0:T(8,128)(2,1)S(1)}, bf16[128,512]{1,0:T(8,128)(2,1)S(1)}, u32[]{:S(2)}, u32[]{:S(2)}) collective-permute-start(bf16[128,512]{1,0:T(8,128)(2,1)S(1)} %get-tuple-element.75), channel_id=1, source_target_pairs={{16,0},{32,16},{48,32},{64,48},{80,64},{96,80},{112,96},{128,112},... | collective-permute-start | bytes 393224 | tf_op jit(solution)/shard_map/ppermute | solution.py:531
  155.1 18.7 %all_to_all.48.sums_in = f32[32,2,128]{2,1,0:T(2,128)S(1)} all-to-all(f32[32,2,128]{2,1,0:T(2,128)S(1)} %get-tuple-element.76), channel_id=1, replica_groups=mesh['gz'=32,'ch'=16] {'gz'}, dimensions={0} | all-to-all | bytes 65536 | tf_op jit(solution)/shard_map/all_to_all | solution.py:534
  173.8 0.0 collective-permute-done.4.low
  173.8 0.0 collective-permute-done.5.high
  173.8 0.0 copy-done.1
  173.8 5.6 %shard_map.135 = (bf16[8,1024]{1,0:T(8,128)(2,1)S(1)}, f32[16,128]{1,0:T(8,128)S(1)}, f32[16,128]{1,0:T(8,128)S(1)}, bf16[1280,128]{1,0:T(8,128)(2,1)S(1)}) custom-call(f32[128,1024]{1,0:T(8,128)S(1)} %get-tuple-element.73.slope, bf16[128,512]{1,0:T(8,128)(2,1)S(1)} %collective-permute-done.4.low, bf16[128,512]{1,0:T(8,128)(2,1)S(1)} %collective-permute-done.5.high, ...), custom_call_target="tpu_custom_call" | custom-call | tf_op jit(solution)/shard_map/pallas_call | solution.py:96
  179.4 18.2 %all_to_all.49.parts = bf16[32,40,128]{2,1,0:T(8,128)(2,1)S(1)} all-to-all(bf16[32,40,128]{2,1,0:T(8,128)(2,1)S(1)} %bitcast.22), channel_id=1, replica_groups=mesh['gz'=32,'ch'=16] {'gz'}, dimensions={0} | all-to-all | bytes 655360 | tf_op jit(solution)/shard_map/all_to_all | solution.py:534
  197.6 0.8 shard_map.136
  198.4 4.2 %all-to-all-start.8 = ((bf16[32,40,128]{2,1,0:T(8,128)(2,1)}), bf16[32,40,128]{2,1,0:T(8,128)(2,1)S(1)}, u32[]{:S(2)}, u32[]{:S(2)}) async-start(bf16[32,40,128]{2,1,0:T(8,128)(2,1)} %shard_map.136), calls=%async_computation.8 | async-start | bytes 655360 | tf_op jit(solution)/shard_map/all_to_all | solution.py:534
  202.5 3.4 %collective-permute-start.6 = (f32[16,128]{1,0:T(8,128)S(1)}, f32[16,128]{1,0:T(8,128)S(1)}, u32[]{:S(2)}, u32[]{:S(2)}) collective-permute-start(f32[16,128]{1,0:T(8,128)S(1)} %get-tuple-element.82), channel_id=1, source_target_pairs={{0,16},{16,32},{32,48},{48,64},{64,80},{80,96},{96,112},{112,128},... | collective-permute-start | bytes 24584 | tf_op jit(solution)/shard_map/ppermute | solution.py:528
  205.9 0.6 copy.25
  206.5 0.6 copy.26
  207.2 1.7 collective-permute-done.6
  208.8 0.6 fusion
  209.4 7.3 %all-to-all-done.8.gathered = bf16[32,40,128]{2,1,0:T(8,128)(2,1)S(1)} async-done(((bf16[32,40,128]{2,1,0:T(8,128)(2,1)}), bf16[32,40,128]{2,1,0:T(8,128)(2,1)S(1)}, u32[]{:S(2)}, u32[]{:S(2)}) %all-to-all-start.8) | async-done | bytes 327712 | tf_op jit(solution)/shard_map/all_to_all | solution.py:534
  216.7 0.8 shard_map.137
Async XLA Ops:
  7.2 12.6 %copy-start.4 = (bf16[16,1,128]{2,0,1:T(8,128)(2,1)S(1)}, bf16[16,1,128]{2,0,1:T(8,128)(2,1)}, u32[]{:S(2)}) copy-start(bf16[16,1,128]{2,0,1:T(8,128)(2,1)} %param.7) | copy-start | bytes 12292
  7.2 13.2 %copy-start.5 = (bf16[27,128,8]{1,2,0:T(8,128)(2,1)S(1)}, bf16[27,128,8]{1,2,0:T(8,128)(2,1)}, u32[]{:S(2)}) copy-start(bf16[27,128,8]{1,2,0:T(8,128)(2,1)} %param.12) | copy-start | bytes 165892
  7.2 13.2 %copy-start.2 = (bf16[27,128,8]{1,2,0:T(8,128)(2,1)S(1)}, bf16[27,128,8]{1,2,0:T(8,128)(2,1)}, u32[]{:S(2)}) copy-start(bf16[27,128,8]{1,2,0:T(8,128)(2,1)} %param.10) | copy-start | bytes 165892
  7.2 75.8 %all-gather.5.cloned.1.call-start = ((), (), s32[]{:S(2)}) async-start(), calls=%async_computation.9 | async-start | bytes 1880064 | tf_op jit(solution)/shard_map/all_gather | solution.py:562
  8.1 11.7 %collective-permute-start = (bf16[8,1280]{1,0:T(8,128)(2,1)S(1)}, bf16[8,1280]{1,0:T(8,128)(2,1)S(1)}, u32[]{:S(2)}, u32[]{:S(2)}) collective-permute-start(bf16[8,1280]{1,0:T(8,128)(2,1)S(1)} %get-tuple-element.48), channel_id=1, source_target_pairs={{0,16},{16,32},{32,48},{48,64},{64,80},{80,96},{96,112},{112,128},... | collective-permute-start | bytes 61448 | tf_op jit(solution)/shard_map/ppermute | solution.py:528
  11.5 8.2 %collective-permute-start.1 = (bf16[8,1280]{1,0:T(8,128)(2,1)S(1)}, bf16[8,1280]{1,0:T(8,128)(2,1)S(1)}, u32[]{:S(2)}, u32[]{:S(2)}) collective-permute-start(bf16[8,1280]{1,0:T(8,128)(2,1)S(1)} %get-tuple-element.49), channel_id=1, source_target_pairs={{16,0},{32,16},{48,32},{64,48},{80,64},{96,80},{112,96},{128,112},... | collective-permute-start | bytes 61448 | tf_op jit(solution)/shard_map/ppermute | solution.py:531
  18.5 14.9 %copy-start.3 = (bf16[27,128,8]{1,2,0:T(8,128)(2,1)S(1)}, bf16[27,128,8]{1,2,0:T(8,128)(2,1)}, u32[]{:S(2)}) copy-start(bf16[27,128,8]{1,2,0:T(8,128)(2,1)} %param.11) | copy-start | bytes 165892
  48.7 33.3 %all-to-all-start.2 = ((bf16[32,16,384]{2,1,0:T(8,128)(2,1)}), bf16[32,16,384]{2,1,0:T(8,128)(2,1)S(1)}, u32[]{:S(2)}, u32[]{:S(2)}) async-start(bf16[32,16,384]{2,1,0:T(8,128)(2,1)} %get-tuple-element.56), calls=%async_computation.2 | async-start | bytes 786432 | tf_op jit(solution)/shard_map/all_to_all | solution.py:534
  64.5 51.8 %all-gather.7.cloned.1.call-start = ((), (), s32[]{:S(2)}) async-start(), calls=%async_computation.10 | async-start | bytes 1114112 | tf_op jit(solution)/shard_map/all_gather | solution.py:563
  83.0 16.9 %all-to-all-start.3 = ((bf16[16,16,1152]{2,1,0:T(8,128)(2,1)}), bf16[16,16,1152]{2,1,0:T(8,128)(2,1)S(1)}, u32[]{:S(2)}, u32[]{:S(2)}) async-start(bf16[16,16,1152]{2,1,0:T(8,128)(2,1)} %shard_map.130), calls=%async_computation.3 | async-start | bytes 1179648 | tf_op jit(solution)/shard_map/all_to_all | solution.py:534
  86.6 1.5 copy-start
  104.4 23.1 %collective-permute-start.2 = (bf16[128,512]{1,0:T(8,128)(2,1)S(1)}, bf16[128,512]{1,0:T(8,128)(2,1)S(1)}, u32[]{:S(2)}, u32[]{:S(2)}) collective-permute-start(bf16[128,512]{1,0:T(8,128)(2,1)S(1)} %get-tuple-element.63), channel_id=1, source_target_pairs={{0,16},{16,32},{32,48},{48,64},{64,80},{80,96},{96,112},{112,128},... | collective-permute-start | bytes 393224 | tf_op jit(solution)/shard_map/ppermute | solution.py:528
  106.7 20.8 %collective-permute-start.3 = (bf16[128,512]{1,0:T(8,128)(2,1)S(1)}, bf16[128,512]{1,0:T(8,128)(2,1)S(1)}, u32[]{:S(2)}, u32[]{:S(2)}) collective-permute-start(bf16[128,512]{1,0:T(8,128)(2,1)S(1)} %get-tuple-element.64), channel_id=1, source_target_pairs={{16,0},{32,16},{48,32},{64,48},{80,64},{96,80},{112,96},{128,112},... | collective-permute-start | bytes 393224 | tf_op jit(solution)/shard_map/ppermute | solution.py:531
  110.2 17.2 %all-to-all-start.4 = ((f32[32,2,128]{2,1,0:T(2,128)}), f32[32,2,128]{2,1,0:T(2,128)S(1)}, u32[]{:S(2)}, u32[]{:S(2)}) async-start(f32[32,2,128]{2,1,0:T(2,128)} %get-tuple-element.65), calls=%async_computation.4 | async-start | bytes 65536 | tf_op jit(solution)/shard_map/all_to_all | solution.py:534
  144.4 29.4 %copy-start.1 = (bf16[27,128,16]{1,2,0:T(8,128)(2,1)S(1)}, bf16[27,128,16]{1,2,0:T(8,128)(2,1)}, u32[]{:S(2)}) copy-start(bf16[27,128,16]{1,2,0:T(8,128)(2,1)} %param.9) | copy-start | bytes 331780
  149.2 24.5 %collective-permute-start.4 = (bf16[128,512]{1,0:T(8,128)(2,1)S(1)}, bf16[128,512]{1,0:T(8,128)(2,1)S(1)}, u32[]{:S(2)}, u32[]{:S(2)}) collective-permute-start(bf16[128,512]{1,0:T(8,128)(2,1)S(1)} %get-tuple-element.74), channel_id=1, source_target_pairs={{0,16},{16,32},{32,48},{48,64},{64,80},{80,96},{96,112},{112,128},... | collective-permute-start | bytes 393224 | tf_op jit(solution)/shard_map/ppermute | solution.py:528
  151.8 22.0 %collective-permute-start.5 = (bf16[128,512]{1,0:T(8,128)(2,1)S(1)}, bf16[128,512]{1,0:T(8,128)(2,1)S(1)}, u32[]{:S(2)}, u32[]{:S(2)}) collective-permute-start(bf16[128,512]{1,0:T(8,128)(2,1)S(1)} %get-tuple-element.75), channel_id=1, source_target_pairs={{16,0},{32,16},{48,32},{64,48},{80,64},{96,80},{112,96},{128,112},... | collective-permute-start | bytes 393224 | tf_op jit(solution)/shard_map/ppermute | solution.py:531
  198.4 18.4 %all-to-all-start.8 = ((bf16[32,40,128]{2,1,0:T(8,128)(2,1)}), bf16[32,40,128]{2,1,0:T(8,128)(2,1)S(1)}, u32[]{:S(2)}, u32[]{:S(2)}) async-start(bf16[32,40,128]{2,1,0:T(8,128)(2,1)} %shard_map.136), calls=%async_computation.8 | async-start | bytes 655360 | tf_op jit(solution)/shard_map/all_to_all | solution.py:534
  202.5 6.3 %collective-permute-start.6 = (f32[16,128]{1,0:T(8,128)S(1)}, f32[16,128]{1,0:T(8,128)S(1)}, u32[]{:S(2)}, u32[]{:S(2)}) collective-permute-start(f32[16,128]{1,0:T(8,128)S(1)} %get-tuple-element.82), channel_id=1, source_target_pairs={{0,16},{16,32},{32,48},{48,64},{64,80},{80,96},{96,112},{112,128},... | collective-permute-start | bytes 24584 | tf_op jit(solution)/shard_map/ppermute | solution.py:528
Sparse Core Ops, SparseCore 0:
  21.2 44.3 all-gather.4
  68.3 46.2 all-gather.6

commit v4 on v3

--- a/solution.py
+++ b/solution.py
@@ -14,6 +14,7 @@
 FINE = 4 * COARSE
 SLAB = 2 * FINE
 HALOED = 4 * FINE
+WIDE = 6 * FINE
 LEAK_SLOPE = 0.01
 KINK_WIDTH = 0.01
 NORM_EPS = 1e-05
@@ -64,9 +65,9 @@
     return jnp.where(source == other, 1.0, 0.0).astype(bf16)
 
 
-def edge_mask(slab, slabs):
-    plane = lax.broadcasted_iota(jnp.int32, (1, HALOED), 1) // FINE
-    outside = ((plane == 0) & (slab == 0)) | ((plane == 3) & (slab == slabs - 1))
+def edge_mask(slab, slabs, width):
+    plane = lax.broadcasted_iota(jnp.int32, (1, SLAB + 2 * width * FINE), 1) // FINE
+    outside = ((plane < width) & (slab == 0)) | ((plane > width + 1) & (slab == slabs - 1))
     return jnp.where(outside, 0.0, 1.0)
 
 
@@ -120,12 +121,11 @@
     cells = coarse[...].astype(f32)
     cells = [cells[:8], cells[8:]]
     skip_planes, cot_planes = skip[...].astype(f32), cotangent[...].astype(f32)
-    last = cells + [skip_planes[:, 1], cot_planes[:, 1]]
-    first = cells + [skip_planes[:, 0], cot_planes[:, 0]]
-    upward[...] = jnp.concatenate(last, axis=1).astype(bf16)
-    downward[...] = jnp.concatenate(first, axis=1).astype(bf16)
+    both = [cot_planes[:, 0], cot_planes[:, 1]]
+    upward[...] = jnp.concatenate(cells + [skip_planes[:, 1]] + both, axis=1).astype(bf16)
+    downward[...] = jnp.concatenate(cells + [skip_planes[:, 0]] + both, axis=1).astype(bf16)
     own_skip[...] = jnp.concatenate([skip_planes[:, 0], skip_planes[:, 1]], axis=1).astype(bf16)
-    own_cot[...] = jnp.concatenate([cot_planes[:, 0], cot_planes[:, 1]], axis=1).astype(bf16)
+    own_cot[...] = jnp.concatenate(both, axis=1).astype(bf16)
 
 
 def mix_kernel(pieces, coarse, low, high, own_cot, mixed, pair, cot_planes):
@@ -141,10 +141,9 @@
     pair[0] = coarse[...]
     pair[1] = after.astype(bf16)
     cot = own_cot[...].astype(f32)
-    lower = jnp.concatenate([below[:, 2 * COARSE + FINE :], cot[:, :FINE]], axis=1)
-    upper = jnp.concatenate([cot[:, FINE:], above[:, 2 * COARSE + FINE :]], axis=1)
-    cot_planes[0:16] = jnp.concatenate([lower, upper], axis=0).astype(bf16)
-    cot_planes[16:32] = jnp.zeros((16, SLAB), bf16)
+    at = 2 * COARSE + FINE
+    slabs = [below[:, at:], cot, above[:, at:], jnp.zeros((8, SLAB), f32)]
+    cot_planes[...] = jnp.concatenate(slabs, axis=0).astype(bf16)
 
 
 def up_kernel(mixed, own_skip, low, high, first_up, first_skip, partial, joined, unfolded):
@@ -304,9 +303,9 @@
 
 
 def second_conv_kernel(
-    packed, matrix, pre, low, high, stats, unfolded
+    packed, matrix, pre, halo, stats, unfolded
 ):
-    mask = edge_mask(lax.axis_index("gz"), stats.shape[0])
+    mask = edge_mask(lax.axis_index("gz"), stats.shape[0], 1)
 
     def prepare(block, carry):
         hidden = activate(read_planes(packed, block)).astype(bf16).astype(f32) * mask
@@ -325,8 +324,7 @@
     mean = jnp.sum(total, axis=1, keepdims=True) / SLAB
     deviation = total - mean
     square = jnp.sum(deviation * deviation, axis=1, keepdims=True)
-    low[...] = deviation[:, :FINE].astype(bf16)
-    high[...] = deviation[:, FINE:].astype(bf16)
+    halo[...] = deviation.astype(bf16)
     row = lax.broadcasted_iota(jnp.int32, (2, 128), 0)
     tile = jnp.where(row < 1, as_row(mean), as_row(square))
     stats[...] = jnp.broadcast_to(tile[None], stats.shape)
@@ -335,7 +333,7 @@
 def second_norm_kernel(
     pre, low, high, stats, far_cot, decoded, normed, slope, inverse_out, sums, cotangent, semaphores
 ):
-    (fetch,) = copies((far_cot.at[:, pl.ds(0, 16)],), (cotangent,), semaphores)
+    (fetch,) = copies((far_cot,), (cotangent,), semaphores)
     slab, share = lax.axis_index("gz"), lax.axis_index("ch")
     slabs = stats.shape[0]
     gathered = stats[...]
@@ -348,22 +346,24 @@
     below = stats[jnp.maximum(slab - 1, 0)][0:1] - mean_row
     above = stats[jnp.minimum(slab + 1, slabs - 1)][0:1] - mean_row
     mean, inverse = as_column(mean_row), as_column(inverse_row)
-    normed[:, :FINE] = (low[...].astype(f32) + as_column(below)) * inverse
-    normed[:, 3 * FINE :] = (high[...].astype(f32) + as_column(above)) * inverse
-    normed[:, FINE : 3 * FINE] = (pre[...] - mean) * inverse
-    own = normed[pl.ds(pl.multiple_of(share * 8, 8), 8), FINE : 3 * FINE]
+    normed[:, :SLAB] = (low[...].astype(f32) + as_column(below)) * inverse
+    normed[:, SLAB : 2 * SLAB] = (pre[...] - mean) * inverse
+    normed[:, 2 * SLAB :] = (high[...].astype(f32) + as_column(above)) * inverse
+    own = normed[pl.ds(pl.multiple_of(share * 8, 8), 8), SLAB : 2 * SLAB]
     decoded[...] = activate(own).astype(bf16)
 
     def prepare(block, carry):
         at = pl.ds(pl.multiple_of(block * 16, 16), 16)
-        slope[at, :] = read_planes(cotangent, block) * activate_slope(normed[at, :])
+        pair = cotangent[pl.ds(2 * block, 2)].astype(f32)
+        planes = [pair[:, row : row + 8].reshape(16, SLAB) for row in (0, 8, 16)]
+        slope[at, :] = jnp.concatenate(planes, axis=1) * activate_slope(normed[at, :])
         return carry
 
     fetch.wait()
     lax.fori_loop(0, 8, prepare, 0)
-    inner = slope[:, FINE : 3 * FINE]
+    inner = slope[:, SLAB : 2 * SLAB]
     one = as_row(jnp.sum(inner, axis=1, keepdims=True))
-    two = as_row(jnp.sum(inner * normed[:, FINE : 3 * FINE], axis=1, keepdims=True))
+    two = as_row(jnp.sum(inner * normed[:, SLAB : 2 * SLAB], axis=1, keepdims=True))
     row = lax.broadcasted_iota(jnp.int32, (2, 128), 0)
     sums[...] = jnp.broadcast_to(jnp.where(row < 1, one, two)[None], sums.shape)
 
@@ -375,12 +375,12 @@
 
 def second_back_kernel(
     normed, slope, inverse_row, sums_in, packed, far_matrix,
-    low, high, slope_one, sums, weight_grad,
+    slope_one, sums, weight_grad,
     unfolded, grads, columns, matrix, own_unfolded, semaphores,
 ):
     (fetch,) = copies((far_matrix,), (matrix,), semaphores)
     slab, share = lax.axis_index("gz"), lax.axis_index("ch")
-    mask = edge_mask(slab, sums.shape[0])
+    mask = edge_mask(slab, sums.shape[0], 2)
     mean_grad, mean_cross = total_means(sums_in)
     columns[0] = jnp.broadcast_to(mean_grad, (C_OUT, 128))
     columns[1] = jnp.broadcast_to(mean_cross, (C_OUT, 128))
@@ -390,32 +390,32 @@
         at = pl.ds(pl.multiple_of(block * 16, 16), 16)
         grad = columns[2, at, :1] * (slope[at, :] - columns[0, at, :1] - normed[at, :] * columns[1, at, :1])
         grad = grad.astype(bf16).astype(f32) * mask
-        grads[at, :] = grad[:, FINE : 3 * FINE]
+        grads[at, :] = grad[:, SLAB : 2 * SLAB]
         unfold_block(grad, unfolded, block, -1)
         return carry
 
     lax.fori_loop(0, 8, prepare, 0)
     fetch.wait()
-    total = jnp.zeros((C_OUT, SLAB), f32)
+    total = jnp.zeros((C_OUT, HALOED), f32)
     for k_z in range(3):
         total = total + jnp.dot(
             matrix[:, k_z * 1152 : k_z * 1152 + 1152],
-            unfolded[:, :, (2 - k_z) * FINE : (2 - k_z) * FINE + SLAB].reshape(1152, SLAB),
+            unfolded[:, :, (2 - k_z) * FINE : (2 - k_z) * FINE + HALOED].reshape(1152, HALOED),
             preferred_element_type=f32,
         )
-    low[...] = total[:, :FINE].astype(bf16)
-    high[...] = total[:, FINE:].astype(bf16)
     both = packed[:, :, :SLAB].astype(f32)
     first_normed = jnp.concatenate(
-        [both[:, :8, FINE:].reshape(C_OUT, FINE), both[:, 8:, :FINE].reshape(C_OUT, FINE)], axis=1
-    )
-    inner = total * activate_slope(first_normed)
-    slope_one[...] = inner
+        [both[:, :8].reshape(C_OUT, SLAB), both[:, 8:].reshape(C_OUT, SLAB)], axis=1
+    )
+    whole = total * activate_slope(first_normed)
+    slope_one[...] = whole
+    inner = whole[:, FINE : 3 * FINE]
     one = as_row(jnp.sum(inner, axis=1, keepdims=True))
-    two = as_row(jnp.sum(inner * first_normed, axis=1, keepdims=True))
+    two = as_row(jnp.sum(inner * first_normed[:, FINE : 3 * FINE], axis=1, keepdims=True))
     row = lax.broadcasted_iota(jnp.int32, (2, 128), 0)
     sums[...] = jnp.broadcast_to(jnp.where(row < 1, one, two)[None], sums.shape)
-    own = activate(read_planes(packed, share // 2)).astype(bf16).astype(f32) * mask
+    own = activate(read_planes(packed, share // 2)).astype(bf16).astype(f32)
+    own = own * edge_mask(slab, sums.shape[0], 1)
     for tap in range(9):
         own_unfolded[tap * 16 : tap * 16 + 16, :] = fine_shift(own, tap // 3 - 1, tap % 3 - 1).astype(bf16)
     odd = share % 2 == 1
@@ -428,13 +428,13 @@
 
 
 def first_back_kernel(
-    slope, low, high, sums_in, packed, far_matrix, up_weight, coarse, joined, second_grad,
+    slope, sums_in, packed, far_matrix, up_weight, coarse, joined, second_grad,
     skip_grad, coarse_own, coarse_next, weight_grads,
     unfolded, grads, columns, spread, up_matrix, matrix, own_unfolded, semaphores,
 ):
     (fetch,) = copies((far_matrix,), (matrix,), semaphores)
     slab = lax.axis_index("gz")
-    mask = edge_mask(slab, sums_in.shape[0])
+    mask = edge_mask(slab, sums_in.shape[0], 1)
     mean_grad, mean_cross = total_means(sums_in)
     columns[0] = jnp.broadcast_to(mean_grad, (C_OUT, 128))
     columns[1] = jnp.broadcast_to(mean_cross, (C_OUT, 128))
@@ -444,10 +444,7 @@
     def prepare(block, carry):
         at = pl.ds(pl.multiple_of(block * 16, 16), 16)
         normed = read_planes(packed, block)
-        bottom = low[at, :].astype(f32) * activate_slope(normed[:, :FINE])
-        top = high[at, :].astype(f32) * activate_slope(normed[:, 3 * FINE :])
-        inner = jnp.concatenate([bottom, slope[at, :], top], axis=1)
-        grad = columns[2, at, :1] * (inner - columns[0, at, :1] - normed * columns[1, at, :1])
+        grad = columns[2, at, :1] * (slope[at, :] - columns[0, at, :1] - normed * columns[1, at, :1])
         grad = grad.astype(bf16).astype(f32) * mask
         grads[at, :] = grad[:, FINE : 3 * FINE]
         unfold_block(grad, unfolded, block, -1)
@@ -540,7 +537,7 @@
     skip_first, second_own = io_major(first_skip), io_major(second_weight)
 
     here = coarse.reshape(16, COARSE)
-    halo = ((8, 2 * COARSE + 2 * FINE), bf16)
+    halo = ((8, 2 * COARSE + 3 * FINE), bf16)
     upper, lower, own_skip, own_cot = call(
         halo_kernel,
         [halo, halo, ((8, SLAB), bf16), ((8, SLAB), bf16)],
@@ -588,52 +585,51 @@
         near_outs=(0,),
     )
     unfolded = pltpu.VMEM((9, 128, HALOED), bf16)
-    second_pre, low, high, stats = call(
+    second_pre, halo, stats = call(
         second_conv_kernel,
         [
-            ((128, SLAB), f32), ((128, FINE), bf16), ((128, FINE), bf16), ((slabs, 2, 128), f32),
+            ((128, SLAB), f32), ((128, SLAB), bf16), ((slabs, 2, 128), f32),
         ],
         (packed, forward),
         [unfolded],
         14,
         near=(1,),
-        near_outs=(0, 1, 2),
+        near_outs=(0, 1),
     )
     decoded, normed, slope, inverse, sums = call(
         second_norm_kernel,
         [
-            ((8, SLAB), bf16), ((128, HALOED), f32), ((128, HALOED), f32), ((8, 128), f32),
+            ((8, SLAB), bf16), ((128, WIDE), f32), ((128, WIDE), f32), ((8, 128), f32),
             ((slabs, 2, 128), f32),
         ],
-        (second_pre, from_below(high), from_above(low), swap(stats, "gz"), cot_planes),
-        [pltpu.VMEM((16, 16, SLAB), bf16), pltpu.SemaphoreType.DMA((1,))],
+        (second_pre, from_below(halo), from_above(halo), swap(stats, "gz"), cot_planes),
+        [pltpu.VMEM((16, 32, SLAB), bf16), pltpu.SemaphoreType.DMA((1,))],
         far=(4,),
         near=(0,),
         near_outs=(1, 2),
     )
-    low, high, slope_one, sums, second_grad = call(
+    slope_one, sums, second_grad = call(
         second_back_kernel,
         [
-            ((128, FINE), bf16), ((128, FINE), bf16), ((128, SLAB), f32), ((slabs, 2, 128), f32),
-            ((216, 128), f32),
+            ((128, HALOED), f32), ((slabs, 2, 128), f32), ((216, 128), f32),
         ],
         (
             normed, slope, inverse, swap(sums, "gz"), packed, backward,
         ),
         [
-            unfolded, pltpu.VMEM((128, SLAB), f32), pltpu.VMEM((3, 128, 128), f32),
+            pltpu.VMEM((9, 128, WIDE), bf16), pltpu.VMEM((128, SLAB), f32), pltpu.VMEM((3, 128, 128), f32),
             pltpu.VMEM((128, 3456), bf16), pltpu.VMEM((144, HALOED), bf16), pltpu.SemaphoreType.DMA((1,)),
         ],
-        15,
+        20,
         far=(5,),
         near=(0, 1),
-        near_outs=(0, 1, 2, 4),
+        near_outs=(0, 2),
     )
     skip_grad, coarse_own, coarse_next, weight_grads = call(
         first_back_kernel,
         [((8, SLAB), bf16), ((16, COARSE), f32), ((16, COARSE), f32), ((GRAD_ROWS, 128), bf16)],
         (
-            slope_one, from_below(high), from_above(low), swap(sums, "gz"), packed, first,
+            slope_one, swap(sums, "gz"), packed, first,
             up_own, pair, joined, second_grad,
         ),
         [
@@ -642,8 +638,8 @@
             pltpu.VMEM((144, 3456), bf16), pltpu.VMEM((144, HALOED), bf16), pltpu.SemaphoreType.DMA((1,)),
         ],
         17,
-        far=(5,),
-        near=(0, 8, 9),
+        far=(3,),
+        near=(0, 6, 7),
     )
     coarse_grad = (coarse_own + from_below(coarse_next)).astype(bf16)
     rows = GRAD_ROWS // slabs

time: 225 us -> 219 us (0.973)
  starting transfers between devices: 53.7 us -> 47.3 us
  Pallas kernels: 24.7 us -> 27 us
    ppermute x3 -> x2, starting transfers between devices: 12.4 us -> 7.58 us  [from_above(): return lax.ppermute(block, 'gz', downward)]
    pallas_call x12, Pallas kernels: 24.7 us -> 27 us  [call(): pl.pallas_call(kernel, out_shape=[out(index, *shape) for index, shape in...]
    ppermute x4 -> x3, starting transfers between devices: 11.7 us -> 10.7 us  [from_below(): return lax.ppermute(block, 'gz', upward)]
  transfers between devices with their start and end apart: 13 -> 11, of which waited for: 5 -> 5; matrix products, arithmetic and copies ran while one was open for 2% -> 2% of each run, Pallas kernels for 4% -> 4%
where the time goes in v4:
time: 219 us; the launch traced here: 218 us
  blocking collectives  75 us (34%)
  waiting for transfers between devices  48 us (22%)
  starting transfers between devices  47.3 us (22%)
  Pallas kernels  27 us (12%)
  between operations  14.2 us (6%)
  local copies, waits for them, and re-layouts  5.33 us (2%)
    all_to_all x5, blocking collectives, swap(): return lax.all_to_all(block, axis, 0, 0, tiled=True)  75 us
    all_to_all x4, waiting for transfers between devices, swap(): return lax.all_to_all(block, axis, 0, 0, tiled=True)  45.6 us
    all_to_all x4, starting transfers between devices, swap(): return lax.all_to_all(block, axis, 0, 0, tiled=True)  29 us
    pallas_call x12, Pallas kernels, call(): pl.pallas_call(kernel, out_shape=[out(index, *shape) for index, shape in...  27 us
    ppermute x3, starting transfers between devices, from_below(): return lax.ppermute(block, 'gz', upward)  10.7 us
    ppermute x2, starting transfers between devices, from_above(): return lax.ppermute(block, 'gz', downward)  7.58 us
  transfers between devices with their start and end apart: 11, of which 5 were waited for; matrix products, arithmetic and copies ran while one was open for 2% of the time, Pallas kernels for 4%

profile of v4, /device:TPU:8, one launch (start us, length us, event | category | flops | bytes accessed | tf_op | source)
XLA Modules:
  0.0 218.2 jit_solution(1626714857492941270)
XLA Ops:
  7.2 0.0 copy-start.4
  7.2 0.0 all-gather.5.cloned.1.call-start
  7.2 0.8 shard_map.126
  8.0 3.5 %collective-permute-start = (bf16[8,1792]{1,0:T(8,128)(2,1)S(1)}, bf16[8,1792]{1,0:T(8,128)(2,1)S(1)}, u32[]{:S(2)}, u32[]{:S(2)}) collective-permute-start(bf16[8,1792]{1,0:T(8,128)(2,1)S(1)} %get-tuple-element.45), channel_id=1, source_target_pairs={{0,16},{16,32},{32,48},{48,64},{64,80},{80,96},{96,112},{112,128},... | collective-permute-start | bytes 86024 | tf_op jit(solution)/shard_map/ppermute | solution.py:525
  11.5 0.0 copy-start.2
  11.5 0.0 copy-start.5
  11.6 5.7 %collective-permute-start.1 = (bf16[8,1792]{1,0:T(8,128)(2,1)S(1)}, bf16[8,1792]{1,0:T(8,128)(2,1)S(1)}, u32[]{:S(2)}, u32[]{:S(2)}) collective-permute-start(bf16[8,1792]{1,0:T(8,128)(2,1)S(1)} %get-tuple-element.46), channel_id=1, source_target_pairs={{16,0},{32,16},{48,32},{64,48},{80,64},{96,80},{112,96},{128,112},... | collective-permute-start | bytes 86024 | tf_op jit(solution)/shard_map/ppermute | solution.py:528
  17.2 1.4 copy.22
  18.6 0.0 copy-start.3
  18.6 0.9 copy.23
  19.5 0.3 copy.24.pieces
  19.8 0.0 collective-permute-done.low
  19.9 0.0 collective-permute-done.1.high
  19.9 0.0 copy-done.4
  19.9 0.7 shard_map.127
  20.6 0.0 copy-done.2
  20.6 0.0 copy-done.5
  20.6 0.7 pad_maximum_fusion
  21.2 0.0 all-gather.5.cloned.1.call-update
  21.2 12.3 %all_to_all.45.mixed = bf16[16,16,640]{2,1,0:T(8,128)(2,1)S(1)} all-to-all(bf16[16,16,640]{2,1,0:T(8,128)(2,1)S(1)} %get-tuple-element.49), channel_id=1, replica_groups=mesh['gz'=32,'ch'=16] {'ch'}, dimensions={0} | all-to-all | bytes 655360 | tf_op jit(solution)/shard_map/all_to_all | solution.py:531
  33.6 0.0 copy-done.3
  33.6 1.2 shard_map.128
  34.7 12.8 %all_to_all.46.parts = bf16[16,16,640]{2,1,0:T(8,128)(2,1)S(1)} all-to-all(bf16[16,16,640]{2,1,0:T(8,128)(2,1)S(1)} %get-tuple-element.51), channel_id=1, replica_groups=mesh['gz'=32,'ch'=16] {'ch'}, dimensions={0} | all-to-all | bytes 655360 | tf_op jit(solution)/shard_map/all_to_all | solution.py:531
  47.6 1.3 shard_map.129
  48.9 15.8 %all-to-all-start.2 = ((bf16[32,16,384]{2,1,0:T(8,128)(2,1)}), bf16[32,16,384]{2,1,0:T(8,128)(2,1)S(1)}, u32[]{:S(2)}, u32[]{:S(2)}) async-start(bf16[32,16,384]{2,1,0:T(8,128)(2,1)} %get-tuple-element.53), calls=%async_computation.2 | async-start | bytes 786432 | tf_op jit(solution)/shard_map/all_to_all | solution.py:531
  64.7 0.0 all-gather.7.cloned.1.call-start
  64.7 0.7 all-gather.7.cloned.1.call-update
  65.4 16.6 %all-to-all-done.2.stats = bf16[32,16,384]{2,1,0:T(8,128)(2,1)S(1)} async-done(((bf16[32,16,384]{2,1,0:T(8,128)(2,1)}), bf16[32,16,384]{2,1,0:T(8,128)(2,1)S(1)}, u32[]{:S(2)}, u32[]{:S(2)}) %all-to-all-start.2) | async-done | bytes 393248 | tf_op jit(solution)/shard_map/all_to_all | solution.py:531
  82.0 1.0 shard_map.130
  83.1 0.0 all-gather.5.cloned.1.call-done
  83.1 3.6 %all-to-all-start.3 = ((bf16[16,16,1152]{2,1,0:T(8,128)(2,1)}), bf16[16,16,1152]{2,1,0:T(8,128)(2,1)S(1)}, u32[]{:S(2)}, u32[]{:S(2)}) async-start(bf16[16,16,1152]{2,1,0:T(8,128)(2,1)} %shard_map.130), calls=%async_computation.3 | async-start | bytes 1179648 | tf_op jit(solution)/shard_map/all_to_all | solution.py:531
  86.6 0.0 copy-start
  86.7 1.5 copy-done
  88.1 1.5 shard_map.131
  89.6 10.3 %all-to-all-done.3.packed = bf16[16,16,1152]{2,1,0:T(8,128)(2,1)S(1)} async-done(((bf16[16,16,1152]{2,1,0:T(8,128)(2,1)}), bf16[16,16,1152]{2,1,0:T(8,128)(2,1)S(1)}, u32[]{:S(2)}, u32[]{:S(2)}) %all-to-all-start.3) | async-done | bytes 589856 | tf_op jit(solution)/shard_map/all_to_all | solution.py:531
  99.9 4.5 %shard_map.132 = (f32[128,1024]{1,0:T(8,128)S(1)}, bf16[128,1024]{1,0:T(8,128)(2,1)S(1)}, f32[32,2,128]{2,1,0:T(2,128)}) custom-call(bf16[16,16,1152]{2,1,0:T(8,128)(2,1)S(1)} %all-to-all-done.3.packed, bf16[128,3456]{1,0:T(8,128)(2,1)S(1)} %get-tuple-element.58.matrix), custom_call_target="tpu_custom_call" | custom-call | tf_op jit(solution)/shard_map/pallas_call | solution.py:97
  104.4 1.9 collective-permute-start.3
  106.3 3.9 %collective-permute-start.2 = (bf16[128,1024]{1,0:T(8,128)(2,1)S(1)}, bf16[128,1024]{1,0:T(8,128)(2,1)S(1)}, u32[]{:S(2)}, u32[]{:S(2)}) collective-permute-start(bf16[128,1024]{1,0:T(8,128)(2,1)S(1)} %get-tuple-element.60), channel_id=1, source_target_pairs={{0,16},{16,32},{32,48},{48,64},{64,80},{80,96},{96,112},{112,128},... | collective-permute-start | bytes 786440 | tf_op jit(solution)/shard_map/ppermute | solution.py:525
  110.2 6.0 %all-to-all-start.4 = ((f32[32,2,128]{2,1,0:T(2,128)}), f32[32,2,128]{2,1,0:T(2,128)S(1)}, u32[]{:S(2)}, u32[]{:S(2)}) async-start(f32[32,2,128]{2,1,0:T(2,128)} %get-tuple-element.61), calls=%async_computation.4 | async-start | bytes 65536 | tf_op jit(solution)/shard_map/all_to_all | solution.py:531
  116.2 0.0 all-gather.7.cloned.1.call-done
  116.2 11.2 %all-to-all-done.4.stats = f32[32,2,128]{2,1,0:T(2,128)S(1)} async-done(((f32[32,2,128]{2,1,0:T(2,128)}), f32[32,2,128]{2,1,0:T(2,128)S(1)}, u32[]{:S(2)}, u32[]{:S(2)}) %all-to-all-start.4) | async-done | bytes 32800 | tf_op jit(solution)/shard_map/all_to_all | solution.py:531
  127.4 0.0 collective-permute-done.3.high
  127.4 0.0 collective-permute-done.2.low
  127.4 1.9 shard_map.133
  129.3 16.1 %all_to_all.47.sums_in = f32[32,2,128]{2,1,0:T(2,128)S(1)} all-to-all(f32[32,2,128]{2,1,0:T(2,128)S(1)} %get-tuple-element.67), channel_id=1, replica_groups=mesh['gz'=32,'ch'=16] {'gz'}, dimensions={0} | all-to-all | bytes 65536 | tf_op jit(solution)/shard_map/all_to_all | solution.py:531
  145.5 0.0 copy-start.1
  145.5 6.9 %shard_map.134 = (f32[128,2048]{1,0:T(8,128)S(1)}, f32[32,2,128]{2,1,0:T(2,128)S(1)}, f32[216,128]{1,0:T(8,128)S(1)}) custom-call(f32[128,3072]{1,0:T(8,128)S(1)} %get-tuple-element.64.normed, f32[128,3072]{1,0:T(8,128)S(1)} %get-tuple-element.65.slope, f32[8,128]{1,0:T(8,128)S(1)} %get-tuple-element.66.inverse_row, f32[32,2,128]{2,1,0:T(2,128)S(1)} %all_to_all.47.sums_in, ...), custom_call_target="tpu_custom_call" | custom-call | tf_op jit(solution)/shard_map/pallas_call | solution.py:97
  152.4 15.3 %all_to_all.48.sums_in = f32[32,2,128]{2,1,0:T(2,128)S(1)} all-to-all(f32[32,2,128]{2,1,0:T(2,128)S(1)} %get-tuple-element.70), channel_id=1, replica_groups=mesh['gz'=32,'ch'=16] {'gz'}, dimensions={0} | all-to-all | bytes 65536 | tf_op jit(solution)/shard_map/all_to_all | solution.py:531
  167.7 0.0 copy-done.1
  167.7 5.6 %shard_map.135 = (bf16[8,1024]{1,0:T(8,128)(2,1)S(1)}, f32[16,128]{1,0:T(8,128)S(1)}, f32[16,128]{1,0:T(8,128)S(1)}, bf16[1280,128]{1,0:T(8,128)(2,1)S(1)}) custom-call(f32[128,2048]{1,0:T(8,128)S(1)} %get-tuple-element.69.slope, f32[32,2,128]{2,1,0:T(2,128)S(1)} %all_to_all.48.sums_in, bf16[16,16,1152]{2,1,0:T(8,128)(2,1)S(1)} %all-to-all-done.3.packed, ...), custom_call_target="tpu_custom_call" | custom-call | tf_op jit(solution)/shard_map/pallas_call | solution.py:97
  173.3 18.4 %all_to_all.49.parts = bf16[32,40,128]{2,1,0:T(8,128)(2,1)S(1)} all-to-all(bf16[32,40,128]{2,1,0:T(8,128)(2,1)S(1)} %bitcast.22), channel_id=1, replica_groups=mesh['gz'=32,'ch'=16] {'gz'}, dimensions={0} | all-to-all | bytes 655360 | tf_op jit(solution)/shard_map/all_to_all | solution.py:531
  191.7 0.8 shard_map.136
  192.5 3.7 %all-to-all-start.8 = ((bf16[32,40,128]{2,1,0:T(8,128)(2,1)}), bf16[32,40,128]{2,1,0:T(8,128)(2,1)S(1)}, u32[]{:S(2)}, u32[]{:S(2)}) async-start(bf16[32,40,128]{2,1,0:T(8,128)(2,1)} %shard_map.136), calls=%async_computation.8 | async-start | bytes 655360 | tf_op jit(solution)/shard_map/all_to_all | solution.py:531
  196.2 3.3 %collective-permute-start.4 = (f32[16,128]{1,0:T(8,128)S(1)}, f32[16,128]{1,0:T(8,128)S(1)}, u32[]{:S(2)}, u32[]{:S(2)}) collective-permute-start(f32[16,128]{1,0:T(8,128)S(1)} %get-tuple-element.76), channel_id=1, source_target_pairs={{0,16},{16,32},{32,48},{48,64},{64,80},{80,96},{96,112},{112,128},... | collective-permute-start | bytes 24584 | tf_op jit(solution)/shard_map/ppermute | solution.py:525
  199.5 0.6 copy.25
  200.1 0.6 copy.26
  200.7 1.7 collective-permute-done.4
  202.4 0.6 fusion
  203.0 7.5 %all-to-all-done.8.gathered = bf16[32,40,128]{2,1,0:T(8,128)(2,1)S(1)} async-done(((bf16[32,40,128]{2,1,0:T(8,128)(2,1)}), bf16[32,40,128]{2,1,0:T(8,128)(2,1)S(1)}, u32[]{:S(2)}, u32[]{:S(2)}) %all-to-all-start.8) | async-done | bytes 327712 | tf_op jit(solution)/shard_map/all_to_all | solution.py:531
  210.5 0.8 shard_map.137
Async XLA Ops:
  7.2 12.7 %copy-start.4 = (bf16[16,1,128]{2,0,1:T(8,128)(2,1)S(1)}, bf16[16,1,128]{2,0,1:T(8,128)(2,1)}, u32[]{:S(2)}) copy-start(bf16[16,1,128]{2,0,1:T(8,128)(2,1)} %param.7) | copy-start | bytes 12292
  7.2 75.9 %all-gather.5.cloned.1.call-start = ((), (), s32[]{:S(2)}) async-start(), calls=%async_computation.9 | async-start | bytes 1880064 | tf_op jit(solution)/shard_map/all_gather | solution.py:559
  8.0 11.8 %collective-permute-start = (bf16[8,1792]{1,0:T(8,128)(2,1)S(1)}, bf16[8,1792]{1,0:T(8,128)(2,1)S(1)}, u32[]{:S(2)}, u32[]{:S(2)}) collective-permute-start(bf16[8,1792]{1,0:T(8,128)(2,1)S(1)} %get-tuple-element.45), channel_id=1, source_target_pairs={{0,16},{16,32},{32,48},{48,64},{64,80},{80,96},{96,112},{112,128},... | collective-permute-start | bytes 86024 | tf_op jit(solution)/shard_map/ppermute | solution.py:525
  11.5 9.0 %copy-start.2 = (bf16[27,128,8]{1,2,0:T(8,128)(2,1)S(1)}, bf16[27,128,8]{1,2,0:T(8,128)(2,1)}, u32[]{:S(2)}) copy-start(bf16[27,128,8]{1,2,0:T(8,128)(2,1)} %param.10) | copy-start | bytes 165892
  11.5 9.0 %copy-start.5 = (bf16[27,128,8]{1,2,0:T(8,128)(2,1)S(1)}, bf16[27,128,8]{1,2,0:T(8,128)(2,1)}, u32[]{:S(2)}) copy-start(bf16[27,128,8]{1,2,0:T(8,128)(2,1)} %param.12) | copy-start | bytes 165892
  11.6 8.3 %collective-permute-start.1 = (bf16[8,1792]{1,0:T(8,128)(2,1)S(1)}, bf16[8,1792]{1,0:T(8,128)(2,1)S(1)}, u32[]{:S(2)}, u32[]{:S(2)}) collective-permute-start(bf16[8,1792]{1,0:T(8,128)(2,1)S(1)} %get-tuple-element.46), channel_id=1, source_target_pairs={{16,0},{32,16},{48,32},{64,48},{80,64},{96,80},{112,96},{128,112},... | collective-permute-start | bytes 86024 | tf_op jit(solution)/shard_map/ppermute | solution.py:528
  18.6 15.0 %copy-start.3 = (bf16[27,128,8]{1,2,0:T(8,128)(2,1)S(1)}, bf16[27,128,8]{1,2,0:T(8,128)(2,1)}, u32[]{:S(2)}) copy-start(bf16[27,128,8]{1,2,0:T(8,128)(2,1)} %param.11) | copy-start | bytes 165892
  48.9 33.1 %all-to-all-start.2 = ((bf16[32,16,384]{2,1,0:T(8,128)(2,1)}), bf16[32,16,384]{2,1,0:T(8,128)(2,1)S(1)}, u32[]{:S(2)}, u32[]{:S(2)}) async-start(bf16[32,16,384]{2,1,0:T(8,128)(2,1)} %get-tuple-element.53), calls=%async_computation.2 | async-start | bytes 786432 | tf_op jit(solution)/shard_map/all_to_all | solution.py:531
  64.7 51.5 %all-gather.7.cloned.1.call-start = ((), (), s32[]{:S(2)}) async-start(), calls=%async_computation.10 | async-start | bytes 1114112 | tf_op jit(solution)/shard_map/all_gather | solution.py:560
  83.1 16.8 %all-to-all-start.3 = ((bf16[16,16,1152]{2,1,0:T(8,128)(2,1)}), bf16[16,16,1152]{2,1,0:T(8,128)(2,1)S(1)}, u32[]{:S(2)}, u32[]{:S(2)}) async-start(bf16[16,16,1152]{2,1,0:T(8,128)(2,1)} %shard_map.130), calls=%async_computation.3 | async-start | bytes 1179648 | tf_op jit(solution)/shard_map/all_to_all | solution.py:531
  86.6 1.5 copy-start
  104.4 23.1 %collective-permute-start.3 = (bf16[128,1024]{1,0:T(8,128)(2,1)S(1)}, bf16[128,1024]{1,0:T(8,128)(2,1)S(1)}, u32[]{:S(2)}, u32[]{:S(2)}) collective-permute-start(bf16[128,1024]{1,0:T(8,128)(2,1)S(1)} %get-tuple-element.60), channel_id=1, source_target_pairs={{16,0},{32,16},{48,32},{64,48},{80,64},{96,80},{112,96},{128,112},... | collective-permute-start | bytes 786440 | tf_op jit(solution)/shard_map/ppermute | solution.py:528
  106.3 21.1 %collective-permute-start.2 = (bf16[128,1024]{1,0:T(8,128)(2,1)S(1)}, bf16[128,1024]{1,0:T(8,128)(2,1)S(1)}, u32[]{:S(2)}, u32[]{:S(2)}) collective-permute-start(bf16[128,1024]{1,0:T(8,128)(2,1)S(1)} %get-tuple-element.60), channel_id=1, source_target_pairs={{0,16},{16,32},{32,48},{48,64},{64,80},{80,96},{96,112},{112,128},... | collective-permute-start | bytes 786440 | tf_op jit(solution)/shard_map/ppermute | solution.py:525
  110.2 17.2 %all-to-all-start.4 = ((f32[32,2,128]{2,1,0:T(2,128)}), f32[32,2,128]{2,1,0:T(2,128)S(1)}, u32[]{:S(2)}, u32[]{:S(2)}) async-start(f32[32,2,128]{2,1,0:T(2,128)} %get-tuple-element.61), calls=%async_computation.4 | async-start | bytes 65536 | tf_op jit(solution)/shard_map/all_to_all | solution.py:531
  145.5 22.2 %copy-start.1 = (bf16[27,128,16]{1,2,0:T(8,128)(2,1)S(1)}, bf16[27,128,16]{1,2,0:T(8,128)(2,1)}, u32[]{:S(2)}) copy-start(bf16[27,128,16]{1,2,0:T(8,128)(2,1)} %param.9) | copy-start | bytes 331780
  192.5 18.0 %all-to-all-start.8 = ((bf16[32,40,128]{2,1,0:T(8,128)(2,1)}), bf16[32,40,128]{2,1,0:T(8,128)(2,1)S(1)}, u32[]{:S(2)}, u32[]{:S(2)}) async-start(bf16[32,40,128]{2,1,0:T(8,128)(2,1)} %shard_map.136), calls=%async_computation.8 | async-start | bytes 655360 | tf_op jit(solution)/shard_map/all_to_all | solution.py:531
  196.2 6.2 %collective-permute-start.4 = (f32[16,128]{1,0:T(8,128)S(1)}, f32[16,128]{1,0:T(8,128)S(1)}, u32[]{:S(2)}, u32[]{:S(2)}) collective-permute-start(f32[16,128]{1,0:T(8,128)S(1)} %get-tuple-element.76), channel_id=1, source_target_pairs={{0,16},{16,32},{32,48},{48,64},{64,80},{80,96},{96,112},{112,128},... | collective-permute-start | bytes 24584 | tf_op jit(solution)/shard_map/ppermute | solution.py:525
Sparse Core Ops, SparseCore 0:
  21.4 44.3 all-gather.4
  68.5 46.1 all-gather.6

commit v5 on v4

--- a/solution.py
+++ b/solution.py
@@ -46,10 +46,6 @@
     inside = (column >= 0) & (column < columns) & (row >= 0) & (row < rows)
     moved = pltpu.roll(values, (-(step_y * columns + step_x)) % extent, 1)
     return moved * jnp.where(inside, 1.0, 0.0)
-
-
-def fine_shift(values, step_y, step_x):
-    return shift(values, step_y, step_x, 2 * YC, 2 * XC)
 
 
 def coarse_shift(values, step_y, step_x):
@@ -182,8 +178,8 @@
     )
     features = jnp.concatenate([upsampled, skip], axis=0)
     joined[...] = features.astype(bf16)
-    for tap in range(9):
-        unfolded[tap * 16 : tap * 16 + 16, :] = fine_shift(features, tap // 3 - 1, tap % 3 - 1).astype(bf16)
+    for tap, moved in enumerate(nine_shifts(features, source_masks(HALOED))):
+        unfolded[tap * 16 : tap * 16 + 16, :] = moved.astype(bf16)
     total = jnp.zeros((C_OUT, SLAB), f32)
     for k_z in range(3):
         matrix = []
@@ -278,9 +274,28 @@
     return jnp.concatenate([pair[:, :8].reshape(16, SLAB), pair[:, 8:].reshape(16, SLAB)], axis=1)
 
 
-def unfold_block(values, unfolded, block, sign):
-    for tap in range(9):
-        moved = fine_shift(values, sign * (tap // 3 - 1), sign * (tap % 3 - 1))
+def source_masks(extent):
+    cell = lax.broadcasted_iota(jnp.int32, (1, extent), 1)
+    column, row = cell % (2 * XC), cell // (2 * XC) % (2 * YC)
+    in_x = {-1: jnp.where(column == 2 * XC - 1, 0.0, 1.0), 1: jnp.where(column == 0, 0.0, 1.0)}
+    in_y = {-1: jnp.where(row == 2 * YC - 1, 0.0, 1.0), 1: jnp.where(row == 0, 0.0, 1.0)}
+    return in_y, in_x
+
+
+def nine_shifts(values, masks):
+    in_y, in_x = masks
+    extent = values.shape[-1]
+    by_x = {0: values, -1: values * in_x[-1], 1: values * in_x[1]}
+    for step_y in (-1, 0, 1):
+        for step_x in (-1, 0, 1):
+            moved = by_x[step_x] if step_y == 0 else by_x[step_x] * in_y[step_y]
+            offset = (-(step_y * 2 * XC + step_x)) % extent
+            yield moved if offset == 0 else pltpu.roll(moved, offset, 1)
+
+
+def unfold_block(values, unfolded, block, sign, masks):
+    for place, moved in enumerate(nine_shifts(values, masks)):
+        tap = place if sign == 1 else 8 - place
         unfolded[tap, pl.ds(pl.multiple_of(block * 16, 16), 16), :] = moved.astype(bf16)
 
 
@@ -306,10 +321,11 @@
     packed, matrix, pre, halo, stats, unfolded
 ):
     mask = edge_mask(lax.axis_index("gz"), stats.shape[0], 1)
+    masks = source_masks(HALOED)
 
     def prepare(block, carry):
         hidden = activate(read_planes(packed, block)).astype(bf16).astype(f32) * mask
-        unfold_block(hidden, unfolded, block, 1)
+        unfold_block(hidden, unfolded, block, 1, masks)
         return carry
 
     lax.fori_loop(0, 8, prepare, 0)
@@ -381,6 +397,7 @@
     (fetch,) = copies((far_matrix,), (matrix,), semaphores)
     slab, share = lax.axis_index("gz"), lax.axis_index("ch")
     mask = edge_mask(slab, sums.shape[0], 2)
+    masks = source_masks(WIDE)
     mean_grad, mean_cross = total_means(sums_in)
     columns[0] = jnp.broadcast_to(mean_grad, (C_OUT, 128))
     columns[1] = jnp.broadcast_to(mean_cross, (C_OUT, 128))
@@ -391,7 +408,7 @@
         grad = columns[2, at, :1] * (slope[at, :] - columns[0, at, :1] - normed[at, :] * columns[1, at, :1])
         grad = grad.astype(bf16).astype(f32) * mask
         grads[at, :] = grad[:, SLAB : 2 * SLAB]
-        unfold_block(grad, unfolded, block, -1)
+        unfold_block(grad, unfolded, block, -1, masks)
         return carry
 
     lax.fori_loop(0, 8, prepare, 0)
@@ -416,8 +433,8 @@
     sums[...] = jnp.broadcast_to(jnp.where(row < 1, one, two)[None], sums.shape)
     own = activate(read_planes(packed, share // 2)).astype(bf16).astype(f32)
     own = own * edge_mask(slab, sums.shape[0], 1)
-    for tap in range(9):
-        own_unfolded[tap * 16 : tap * 16 + 16, :] = fine_shift(own, tap // 3 - 1, tap % 3 - 1).astype(bf16)
+    for tap, moved in enumerate(nine_shifts(own, source_masks(HALOED))):
+        own_unfolded[tap * 16 : tap * 16 + 16, :] = moved.astype(bf16)
     odd = share % 2 == 1
     turned = jnp.transpose(grads[...]).astype(bf16)
     for k_z in range(3):
@@ -435,6 +452,7 @@
     (fetch,) = copies((far_matrix,), (matrix,), semaphores)
     slab = lax.axis_index("gz")
     mask = edge_mask(slab, sums_in.shape[0], 1)
+    masks = source_masks(HALOED)
     mean_grad, mean_cross = total_means(sums_in)
     columns[0] = jnp.broadcast_to(mean_grad, (C_OUT, 128))
     columns[1] = jnp.broadcast_to(mean_cross, (C_OUT, 128))
@@ -447,7 +465,7 @@
         grad = columns[2, at, :1] * (slope[at, :] - columns[0, at, :1] - normed * columns[1, at, :1])
         grad = grad.astype(bf16).astype(f32) * mask
         grads[at, :] = grad[:, FINE : 3 * FINE]
-        unfold_block(grad, unfolded, block, -1)
+        unfold_block(grad, unfolded, block, -1, masks)
         return carry
 
     lax.fori_loop(0, 8, prepare, 0)
@@ -490,8 +508,8 @@
             at = (k_z * 9 + tap) * 16
             weight_grads[at : at + 16, :] = product[:, tap * 128 : tap * 128 + 128].astype(bf16)
     own = joined[...].astype(f32)
-    for tap in range(9):
-        own_unfolded[tap * 16 : tap * 16 + 16, :] = fine_shift(own, tap // 3 - 1, tap % 3 - 1).astype(bf16)
+    for tap, moved in enumerate(nine_shifts(own, masks)):
+        own_unfolded[tap * 16 : tap * 16 + 16, :] = moved.astype(bf16)
     turned = jnp.transpose(grads[...]).astype(bf16)
     for k_z in range(3):
         product = jnp.dot(

time: 219 us -> 217 us (level)
  no operation moved by 1% of the time
where the time goes in v5:
time: 217 us
  blocking collectives  75 us (35%)
  waiting for transfers between devices  48 us (22%)
  starting transfers between devices  47.7 us (22%)
  Pallas kernels  25 us (12%)
  between operations  14.2 us (7%)
  local copies, waits for them, and re-layouts  5.33 us (2%)
    all_to_all x5, blocking collectives, swap(): return lax.all_to_all(block, axis, 0, 0, tiled=True)  75 us
    all_to_all x4, waiting for transfers between devices, swap(): return lax.all_to_all(block, axis, 0, 0, tiled=True)  46.3 us
    all_to_all x4, starting transfers between devices, swap(): return lax.all_to_all(block, axis, 0, 0, tiled=True)  29.3 us
    pallas_call x12, Pallas kernels, call(): pl.pallas_call(kernel, out_shape=[out(index, *shape) for index, shape in...  25 us
    ppermute x3, starting transfers between devices, from_below(): return lax.ppermute(block, 'gz', upward)  10.8 us
    ppermute x2, starting transfers between devices, from_above(): return lax.ppermute(block, 'gz', downward)  7.58 us
  transfers between devices with their start and end apart: 11, of which 5 were waited for; matrix products, arithmetic and copies ran while one was open for 2% of the time, Pallas kernels for 4%

profile of v5, /device:TPU:8, one launch (start us, length us, event | category | flops | bytes accessed | tf_op | source)
XLA Modules:
  0.0 216.5 jit_solution(16492873128765429208)
XLA Ops:
  7.2 0.0 copy-start.4
  7.2 0.0 all-gather.5.cloned.1.call-start
  7.2 0.8 shard_map.126
  8.0 3.5 %collective-permute-start = (bf16[8,1792]{1,0:T(8,128)(2,1)S(1)}, bf16[8,1792]{1,0:T(8,128)(2,1)S(1)}, u32[]{:S(2)}, u32[]{:S(2)}) collective-permute-start(bf16[8,1792]{1,0:T(8,128)(2,1)S(1)} %get-tuple-element.45), channel_id=1, source_target_pairs={{0,16},{16,32},{32,48},{48,64},{64,80},{80,96},{96,112},{112,128},... | collective-permute-start | bytes 86024 | tf_op jit(solution)/shard_map/ppermute | solution.py:543
  11.5 0.0 copy-start.2
  11.5 0.0 copy-start.5
  11.6 5.7 %collective-permute-start.1 = (bf16[8,1792]{1,0:T(8,128)(2,1)S(1)}, bf16[8,1792]{1,0:T(8,128)(2,1)S(1)}, u32[]{:S(2)}, u32[]{:S(2)}) collective-permute-start(bf16[8,1792]{1,0:T(8,128)(2,1)S(1)} %get-tuple-element.46), channel_id=1, source_target_pairs={{16,0},{32,16},{48,32},{64,48},{80,64},{96,80},{112,96},{128,112},... | collective-permute-start | bytes 86024 | tf_op jit(solution)/shard_map/ppermute | solution.py:546
  17.2 1.4 copy.22
  18.6 0.0 copy-start.3
  18.6 0.9 copy.23
  19.5 0.3 copy.24.pieces
  19.8 0.0 collective-permute-done.low
  19.9 0.0 collective-permute-done.1.high
  19.9 0.0 copy-done.4
  19.9 0.7 shard_map.127
  20.6 0.0 copy-done.2
  20.6 0.0 copy-done.5
  20.6 0.7 pad_maximum_fusion
  21.2 0.0 all-gather.5.cloned.1.call-update
  21.2 12.3 %all_to_all.45.mixed = bf16[16,16,640]{2,1,0:T(8,128)(2,1)S(1)} all-to-all(bf16[16,16,640]{2,1,0:T(8,128)(2,1)S(1)} %get-tuple-element.49), channel_id=1, replica_groups=mesh['gz'=32,'ch'=16] {'ch'}, dimensions={0} | all-to-all | bytes 655360 | tf_op jit(solution)/shard_map/all_to_all | solution.py:549
  33.6 0.0 copy-done.3
  33.6 1.2 shard_map.128
  34.8 12.8 %all_to_all.46.parts = bf16[16,16,640]{2,1,0:T(8,128)(2,1)S(1)} all-to-all(bf16[16,16,640]{2,1,0:T(8,128)(2,1)S(1)} %get-tuple-element.51), channel_id=1, replica_groups=mesh['gz'=32,'ch'=16] {'ch'}, dimensions={0} | all-to-all | bytes 655360 | tf_op jit(solution)/shard_map/all_to_all | solution.py:549
  47.6 1.3 shard_map.129
  48.9 15.8 %all-to-all-start.2 = ((bf16[32,16,384]{2,1,0:T(8,128)(2,1)}), bf16[32,16,384]{2,1,0:T(8,128)(2,1)S(1)}, u32[]{:S(2)}, u32[]{:S(2)}) async-start(bf16[32,16,384]{2,1,0:T(8,128)(2,1)} %get-tuple-element.53), calls=%async_computation.2 | async-start | bytes 786432 | tf_op jit(solution)/shard_map/all_to_all | solution.py:549
  64.7 0.0 all-gather.7.cloned.1.call-start
  64.7 0.7 all-gather.7.cloned.1.call-update
  65.4 16.6 %all-to-all-done.2.stats = bf16[32,16,384]{2,1,0:T(8,128)(2,1)S(1)} async-done(((bf16[32,16,384]{2,1,0:T(8,128)(2,1)}), bf16[32,16,384]{2,1,0:T(8,128)(2,1)S(1)}, u32[]{:S(2)}, u32[]{:S(2)}) %all-to-all-start.2) | async-done | bytes 393248 | tf_op jit(solution)/shard_map/all_to_all | solution.py:549
  82.0 1.0 shard_map.130
  83.0 0.0 all-gather.5.cloned.1.call-done
  83.0 3.6 %all-to-all-start.3 = ((bf16[16,16,1152]{2,1,0:T(8,128)(2,1)}), bf16[16,16,1152]{2,1,0:T(8,128)(2,1)S(1)}, u32[]{:S(2)}, u32[]{:S(2)}) async-start(bf16[16,16,1152]{2,1,0:T(8,128)(2,1)} %shard_map.130), calls=%async_computation.3 | async-start | bytes 1179648 | tf_op jit(solution)/shard_map/all_to_all | solution.py:549
  86.6 0.0 copy-start
  86.7 1.5 copy-done
  88.1 1.5 shard_map.131
  89.6 10.3 %all-to-all-done.3.packed = bf16[16,16,1152]{2,1,0:T(8,128)(2,1)S(1)} async-done(((bf16[16,16,1152]{2,1,0:T(8,128)(2,1)}), bf16[16,16,1152]{2,1,0:T(8,128)(2,1)S(1)}, u32[]{:S(2)}, u32[]{:S(2)}) %all-to-all-start.3) | async-done | bytes 589856 | tf_op jit(solution)/shard_map/all_to_all | solution.py:549
  99.9 4.1 %shard_map.132 = (f32[128,1024]{1,0:T(8,128)S(1)}, bf16[128,1024]{1,0:T(8,128)(2,1)S(1)}, f32[32,2,128]{2,1,0:T(2,128)}) custom-call(bf16[16,16,1152]{2,1,0:T(8,128)(2,1)S(1)} %all-to-all-done.3.packed, bf16[128,3456]{1,0:T(8,128)(2,1)S(1)} %get-tuple-element.58.matrix), custom_call_target="tpu_custom_call" | custom-call | tf_op jit(solution)/shard_map/pallas_call | solution.py:93
  104.0 1.9 collective-permute-start.3
  105.9 3.9 %collective-permute-start.2 = (bf16[128,1024]{1,0:T(8,128)(2,1)S(1)}, bf16[128,1024]{1,0:T(8,128)(2,1)S(1)}, u32[]{:S(2)}, u32[]{:S(2)}) collective-permute-start(bf16[128,1024]{1,0:T(8,128)(2,1)S(1)} %get-tuple-element.60), channel_id=1, source_target_pairs={{0,16},{16,32},{32,48},{48,64},{64,80},{80,96},{96,112},{112,128},... | collective-permute-start | bytes 786440 | tf_op jit(solution)/shard_map/ppermute | solution.py:543
  109.8 6.0 %all-to-all-start.4 = ((f32[32,2,128]{2,1,0:T(2,128)}), f32[32,2,128]{2,1,0:T(2,128)S(1)}, u32[]{:S(2)}, u32[]{:S(2)}) async-start(f32[32,2,128]{2,1,0:T(2,128)} %get-tuple-element.61), calls=%async_computation.4 | async-start | bytes 65536 | tf_op jit(solution)/shard_map/all_to_all | solution.py:549
  115.8 0.0 all-gather.7.cloned.1.call-done
  115.8 11.2 %all-to-all-done.4.stats = f32[32,2,128]{2,1,0:T(2,128)S(1)} async-done(((f32[32,2,128]{2,1,0:T(2,128)}), f32[32,2,128]{2,1,0:T(2,128)S(1)}, u32[]{:S(2)}, u32[]{:S(2)}) %all-to-all-start.4) | async-done | bytes 32800 | tf_op jit(solution)/shard_map/all_to_all | solution.py:549
  127.0 0.0 collective-permute-done.3.high
  127.0 0.0 collective-permute-done.2.low
  127.0 1.9 shard_map.133
  128.9 16.4 %all_to_all.47.sums_in = f32[32,2,128]{2,1,0:T(2,128)S(1)} all-to-all(f32[32,2,128]{2,1,0:T(2,128)S(1)} %get-tuple-element.67), channel_id=1, replica_groups=mesh['gz'=32,'ch'=16] {'gz'}, dimensions={0} | all-to-all | bytes 65536 | tf_op jit(solution)/shard_map/all_to_all | solution.py:549
  145.3 0.0 copy-start.1
  145.3 5.9 %shard_map.134 = (f32[128,2048]{1,0:T(8,128)S(1)}, f32[32,2,128]{2,1,0:T(2,128)S(1)}, f32[216,128]{1,0:T(8,128)S(1)}) custom-call(f32[128,3072]{1,0:T(8,128)S(1)} %get-tuple-element.64.normed, f32[128,3072]{1,0:T(8,128)S(1)} %get-tuple-element.65.slope, f32[8,128]{1,0:T(8,128)S(1)} %get-tuple-element.66.inverse_row, f32[32,2,128]{2,1,0:T(2,128)S(1)} %all_to_all.47.sums_in, ...), custom_call_target="tpu_custom_call" | custom-call | tf_op jit(solution)/shard_map/pallas_call | solution.py:93
  151.2 15.2 %all_to_all.48.sums_in = f32[32,2,128]{2,1,0:T(2,128)S(1)} all-to-all(f32[32,2,128]{2,1,0:T(2,128)S(1)} %get-tuple-element.70), channel_id=1, replica_groups=mesh['gz'=32,'ch'=16] {'gz'}, dimensions={0} | all-to-all | bytes 65536 | tf_op jit(solution)/shard_map/all_to_all | solution.py:549
  166.4 0.0 copy-done.1
  166.4 5.1 %shard_map.135 = (bf16[8,1024]{1,0:T(8,128)(2,1)S(1)}, f32[16,128]{1,0:T(8,128)S(1)}, f32[16,128]{1,0:T(8,128)S(1)}, bf16[1280,128]{1,0:T(8,128)(2,1)S(1)}) custom-call(f32[128,2048]{1,0:T(8,128)S(1)} %get-tuple-element.69.slope, f32[32,2,128]{2,1,0:T(2,128)S(1)} %all_to_all.48.sums_in, bf16[16,16,1152]{2,1,0:T(8,128)(2,1)S(1)} %all-to-all-done.3.packed, ...), custom_call_target="tpu_custom_call" | custom-call | tf_op jit(solution)/shard_map/pallas_call | solution.py:93
  171.5 18.2 %all_to_all.49.parts = bf16[32,40,128]{2,1,0:T(8,128)(2,1)S(1)} all-to-all(bf16[32,40,128]{2,1,0:T(8,128)(2,1)S(1)} %bitcast.22), channel_id=1, replica_groups=mesh['gz'=32,'ch'=16] {'gz'}, dimensions={0} | all-to-all | bytes 655360 | tf_op jit(solution)/shard_map/all_to_all | solution.py:549
  189.7 0.8 shard_map.136
  190.5 4.0 %all-to-all-start.8 = ((bf16[32,40,128]{2,1,0:T(8,128)(2,1)}), bf16[32,40,128]{2,1,0:T(8,128)(2,1)S(1)}, u32[]{:S(2)}, u32[]{:S(2)}) async-start(bf16[32,40,128]{2,1,0:T(8,128)(2,1)} %shard_map.136), calls=%async_computation.8 | async-start | bytes 655360 | tf_op jit(solution)/shard_map/all_to_all | solution.py:549
  194.5 3.4 %collective-permute-start.4 = (f32[16,128]{1,0:T(8,128)S(1)}, f32[16,128]{1,0:T(8,128)S(1)}, u32[]{:S(2)}, u32[]{:S(2)}) collective-permute-start(f32[16,128]{1,0:T(8,128)S(1)} %get-tuple-element.76), channel_id=1, source_target_pairs={{0,16},{16,32},{32,48},{48,64},{64,80},{80,96},{96,112},{112,128},... | collective-permute-start | bytes 24584 | tf_op jit(solution)/shard_map/ppermute | solution.py:543
  197.9 0.6 copy.25
  198.5 0.6 copy.26
  199.1 0.9 collective-permute-done.4
  200.0 0.6 fusion
  200.6 8.3 %all-to-all-done.8.gathered = bf16[32,40,128]{2,1,0:T(8,128)(2,1)S(1)} async-done(((bf16[32,40,128]{2,1,0:T(8,128)(2,1)}), bf16[32,40,128]{2,1,0:T(8,128)(2,1)S(1)}, u32[]{:S(2)}, u32[]{:S(2)}) %all-to-all-start.8) | async-done | bytes 327712 | tf_op jit(solution)/shard_map/all_to_all | solution.py:549
  208.9 0.8 shard_map.137
Async XLA Ops:
  7.2 12.7 %copy-start.4 = (bf16[16,1,128]{2,0,1:T(8,128)(2,1)S(1)}, bf16[16,1,128]{2,0,1:T(8,128)(2,1)}, u32[]{:S(2)}) copy-start(bf16[16,1,128]{2,0,1:T(8,128)(2,1)} %param.7) | copy-start | bytes 12292
  7.2 75.9 %all-gather.5.cloned.1.call-start = ((), (), s32[]{:S(2)}) async-start(), calls=%async_computation.9 | async-start | bytes 1880064 | tf_op jit(solution)/shard_map/all_gather | solution.py:577
  8.0 11.8 %collective-permute-start = (bf16[8,1792]{1,0:T(8,128)(2,1)S(1)}, bf16[8,1792]{1,0:T(8,128)(2,1)S(1)}, u32[]{:S(2)}, u32[]{:S(2)}) collective-permute-start(bf16[8,1792]{1,0:T(8,128)(2,1)S(1)} %get-tuple-element.45), channel_id=1, source_target_pairs={{0,16},{16,32},{32,48},{48,64},{64,80},{80,96},{96,112},{112,128},... | collective-permute-start | bytes 86024 | tf_op jit(solution)/shard_map/ppermute | solution.py:543
  11.5 9.0 %copy-start.2 = (bf16[27,128,8]{1,2,0:T(8,128)(2,1)S(1)}, bf16[27,128,8]{1,2,0:T(8,128)(2,1)}, u32[]{:S(2)}) copy-start(bf16[27,128,8]{1,2,0:T(8,128)(2,1)} %param.10) | copy-start | bytes 165892
  11.5 9.0 %copy-start.5 = (bf16[27,128,8]{1,2,0:T(8,128)(2,1)S(1)}, bf16[27,128,8]{1,2,0:T(8,128)(2,1)}, u32[]{:S(2)}) copy-start(bf16[27,128,8]{1,2,0:T(8,128)(2,1)} %param.12) | copy-start | bytes 165892
  11.6 8.3 %collective-permute-start.1 = (bf16[8,1792]{1,0:T(8,128)(2,1)S(1)}, bf16[8,1792]{1,0:T(8,128)(2,1)S(1)}, u32[]{:S(2)}, u32[]{:S(2)}) collective-permute-start(bf16[8,1792]{1,0:T(8,128)(2,1)S(1)} %get-tuple-element.46), channel_id=1, source_target_pairs={{16,0},{32,16},{48,32},{64,48},{80,64},{96,80},{112,96},{128,112},... | collective-permute-start | bytes 86024 | tf_op jit(solution)/shard_map/ppermute | solution.py:546
  18.6 15.0 %copy-start.3 = (bf16[27,128,8]{1,2,0:T(8,128)(2,1)S(1)}, bf16[27,128,8]{1,2,0:T(8,128)(2,1)}, u32[]{:S(2)}) copy-start(bf16[27,128,8]{1,2,0:T(8,128)(2,1)} %param.11) | copy-start | bytes 165892
  48.9 33.1 %all-to-all-start.2 = ((bf16[32,16,384]{2,1,0:T(8,128)(2,1)}), bf16[32,16,384]{2,1,0:T(8,128)(2,1)S(1)}, u32[]{:S(2)}, u32[]{:S(2)}) async-start(bf16[32,16,384]{2,1,0:T(8,128)(2,1)} %get-tuple-element.53), calls=%async_computation.2 | async-start | bytes 786432 | tf_op jit(solution)/shard_map/all_to_all | solution.py:549
  64.7 51.1 %all-gather.7.cloned.1.call-start = ((), (), s32[]{:S(2)}) async-start(), calls=%async_computation.10 | async-start | bytes 1114112 | tf_op jit(solution)/shard_map/all_gather | solution.py:578
  83.0 16.8 %all-to-all-start.3 = ((bf16[16,16,1152]{2,1,0:T(8,128)(2,1)}), bf16[16,16,1152]{2,1,0:T(8,128)(2,1)S(1)}, u32[]{:S(2)}, u32[]{:S(2)}) async-start(bf16[16,16,1152]{2,1,0:T(8,128)(2,1)} %shard_map.130), calls=%async_computation.3 | async-start | bytes 1179648 | tf_op jit(solution)/shard_map/all_to_all | solution.py:549
  86.6 1.5 copy-start
  104.0 23.1 %collective-permute-start.3 = (bf16[128,1024]{1,0:T(8,128)(2,1)S(1)}, bf16[128,1024]{1,0:T(8,128)(2,1)S(1)}, u32[]{:S(2)}, u32[]{:S(2)}) collective-permute-start(bf16[128,1024]{1,0:T(8,128)(2,1)S(1)} %get-tuple-element.60), channel_id=1, source_target_pairs={{16,0},{32,16},{48,32},{64,48},{80,64},{96,80},{112,96},{128,112},... | collective-permute-start | bytes 786440 | tf_op jit(solution)/shard_map/ppermute | solution.py:546
  105.9 21.2 %collective-permute-start.2 = (bf16[128,1024]{1,0:T(8,128)(2,1)S(1)}, bf16[128,1024]{1,0:T(8,128)(2,1)S(1)}, u32[]{:S(2)}, u32[]{:S(2)}) collective-permute-start(bf16[128,1024]{1,0:T(8,128)(2,1)S(1)} %get-tuple-element.60), channel_id=1, source_target_pairs={{0,16},{16,32},{32,48},{48,64},{64,80},{80,96},{96,112},{112,128},... | collective-permute-start | bytes 786440 | tf_op jit(solution)/shard_map/ppermute | solution.py:543
  109.8 17.2 %all-to-all-start.4 = ((f32[32,2,128]{2,1,0:T(2,128)}), f32[32,2,128]{2,1,0:T(2,128)S(1)}, u32[]{:S(2)}, u32[]{:S(2)}) async-start(f32[32,2,128]{2,1,0:T(2,128)} %get-tuple-element.61), calls=%async_computation.4 | async-start | bytes 65536 | tf_op jit(solution)/shard_map/all_to_all | solution.py:549
  145.3 21.1 %copy-start.1 = (bf16[27,128,16]{1,2,0:T(8,128)(2,1)S(1)}, bf16[27,128,16]{1,2,0:T(8,128)(2,1)}, u32[]{:S(2)}) copy-start(bf16[27,128,16]{1,2,0:T(8,128)(2,1)} %param.9) | copy-start | bytes 331780
  190.5 18.4 %all-to-all-start.8 = ((bf16[32,40,128]{2,1,0:T(8,128)(2,1)}), bf16[32,40,128]{2,1,0:T(8,128)(2,1)S(1)}, u32[]{:S(2)}, u32[]{:S(2)}) async-start(bf16[32,40,128]{2,1,0:T(8,128)(2,1)} %shard_map.136), calls=%async_computation.8 | async-start | bytes 655360 | tf_op jit(solution)/shard_map/all_to_all | solution.py:549
  194.5 5.5 %collective-permute-start.4 = (f32[16,128]{1,0:T(8,128)S(1)}, f32[16,128]{1,0:T(8,128)S(1)}, u32[]{:S(2)}, u32[]{:S(2)}) collective-permute-start(f32[16,128]{1,0:T(8,128)S(1)} %get-tuple-element.76), channel_id=1, source_target_pairs={{0,16},{16,32},{32,48},{48,64},{64,80},{80,96},{96,112},{112,128},... | collective-permute-start | bytes 24584 | tf_op jit(solution)/shard_map/ppermute | solution.py:543
Sparse Core Ops, SparseCore 0:
  21.4 44.3 all-gather.4
  68.5 46.0 all-gather.6

commit v6 on v5

--- a/solution.py
+++ b/solution.py
@@ -304,7 +304,11 @@
     return both[:, first * 8 : first * 8 + 8].reshape(C_OUT, C_OUT)
 
 
-def matrix_kernel(weights, first_skip, forward, far_backward, far_first, backward, first, semaphores):
+def matrix_kernel(
+    weights, first_skip, up_weight, joined,
+    forward, far_backward, far_first, far_up, far_interleave, far_unfolded,
+    backward, first, up_matrix, interleave, unfolded, semaphores,
+):
     for tap in range(27):
         at = slice(tap * 128, tap * 128 + 128)
         second = tap_matrix(weights, tap, 0)
@@ -313,7 +317,15 @@
         skip_part = jnp.concatenate([first_skip[tap].astype(f32), jnp.zeros((8, 128), f32)], axis=0)
         first[0:128, at] = tap_matrix(weights, tap, 1).astype(bf16)
         first[128:144, at] = skip_part.astype(bf16)
-    for copy in copies((backward, first), (far_backward, far_first), semaphores):
+    for tap in range(27):
+        at = (tap // 9) * 1152 + (tap % 9) * 128
+        up_matrix[:, at : at + 128] = up_weight[tap]
+    interleave[...] = interleave_matrix(True)
+    for tap, moved in enumerate(nine_shifts(joined[...].astype(f32), source_masks(HALOED))):
+        unfolded[tap * 16 : tap * 16 + 16, :] = moved.astype(bf16)
+    made = (backward, first, up_matrix, interleave, unfolded)
+    kept = (far_backward, far_first, far_up, far_interleave, far_unfolded)
+    for copy in copies(made, kept, semaphores):
         copy.wait()
 
 
@@ -445,11 +457,12 @@
 
 
 def first_back_kernel(
-    slope, sums_in, packed, far_matrix, up_weight, coarse, joined, second_grad,
+    slope, sums_in, packed, far_matrix, far_up, coarse, far_unfolded, second_grad, far_interleave,
     skip_grad, coarse_own, coarse_next, weight_grads,
-    unfolded, grads, columns, spread, up_matrix, matrix, own_unfolded, semaphores,
+    unfolded, grads, columns, spread, up_matrix, matrix, own_unfolded, interleave, semaphores,
 ):
-    (fetch,) = copies((far_matrix,), (matrix,), semaphores)
+    kept = (far_matrix, far_up, far_unfolded, far_interleave)
+    fetches = copies(kept, (matrix, up_matrix, own_unfolded, interleave), semaphores)
     slab = lax.axis_index("gz")
     mask = edge_mask(slab, sums_in.shape[0], 1)
     masks = source_masks(HALOED)
@@ -469,7 +482,8 @@
         return carry
 
     lax.fori_loop(0, 8, prepare, 0)
-    fetch.wait()
+    for copy in fetches:
+        copy.wait()
     total = jnp.zeros((144, SLAB), f32)
     for k_z in range(3):
         total = total + jnp.dot(
@@ -480,7 +494,7 @@
     skip_grad[...] = total[128:136].astype(bf16)
     d_up = jnp.concatenate([total[:128, :FINE], total[:128, FINE:]], axis=0).astype(bf16)
     last = (((1,), (1,)), ((), ()))
-    parted = jnp.dot(d_up, interleave_matrix(True), preferred_element_type=f32)
+    parted = jnp.dot(d_up, interleave[...], preferred_element_type=f32)
     for y_par in (0, 1):
         for x_par in (0, 1):
             at = (y_par * 2 + x_par) * COARSE
@@ -493,9 +507,6 @@
                     spread[tap * 128 : tap * 128 + 128, :] = coarse_shift(
                         source, -y_off, -x_off
                     ).astype(bf16)
-    for tap in range(27):
-        at = (tap // 9) * 1152 + (tap % 9) * 128
-        up_matrix[:, at : at + 128] = up_weight[tap]
     low_plane, high_plane = spread[:, :COARSE], spread[:, COARSE:]
     coarse_own[...] = jnp.dot(
         up_matrix[:, 1152:2304], low_plane, preferred_element_type=f32
@@ -507,9 +518,6 @@
         for tap in range(9):
             at = (k_z * 9 + tap) * 16
             weight_grads[at : at + 16, :] = product[:, tap * 128 : tap * 128 + 128].astype(bf16)
-    own = joined[...].astype(f32)
-    for tap, moved in enumerate(nine_shifts(own, masks)):
-        own_unfolded[tap * 16 : tap * 16 + 16, :] = moved.astype(bf16)
     turned = jnp.transpose(grads[...]).astype(bf16)
     for k_z in range(3):
         product = jnp.dot(
@@ -594,12 +602,16 @@
     )
     packed, kernels = lax.optimization_barrier((packed, kernels))
     packed = swap(packed, "ch")
-    forward, backward, first = call(
+    kept = [
+        ((128, 3456), bf16), ((144, 3456), bf16), ((16, 3456), bf16), ((FINE, FINE), bf16), ((144, HALOED), bf16),
+    ]
+    forward, backward, first, up_matrix, interleave, first_unfolded = call(
         matrix_kernel,
-        [((128, 3456), bf16), ((128, 3456), bf16), ((144, 3456), bf16)],
-        (kernels, skip_first),
-        [pltpu.VMEM((128, 3456), bf16), pltpu.VMEM((144, 3456), bf16), pltpu.SemaphoreType.DMA((2,))],
-        far_outs=(1, 2),
+        [((128, 3456), bf16)] + kept,
+        (kernels, skip_first, up_own, joined),
+        [pltpu.VMEM(*shape) for shape in kept] + [pltpu.SemaphoreType.DMA((5,))],
+        10,
+        far_outs=(1, 2, 3, 4, 5),
         near_outs=(0,),
     )
     unfolded = pltpu.VMEM((9, 128, HALOED), bf16)
@@ -648,16 +660,17 @@
         [((8, SLAB), bf16), ((16, COARSE), f32), ((16, COARSE), f32), ((GRAD_ROWS, 128), bf16)],
         (
             slope_one, swap(sums, "gz"), packed, first,
-            up_own, pair, joined, second_grad,
+            up_matrix, pair, first_unfolded, second_grad, interleave,
         ),
         [
             unfolded, pltpu.VMEM((128, SLAB), f32), pltpu.VMEM((3, 128, 128), f32),
             pltpu.VMEM((1152, 2 * COARSE), bf16), pltpu.VMEM((16, 3456), bf16),
-            pltpu.VMEM((144, 3456), bf16), pltpu.VMEM((144, HALOED), bf16), pltpu.SemaphoreType.DMA((1,)),
+            pltpu.VMEM((144, 3456), bf16), pltpu.VMEM((144, HALOED), bf16), pltpu.VMEM((FINE, FINE), bf16),
+            pltpu.SemaphoreType.DMA((4,)),
         ],
-        17,
-        far=(3,),
-        near=(0, 6, 7),
+        18,
+        far=(3, 4, 6, 8),
+        near=(0, 7),
     )
     coarse_grad = (coarse_own + from_below(coarse_next)).astype(bf16)
     rows = GRAD_ROWS // slabs

time: 217 us -> 218 us (level)
  no operation moved by 1% of the time
where the time goes in v6:
time: 218 us; the launch traced here: 217 us
  blocking collectives  75 us (34%)
  starting transfers between devices  47.9 us (22%)
  waiting for transfers between devices  47.5 us (22%)
  Pallas kernels  25.4 us (12%)
  between operations  14.2 us (7%)
  local copies, waits for them, and re-layouts  5.32 us (2%)
    all_to_all x5, blocking collectives, swap(): return lax.all_to_all(block, axis, 0, 0, tiled=True)  75 us
    all_to_all x4, waiting for transfers between devices, swap(): return lax.all_to_all(block, axis, 0, 0, tiled=True)  45.9 us
    all_to_all x4, starting transfers between devices, swap(): return lax.all_to_all(block, axis, 0, 0, tiled=True)  29.4 us
    pallas_call x12, Pallas kernels, call(): pl.pallas_call(kernel, out_shape=[out(index, *shape) for index, shape in...  25.4 us
    ppermute x3, starting transfers between devices, from_below(): return lax.ppermute(block, 'gz', upward)  10.8 us
    ppermute x2, starting transfers between devices, from_above(): return lax.ppermute(block, 'gz', downward)  7.58 us
  transfers between devices with their start and end apart: 11, of which 5 were waited for; matrix products, arithmetic and copies ran while one was open for 2% of the time, Pallas kernels for 4%

profile of v6, /device:TPU:8, one launch (start us, length us, event | category | flops | bytes accessed | tf_op | source)
XLA Modules:
  0.0 216.6 jit_solution(917572022988227637)
XLA Ops:
  7.2 0.0 copy-start.4
  7.2 0.0 all-gather.5.cloned.1.call-start
  7.2 0.8 shard_map.126
  8.0 3.5 %collective-permute-start = (bf16[8,1792]{1,0:T(8,128)(2,1)S(1)}, bf16[8,1792]{1,0:T(8,128)(2,1)S(1)}, u32[]{:S(2)}, u32[]{:S(2)}) collective-permute-start(bf16[8,1792]{1,0:T(8,128)(2,1)S(1)} %get-tuple-element.48), channel_id=1, source_target_pairs={{0,16},{16,32},{32,48},{48,64},{64,80},{80,96},{96,112},{112,128},... | collective-permute-start | bytes 86024 | tf_op jit(solution)/shard_map/ppermute | solution.py:551
  11.5 0.0 copy-start.3
  11.5 0.0 copy-start.5
  11.6 5.7 %collective-permute-start.1 = (bf16[8,1792]{1,0:T(8,128)(2,1)S(1)}, bf16[8,1792]{1,0:T(8,128)(2,1)S(1)}, u32[]{:S(2)}, u32[]{:S(2)}) collective-permute-start(bf16[8,1792]{1,0:T(8,128)(2,1)S(1)} %get-tuple-element.49), channel_id=1, source_target_pairs={{16,0},{32,16},{48,32},{64,48},{80,64},{96,80},{112,96},{128,112},... | collective-permute-start | bytes 86024 | tf_op jit(solution)/shard_map/ppermute | solution.py:554
  17.2 1.4 copy.22
  18.6 0.0 copy-start.2
  18.6 0.9 copy.23
  19.5 0.3 copy.24.pieces
  19.8 0.0 collective-permute-done.low
  19.8 0.0 collective-permute-done.1.high
  19.9 0.0 copy-done.4
  19.9 0.7 shard_map.127
  20.5 0.0 copy-done.3
  20.5 0.0 copy-done.5
  20.5 0.7 pad_maximum_fusion
  21.2 0.0 all-gather.5.cloned.1.call-update
  21.2 12.3 %all_to_all.45.mixed = bf16[16,16,640]{2,1,0:T(8,128)(2,1)S(1)} all-to-all(bf16[16,16,640]{2,1,0:T(8,128)(2,1)S(1)} %get-tuple-element.52), channel_id=1, replica_groups=mesh['gz'=32,'ch'=16] {'ch'}, dimensions={0} | all-to-all | bytes 655360 | tf_op jit(solution)/shard_map/all_to_all | solution.py:557
  33.6 0.0 copy-done.2
  33.6 1.2 shard_map.128
  34.8 12.8 %all_to_all.46.parts = bf16[16,16,640]{2,1,0:T(8,128)(2,1)S(1)} all-to-all(bf16[16,16,640]{2,1,0:T(8,128)(2,1)S(1)} %get-tuple-element.54), channel_id=1, replica_groups=mesh['gz'=32,'ch'=16] {'ch'}, dimensions={0} | all-to-all | bytes 655360 | tf_op jit(solution)/shard_map/all_to_all | solution.py:557
  47.6 1.3 shard_map.129
  48.9 0.0 copy-start.1
  48.9 15.9 %all-to-all-start.2 = ((bf16[32,16,384]{2,1,0:T(8,128)(2,1)}), bf16[32,16,384]{2,1,0:T(8,128)(2,1)S(1)}, u32[]{:S(2)}, u32[]{:S(2)}) async-start(bf16[32,16,384]{2,1,0:T(8,128)(2,1)} %get-tuple-element.56), calls=%async_computation.2 | async-start | bytes 786432 | tf_op jit(solution)/shard_map/all_to_all | solution.py:557
  64.8 0.0 all-gather.7.cloned.1.call-start
  64.9 0.7 all-gather.7.cloned.1.call-update
  65.6 16.6 %all-to-all-done.2.stats = bf16[32,16,384]{2,1,0:T(8,128)(2,1)S(1)} async-done(((bf16[32,16,384]{2,1,0:T(8,128)(2,1)}), bf16[32,16,384]{2,1,0:T(8,128)(2,1)S(1)}, u32[]{:S(2)}, u32[]{:S(2)}) %all-to-all-start.2) | async-done | bytes 393248 | tf_op jit(solution)/shard_map/all_to_all | solution.py:557
  82.2 1.0 shard_map.130
  83.2 0.0 all-gather.5.cloned.1.call-done
  83.2 3.6 %all-to-all-start.3 = ((bf16[16,16,1152]{2,1,0:T(8,128)(2,1)}), bf16[16,16,1152]{2,1,0:T(8,128)(2,1)S(1)}, u32[]{:S(2)}, u32[]{:S(2)}) async-start(bf16[16,16,1152]{2,1,0:T(8,128)(2,1)} %shard_map.130), calls=%async_computation.3 | async-start | bytes 1179648 | tf_op jit(solution)/shard_map/all_to_all | solution.py:557
  86.8 0.0 copy-done.1
  86.8 0.0 copy-start
  86.8 1.5 copy-done
  88.3 2.0 shard_map.131
  90.2 9.8 %all-to-all-done.3.packed = bf16[16,16,1152]{2,1,0:T(8,128)(2,1)S(1)} async-done(((bf16[16,16,1152]{2,1,0:T(8,128)(2,1)}), bf16[16,16,1152]{2,1,0:T(8,128)(2,1)S(1)}, u32[]{:S(2)}, u32[]{:S(2)}) %all-to-all-start.3) | async-done | bytes 589856 | tf_op jit(solution)/shard_map/all_to_all | solution.py:557
  100.0 4.1 %shard_map.132 = (f32[128,1024]{1,0:T(8,128)S(1)}, bf16[128,1024]{1,0:T(8,128)(2,1)S(1)}, f32[32,2,128]{2,1,0:T(2,128)}) custom-call(bf16[16,16,1152]{2,1,0:T(8,128)(2,1)S(1)} %all-to-all-done.3.packed, bf16[128,3456]{1,0:T(8,128)(2,1)S(1)} %get-tuple-element.62.matrix), custom_call_target="tpu_custom_call" | custom-call | tf_op jit(solution)/shard_map/pallas_call | solution.py:93
  104.1 1.9 collective-permute-start.3
  106.0 3.9 %collective-permute-start.2 = (bf16[128,1024]{1,0:T(8,128)(2,1)S(1)}, bf16[128,1024]{1,0:T(8,128)(2,1)S(1)}, u32[]{:S(2)}, u32[]{:S(2)}) collective-permute-start(bf16[128,1024]{1,0:T(8,128)(2,1)S(1)} %get-tuple-element.64), channel_id=1, source_target_pairs={{0,16},{16,32},{32,48},{48,64},{64,80},{80,96},{96,112},{112,128},... | collective-permute-start | bytes 786440 | tf_op jit(solution)/shard_map/ppermute | solution.py:551
  110.0 6.0 %all-to-all-start.4 = ((f32[32,2,128]{2,1,0:T(2,128)}), f32[32,2,128]{2,1,0:T(2,128)S(1)}, u32[]{:S(2)}, u32[]{:S(2)}) async-start(f32[32,2,128]{2,1,0:T(2,128)} %get-tuple-element.65), calls=%async_computation.4 | async-start | bytes 65536 | tf_op jit(solution)/shard_map/all_to_all | solution.py:557
  115.9 0.0 all-gather.7.cloned.1.call-done
  116.0 11.2 %all-to-all-done.4.stats = f32[32,2,128]{2,1,0:T(2,128)S(1)} async-done(((f32[32,2,128]{2,1,0:T(2,128)}), f32[32,2,128]{2,1,0:T(2,128)S(1)}, u32[]{:S(2)}, u32[]{:S(2)}) %all-to-all-start.4) | async-done | bytes 32800 | tf_op jit(solution)/shard_map/all_to_all | solution.py:557
  127.2 0.0 collective-permute-done.3.high
  127.2 0.0 collective-permute-done.2.low
  127.2 1.9 shard_map.133
  129.1 16.3 %all_to_all.47.sums_in = f32[32,2,128]{2,1,0:T(2,128)S(1)} all-to-all(f32[32,2,128]{2,1,0:T(2,128)S(1)} %get-tuple-element.71), channel_id=1, replica_groups=mesh['gz'=32,'ch'=16] {'gz'}, dimensions={0} | all-to-all | bytes 65536 | tf_op jit(solution)/shard_map/all_to_all | solution.py:557
  145.4 5.9 %shard_map.134 = (f32[128,2048]{1,0:T(8,128)S(1)}, f32[32,2,128]{2,1,0:T(2,128)S(1)}, f32[216,128]{1,0:T(8,128)S(1)}) custom-call(f32[128,3072]{1,0:T(8,128)S(1)} %get-tuple-element.68.normed, f32[128,3072]{1,0:T(8,128)S(1)} %get-tuple-element.69.slope, f32[8,128]{1,0:T(8,128)S(1)} %get-tuple-element.70.inverse_row, f32[32,2,128]{2,1,0:T(2,128)S(1)} %all_to_all.47.sums_in, ...), custom_call_target="tpu_custom_call" | custom-call | tf_op jit(solution)/shard_map/pallas_call | solution.py:93
  151.3 15.2 %all_to_all.48.sums_in = f32[32,2,128]{2,1,0:T(2,128)S(1)} all-to-all(f32[32,2,128]{2,1,0:T(2,128)S(1)} %get-tuple-element.74), channel_id=1, replica_groups=mesh['gz'=32,'ch'=16] {'gz'}, dimensions={0} | all-to-all | bytes 65536 | tf_op jit(solution)/shard_map/all_to_all | solution.py:557
  166.5 5.0 %shard_map.135 = (bf16[8,1024]{1,0:T(8,128)(2,1)S(1)}, f32[16,128]{1,0:T(8,128)S(1)}, f32[16,128]{1,0:T(8,128)S(1)}, bf16[1280,128]{1,0:T(8,128)(2,1)S(1)}) custom-call(f32[128,2048]{1,0:T(8,128)S(1)} %get-tuple-element.73.slope, f32[32,2,128]{2,1,0:T(2,128)S(1)} %all_to_all.48.sums_in, bf16[16,16,1152]{2,1,0:T(8,128)(2,1)S(1)} %all-to-all-done.3.packed, ...), custom_call_target="tpu_custom_call" | custom-call | tf_op jit(solution)/shard_map/pallas_call | solution.py:93
  171.6 18.2 %all_to_all.49.parts = bf16[32,40,128]{2,1,0:T(8,128)(2,1)S(1)} all-to-all(bf16[32,40,128]{2,1,0:T(8,128)(2,1)S(1)} %bitcast.22), channel_id=1, replica_groups=mesh['gz'=32,'ch'=16] {'gz'}, dimensions={0} | all-to-all | bytes 655360 | tf_op jit(solution)/shard_map/all_to_all | solution.py:557
  189.8 0.8 shard_map.136
  190.6 4.0 %all-to-all-start.8 = ((bf16[32,40,128]{2,1,0:T(8,128)(2,1)}), bf16[32,40,128]{2,1,0:T(8,128)(2,1)S(1)}, u32[]{:S(2)}, u32[]{:S(2)}) async-start(bf16[32,40,128]{2,1,0:T(8,128)(2,1)} %shard_map.136), calls=%async_computation.8 | async-start | bytes 655360 | tf_op jit(solution)/shard_map/all_to_all | solution.py:557
  194.6 3.4 %collective-permute-start.4 = (f32[16,128]{1,0:T(8,128)S(1)}, f32[16,128]{1,0:T(8,128)S(1)}, u32[]{:S(2)}, u32[]{:S(2)}) collective-permute-start(f32[16,128]{1,0:T(8,128)S(1)} %get-tuple-element.82), channel_id=1, source_target_pairs={{0,16},{16,32},{32,48},{48,64},{64,80},{80,96},{96,112},{112,128},... | collective-permute-start | bytes 24584 | tf_op jit(solution)/shard_map/ppermute | solution.py:551
  198.0 0.6 copy.25
  198.6 0.6 copy.26
  199.2 0.9 collective-permute-done.4
  200.1 0.6 fusion
  200.7 8.3 %all-to-all-done.8.gathered = bf16[32,40,128]{2,1,0:T(8,128)(2,1)S(1)} async-done(((bf16[32,40,128]{2,1,0:T(8,128)(2,1)}), bf16[32,40,128]{2,1,0:T(8,128)(2,1)S(1)}, u32[]{:S(2)}, u32[]{:S(2)}) %all-to-all-start.8) | async-done | bytes 327712 | tf_op jit(solution)/shard_map/all_to_all | solution.py:557
  209.0 0.8 shard_map.137
Async XLA Ops:
  7.2 12.7 %copy-start.4 = (bf16[16,1,128]{2,0,1:T(8,128)(2,1)S(1)}, bf16[16,1,128]{2,0,1:T(8,128)(2,1)}, u32[]{:S(2)}) copy-start(bf16[16,1,128]{2,0,1:T(8,128)(2,1)} %param.7) | copy-start | bytes 12292
  7.2 76.0 %all-gather.5.cloned.1.call-start = ((), (), s32[]{:S(2)}) async-start(), calls=%async_computation.9 | async-start | bytes 1880064 | tf_op jit(solution)/shard_map/all_gather | solution.py:585
  8.0 11.8 %collective-permute-start = (bf16[8,1792]{1,0:T(8,128)(2,1)S(1)}, bf16[8,1792]{1,0:T(8,128)(2,1)S(1)}, u32[]{:S(2)}, u32[]{:S(2)}) collective-permute-start(bf16[8,1792]{1,0:T(8,128)(2,1)S(1)} %get-tuple-element.48), channel_id=1, source_target_pairs={{0,16},{16,32},{32,48},{48,64},{64,80},{80,96},{96,112},{112,128},... | collective-permute-start | bytes 86024 | tf_op jit(solution)/shard_map/ppermute | solution.py:551
  11.5 9.0 %copy-start.3 = (bf16[27,128,8]{1,2,0:T(8,128)(2,1)S(1)}, bf16[27,128,8]{1,2,0:T(8,128)(2,1)}, u32[]{:S(2)}) copy-start(bf16[27,128,8]{1,2,0:T(8,128)(2,1)} %param.10) | copy-start | bytes 165892
  11.5 9.0 %copy-start.5 = (bf16[27,128,8]{1,2,0:T(8,128)(2,1)S(1)}, bf16[27,128,8]{1,2,0:T(8,128)(2,1)}, u32[]{:S(2)}) copy-start(bf16[27,128,8]{1,2,0:T(8,128)(2,1)} %param.12) | copy-start | bytes 165892
  11.6 8.3 %collective-permute-start.1 = (bf16[8,1792]{1,0:T(8,128)(2,1)S(1)}, bf16[8,1792]{1,0:T(8,128)(2,1)S(1)}, u32[]{:S(2)}, u32[]{:S(2)}) collective-permute-start(bf16[8,1792]{1,0:T(8,128)(2,1)S(1)} %get-tuple-element.49), channel_id=1, source_target_pairs={{16,0},{32,16},{48,32},{64,48},{80,64},{96,80},{112,96},{128,112},... | collective-permute-start | bytes 86024 | tf_op jit(solution)/shard_map/ppermute | solution.py:554
  18.6 15.0 %copy-start.2 = (bf16[27,128,8]{1,2,0:T(8,128)(2,1)S(1)}, bf16[27,128,8]{1,2,0:T(8,128)(2,1)}, u32[]{:S(2)}) copy-start(bf16[27,128,8]{1,2,0:T(8,128)(2,1)} %param.11) | copy-start | bytes 165892
  48.9 37.9 %copy-start.1 = (bf16[27,128,16]{1,2,0:T(8,128)(2,1)S(1)}, bf16[27,128,16]{1,2,0:T(8,128)(2,1)}, u32[]{:S(2)}) copy-start(bf16[27,128,16]{1,2,0:T(8,128)(2,1)} %param.9) | copy-start | bytes 331780
  48.9 33.3 %all-to-all-start.2 = ((bf16[32,16,384]{2,1,0:T(8,128)(2,1)}), bf16[32,16,384]{2,1,0:T(8,128)(2,1)S(1)}, u32[]{:S(2)}, u32[]{:S(2)}) async-start(bf16[32,16,384]{2,1,0:T(8,128)(2,1)} %get-tuple-element.56), calls=%async_computation.2 | async-start | bytes 786432 | tf_op jit(solution)/shard_map/all_to_all | solution.py:557
  64.8 51.1 %all-gather.7.cloned.1.call-start = ((), (), s32[]{:S(2)}) async-start(), calls=%async_computation.10 | async-start | bytes 1114112 | tf_op jit(solution)/shard_map/all_gather | solution.py:586
  83.2 16.8 %all-to-all-start.3 = ((bf16[16,16,1152]{2,1,0:T(8,128)(2,1)}), bf16[16,16,1152]{2,1,0:T(8,128)(2,1)S(1)}, u32[]{:S(2)}, u32[]{:S(2)}) async-start(bf16[16,16,1152]{2,1,0:T(8,128)(2,1)} %shard_map.130), calls=%async_computation.3 | async-start | bytes 1179648 | tf_op jit(solution)/shard_map/all_to_all | solution.py:557
  86.8 1.5 copy-start
  104.1 23.0 %collective-permute-start.3 = (bf16[128,1024]{1,0:T(8,128)(2,1)S(1)}, bf16[128,1024]{1,0:T(8,128)(2,1)S(1)}, u32[]{:S(2)}, u32[]{:S(2)}) collective-permute-start(bf16[128,1024]{1,0:T(8,128)(2,1)S(1)} %get-tuple-element.64), channel_id=1, source_target_pairs={{16,0},{32,16},{48,32},{64,48},{80,64},{96,80},{112,96},{128,112},... | collective-permute-start | bytes 786440 | tf_op jit(solution)/shard_map/ppermute | solution.py:554
  106.0 21.1 %collective-permute-start.2 = (bf16[128,1024]{1,0:T(8,128)(2,1)S(1)}, bf16[128,1024]{1,0:T(8,128)(2,1)S(1)}, u32[]{:S(2)}, u32[]{:S(2)}) collective-permute-start(bf16[128,1024]{1,0:T(8,128)(2,1)S(1)} %get-tuple-element.64), channel_id=1, source_target_pairs={{0,16},{16,32},{32,48},{48,64},{64,80},{80,96},{96,112},{112,128},... | collective-permute-start | bytes 786440 | tf_op jit(solution)/shard_map/ppermute | solution.py:551
  110.0 17.2 %all-to-all-start.4 = ((f32[32,2,128]{2,1,0:T(2,128)}), f32[32,2,128]{2,1,0:T(2,128)S(1)}, u32[]{:S(2)}, u32[]{:S(2)}) async-start(f32[32,2,128]{2,1,0:T(2,128)} %get-tuple-element.65), calls=%async_computation.4 | async-start | bytes 65536 | tf_op jit(solution)/shard_map/all_to_all | solution.py:557
  190.6 18.4 %all-to-all-start.8 = ((bf16[32,40,128]{2,1,0:T(8,128)(2,1)}), bf16[32,40,128]{2,1,0:T(8,128)(2,1)S(1)}, u32[]{:S(2)}, u32[]{:S(2)}) async-start(bf16[32,40,128]{2,1,0:T(8,128)(2,1)} %shard_map.136), calls=%async_computation.8 | async-start | bytes 655360 | tf_op jit(solution)/shard_map/all_to_all | solution.py:557
  194.6 5.5 %collective-permute-start.4 = (f32[16,128]{1,0:T(8,128)S(1)}, f32[16,128]{1,0:T(8,128)S(1)}, u32[]{:S(2)}, u32[]{:S(2)}) collective-permute-start(f32[16,128]{1,0:T(8,128)S(1)} %get-tuple-element.82), channel_id=1, source_target_pairs={{0,16},{16,32},{32,48},{48,64},{64,80},{80,96},{96,112},{112,128},... | collective-permute-start | bytes 24584 | tf_op jit(solution)/shard_map/ppermute | solution.py:551
Sparse Core Ops, SparseCore 0:
  21.4 44.3 all-gather.4
  68.5 46.2 all-gather.6
